TPU v7x, 512 devices: a whole 4x8x8 slice. The times are simulated.
512 devices in a mesh: seq: 128 (over x, z_lo, y, core), head: 4 (over z_hi).
Axes of the slice: x: 4, y: 8, z: 8 (z_hi: 4, z_lo: 2; z = z_hi * 2 + z_lo), core: 2. Of those that a mesh axis runs over, the one named last changes fastest.
Arguments:
- queries: bfloat16 [8192, 12, 128], P('seq', 'head'), may hold values from -6 to 6
- keys: bfloat16 [8192, 12, 128], P('seq', 'head'), may hold values from -6 to 6
- values: bfloat16 [8192, 12, 128], P('seq', 'head'), may hold values from -6 to 6
- out_weight: bfloat16 [768, 768], P('head'), may hold values from -0.21875 to 0.21875
- offsets: int32 [12], P('head'), may hold values from 0 to 127
- out_grad: bfloat16 [8192, 1536], P('seq', 'head'), may hold values from -6 to 6
Outputs:
- output: bfloat16 [8192, 1536], P('seq', 'head')
- query_grad: bfloat16 [8192, 12, 128], P('seq', 'head')
- key_grad: bfloat16 [8192, 12, 128], P('seq', 'head')
- value_grad: bfloat16 [8192, 12, 128], P('seq', 'head')
- weight_grad: float32 [768, 768], P('head')
All inputs are finite; a program needn't handle non-finite values.
Results may differ from a plain program's by a relative error of at most 0.029.
Values may be sent and summed in bfloat16 or wider, within the bound.
No kernel may reach another device: no remote copies, remote signals or barrier semaphores. Data moves between devices by JAX's collectives and lax.ppermute only.
A program may use at most 64 MiB of HBM per device.

v0:
```python
import jax
import jax.numpy as jnp
from jax import lax
from jax.sharding import PartitionSpec as P


def swapped(shard, axis, bit):
    return lax.ppermute(shard, axis, [(i, i ^ 1 << bit) for i in range(lax.axis_size(axis))])


def level_mask(offsets, stride, dtype):
    return (jnp.arange(stride)[:, None] == (offsets % stride)[None, :]).astype(dtype)


def select(block, offsets, stride):
    mask = level_mask(offsets, stride, block.dtype)
    mask = mask.reshape((1, stride, mask.shape[1]) + (1,) * (block.ndim - 2))
    rows = block.reshape((block.shape[0] // stride, stride) + block.shape[1:])
    return jnp.sum(rows * mask, axis=1)


def spread(part, offsets, stride):
    mask = level_mask(offsets, stride, jnp.float32)
    mask = mask.reshape((1, stride, mask.shape[1]) + (1,) * (part.ndim - 2))
    whole = part[:, None] * mask
    return whole.reshape((part.shape[0] * stride,) + part.shape[1:])


def present(offsets, rows, stride):
    return jnp.arange(rows)[:, None] % stride == (offsets % stride)[None, :]


def join(mine, other, rank, bit):
    lower = rank // 2**bit % 2 == 0
    return jnp.where(
        lower, jnp.concatenate([mine, other], axis=0), jnp.concatenate([other, mine], axis=0)
    )


def split(buffer, rank, bit):
    half = buffer.shape[0] // 2
    lower = rank // 2**bit % 2 == 0
    keep = jnp.where(lower, buffer[:half], buffer[half:])
    send = jnp.where(lower, buffer[half:], buffer[:half])
    return (keep, send)


def unpack_pairs(packed):
    pairs, heads_here, double = packed.shape
    return (
        packed.reshape(pairs, heads_here, 2, double // 2)
        .transpose(0, 2, 1, 3)
        .reshape(pairs * 2, heads_here, double // 2)
    )


def pack_pairs(block):
    count, heads_here, size = block.shape
    return (
        block.reshape(count // 2, 2, heads_here, size)
        .transpose(0, 2, 1, 3)
        .reshape(count // 2, heads_here, 2 * size)
    )


def gather_apart(key_block, value_block, offsets, rank, levels):
    key_sets = [key_block]
    value_sets = [value_block]
    for level in range(1, levels):
        stride = 2**level
        key_buf = select(key_block, offsets, stride)
        value_buf = select(value_block, offsets, stride)
        for bit in range(level):
            key_other, value_other = swapped((key_buf, value_buf), "seq", bit)
            key_buf = join(key_buf, key_other, rank, bit)
            value_buf = join(value_buf, value_other, rank, bit)
        key_sets.append(key_buf)
        value_sets.append(value_buf)
    return (key_sets, value_sets)


def return_apart(dk_sets, dv_sets, offsets, rank, levels):
    key_total = dk_sets[0]
    value_total = dv_sets[0]
    for level in range(1, levels):
        key_buf = dk_sets[level]
        value_buf = dv_sets[level]
        for bit in reversed(range(level)):
            key_keep, key_send = split(key_buf, rank, bit)
            value_keep, value_send = split(value_buf, rank, bit)
            key_in, value_in = swapped((key_send, value_send), "seq", bit)
            key_buf = key_keep + key_in
            value_buf = value_keep + value_in
        key_total = key_total + spread(key_buf, offsets, 2**level)
        value_total = value_total + spread(value_buf, offsets, 2**level)
    return (key_total, value_total)


def level_forward(query_part, key_set, value_set, scale):
    scores = (
        jnp.einsum("qhd,khd->hqk", query_part, key_set, preferred_element_type=jnp.float32) * scale
    )
    top = jnp.max(scores, axis=2, keepdims=True)
    expd = jnp.exp(scores - top)
    total = jnp.sum(expd, axis=2, keepdims=True)
    probs = (expd / total).astype(jnp.bfloat16)
    part = jnp.einsum("hqk,khd->qhd", probs, value_set, preferred_element_type=jnp.float32)
    lse = (top + jnp.log(total))[:, :, 0].T
    return (part, lse)


def level_backward(query_part, key_set, value_set, grad_part, lse_part, delta_part, scale):
    scores = (
        jnp.einsum("qhd,khd->hqk", query_part, key_set, preferred_element_type=jnp.float32) * scale
    )
    probs = jnp.exp(scores - lse_part.T[:, :, None])
    rounded = probs.astype(jnp.bfloat16)
    dv_set = jnp.einsum("hqk,qhd->khd", rounded, grad_part, preferred_element_type=jnp.float32)
    dprob = jnp.einsum("qhd,khd->hqk", grad_part, value_set, preferred_element_type=jnp.float32)
    dscore = (probs * (dprob - delta_part.T[:, :, None]) * scale).astype(jnp.bfloat16)
    dq_part = jnp.einsum("hqk,khd->qhd", dscore, key_set, preferred_element_type=jnp.float32)
    dk_set = jnp.einsum("hqk,qhd->khd", dscore, query_part, preferred_element_type=jnp.float32)
    return (dq_part, dk_set, dv_set)


def shards(queries, keys, values, out_weight, offsets, out_grad):
    rows = queries.shape[0] * 2
    local_heads = queries.shape[1]
    head_size = queries.shape[2] // 2
    model_width = out_weight.shape[1]
    scale = head_size ** (-0.5)
    levels = lax.axis_size("seq").bit_length()
    rank = lax.axis_index("seq")
    shape3 = (rows, local_heads, head_size)
    query_block = unpack_pairs(queries)
    key_block = unpack_pairs(keys)
    value_block = unpack_pairs(values)
    key_sets, value_sets = gather_apart(key_block, value_block, offsets, rank, levels)
    parts = []
    lses = []
    for level in range(levels):
        stride = 2**level
        query_part = select(query_block, offsets, stride)
        part, lse = level_forward(query_part, key_sets[level], value_sets[level], scale)
        parts.append(spread(part, offsets, stride))
        lses.append(
            jnp.where(present(offsets, rows, stride), spread(lse, offsets, stride), -jnp.inf)
        )
    stacked = jnp.stack(lses)
    top = jnp.max(stacked, axis=0)
    lse_all = top + jnp.log(jnp.sum(jnp.exp(stacked - top), axis=0))
    combined = parts[0] * jnp.exp(lses[0] - lse_all)[:, :, None]
    for level in range(1, levels):
        combined = combined + parts[level] * jnp.exp(lses[level] - lse_all)[:, :, None]
    attn = combined.astype(jnp.bfloat16).reshape(rows, local_heads * head_size)
    partial_value = jnp.dot(attn, out_weight, preferred_element_type=jnp.float32).reshape(
        rows // 2, 2 * model_width
    )
    output = lax.psum_scatter(partial_value, "head", scatter_dimension=1, tiled=True).astype(
        jnp.bfloat16
    )
    full_grad = lax.all_gather(out_grad, "head", axis=1, tiled=True).reshape(rows, model_width)
    d_attn = lax.dot_general(
        full_grad, out_weight, (((1,), (1,)), ((), ())), preferred_element_type=jnp.float32
    ).astype(jnp.bfloat16)
    weight_term = lax.dot_general(
        attn, full_grad, (((0,), (0,)), ((), ())), preferred_element_type=jnp.float32
    )
    weight_grad = lax.psum(weight_term, "seq")
    grad_block = d_attn.reshape(shape3)
    delta = jnp.sum(
        grad_block.astype(jnp.float32) * attn.reshape(shape3).astype(jnp.float32), axis=2
    )
    dq_total = jnp.zeros(shape3, jnp.float32)
    dk_sets = []
    dv_sets = []
    for level in range(levels):
        stride = 2**level
        query_part = select(query_block, offsets, stride)
        grad_part = select(grad_block, offsets, stride)
        lse_part = select(lse_all, offsets, stride)
        delta_part = select(delta, offsets, stride)
        dq_part, dk_set, dv_set = level_backward(
            query_part, key_sets[level], value_sets[level], grad_part, lse_part, delta_part, scale
        )
        dq_total = dq_total + spread(dq_part, offsets, stride)
        dk_sets.append(dk_set)
        dv_sets.append(dv_set)
    dk_total, dv_total = return_apart(dk_sets, dv_sets, offsets, rank, levels)
    query_grad = pack_pairs(dq_total.astype(jnp.bfloat16))
    key_grad = pack_pairs(dk_total.astype(jnp.bfloat16))
    value_grad = pack_pairs(dv_total.astype(jnp.bfloat16))
    return (output, query_grad, key_grad, value_grad, weight_grad)


def solution(mesh):
    return jax.shard_map(
        shards,
        mesh=mesh,
        in_specs=(
            P("seq", "head", None),
            P("seq", "head", None),
            P("seq", "head", None),
            P("head", None),
            P("head"),
            P("seq", "head"),
        ),
        out_specs=(
            P("seq", "head"),
            P("seq", "head", None),
            P("seq", "head", None),
            P("seq", "head", None),
            P("head", None),
        ),
        check_vma=False,
    )
```

profile of v0, /device:TPU:1, one launch (start us, length us, event | category | flops | bytes accessed | tf_op | source)
XLA Modules:
  0.0 1477.6 jit_solution(7484071367372681459)
XLA Ops:
  14.0 18.2 %all_gather.3 = bf16[64,1536]{1,0:T(8,128)(2,1)S(1)} all-gather(bf16[64,384]{1,0:T(8,128)(2,1)S(1)} %copy-done.127), channel_id=1, replica_groups=mesh['seq'=128,'head'=4] {'head'}, dimensions={1}, use_global_device_ids=true | all-gather | bytes 245760 | tf_op jit(solution)/shard_map/all_gather | solution.py:162
  32.9 5.8 fusion.55
  38.8 4.9 collective-permute-start.15
  96.1 3.2 collective-permute-start.22
  101.0 3.2 collective-permute-start.50
  105.8 4.4 collective-permute-start.3
  112.5 3.2 collective-permute-start.16
  117.3 3.2 collective-permute-start.44
  122.1 4.2 collective-permute-start.23
  127.8 4.2 collective-permute-start.51
  133.6 7.0 collective-permute-start.1
  142.9 3.3 collective-permute-start.11
  147.7 3.3 collective-permute-start.39
  152.5 4.5 collective-permute-start.17
  158.5 4.3 collective-permute-start.45
  164.2 8.2 collective-permute-start.24
  173.9 7.3 collective-permute-start.52
  182.6 8.9 collective-permute-start
  203.3 3.7 collective-permute-start.12
  209.1 3.7 collective-permute-start.40
  214.8 7.9 collective-permute-start.18
  224.2 7.3 collective-permute-start.46
  233.0 3.8 collective-permute-start.25
  238.1 3.3 collective-permute-start.53
  248.5 3.3 collective-permute-start.8
  254.9 7.2 collective-permute-start.13
  265.6 3.3 collective-permute-start.19
  272.3 3.1 collective-permute-start.26
  284.5 3.3 collective-permute-start.5
  291.6 7.2 collective-permute-start.9
  308.6 3.4 collective-permute-start.14
  320.7 3.1 collective-permute-start.20
  333.5 4.7 collective-permute-start.27
  417.1 3.1 collective-permute-start.71
  420.4 4.4 collective-permute-start.77
  425.6 3.3 collective-permute-start.66
  429.6 7.2 collective-permute-start.62
  446.5 3.4 collective-permute-start.57
  450.0 18.9 %collective-permute-start.56 = (f32[64,3,64]{0,2,1:T(8,128)S(1)}, f32[64,3,64]{0,2,1:T(8,128)S(1)}, u32[]{:S(2)}, u32[]{:S(2)}) collective-permute-start(f32[64,3,64]{0,2,1:T(8,128)S(1)} %slice_select_fusion.43), channel_id=1, source_target_pairs={{0,4},{4,0},{8,12},{12,8},{16,20},{20,16},{24,28},{28,24},{32,36},... | collective-permute-start | bytes 147464 | tf_op jit(solution)/shard_map/ppermute | solution.py:8
  473.6 3.3 collective-permute-start.105
  482.2 3.1 collective-permute-start.90
  489.1 3.1 collective-permute-start.85
  493.0 3.3 collective-permute-start.84
  497.2 3.3 collective-permute-start.72
  503.4 7.5 collective-permute-start.67
  513.9 3.3 collective-permute-start.60
  518.5 3.3 collective-permute-start.58
  525.0 3.4 collective-permute-start.106
  529.3 3.1 collective-permute-start.95
  536.3 4.4 collective-permute-done.95
  546.2 4.9 collective-permute-start.73
  551.2 3.3 collective-permute-start.79
  557.6 3.3 collective-permute-start.64
  560.9 3.0 collective-permute-start.61
  569.3 5.3 collective-permute-start.101
  577.8 3.7 collective-permute-start.96
  584.7 4.2 collective-permute-start.74
  593.1 3.3 collective-permute-start.69
  596.7 4.0 collective-permute-start.65
  603.8 6.5 collective-permute-start.108
  616.0 3.6 collective-permute-start.75
  625.1 3.6 collective-permute-start.103
  636.0 3.4 collective-permute-start.82
  654.8 813.2 %all-reduce.2.cloned.1.call-done = f32[192,768]{1,0:T(8,128)} async-done(((f32[192,768]{1,0:T(8,128)}), f32[192,768]{1,0:T(8,128)}) %all-reduce.2.cloned.1.call-update) | async-done | bytes 589840 | tf_op jit(solution)/shard_map/psum | solution.py:169
  (1269 shorter events, 339.7 us)
Async XLA Ops:
  8.0 645.2 %reduce-scatter.2.cloned.1.call-start = ((), (), s32[]{:S(2)}) async-start(), calls=%async_computation.1 | async-start | bytes 491520 | tf_op jit(solution)/shard_map/reduce_scatter | solution.py:159
  38.8 54.7 %collective-permute-start.15 = (bf16[2,3,64]{2,0,1:T(2,128)(2,1)S(1)}, bf16[2,3,64]{2,0,1:T(2,128)(2,1)S(1)}, u32[]{:S(2)}, u32[]{:S(2)}) collective-permute-start(bf16[2,3,64]{2,0,1:T(2,128)(2,1)S(1)} %bitcast_reduce_fusion.3), channel_id=1, source_target_pairs={{0,4},{4,0},{8,12},{12,8},{16,20},{20,16},{24,28},{28,24},{32,36},... | collective-permute-start | bytes 2312 | tf_op jit(solution)/shard_map/ppermute | solution.py:8
  43.8 52.3 %collective-permute-start.43 = (bf16[2,3,64]{2,0,1:T(2,128)(2,1)S(1)}, bf16[2,3,64]{2,0,1:T(2,128)(2,1)S(1)}, u32[]{:S(2)}, u32[]{:S(2)}) collective-permute-start(bf16[2,3,64]{2,0,1:T(2,128)(2,1)S(1)} %bitcast_reduce_fusion), channel_id=1, source_target_pairs={{0,4},{4,0},{8,12},{12,8},{16,20},{20,16},{24,28},{28,24},{32,36},... | collective-permute-start | bytes 2312 | tf_op jit(solution)/shard_map/ppermute | solution.py:8
  45.8 64.5 %collective-permute-start.10 = (bf16[4,3,64]{2,0,1:T(4,128)(2,1)S(1)}, bf16[4,3,64]{2,0,1:T(4,128)(2,1)S(1)}, u32[]{:S(2)}, u32[]{:S(2)}) collective-permute-start(bf16[4,3,64]{2,0,1:T(4,128)(2,1)S(1)} %bitcast_reduce_fusion.5), channel_id=1, source_target_pairs={{0,4},{4,0},{8,12},{12,8},{16,20},{20,16},{24,28},{28,24},{32,36},... | collective-permute-start | bytes 4616 | tf_op jit(solution)/shard_map/ppermute | solution.py:8
  48.2 64.2 %collective-permute-start.38 = (bf16[4,3,64]{2,0,1:T(4,128)(2,1)S(1)}, bf16[4,3,64]{2,0,1:T(4,128)(2,1)S(1)}, u32[]{:S(2)}, u32[]{:S(2)}) collective-permute-start(bf16[4,3,64]{2,0,1:T(4,128)(2,1)S(1)} %bitcast_reduce_fusion.1), channel_id=1, source_target_pairs={{0,4},{4,0},{8,12},{12,8},{16,20},{20,16},{24,28},{28,24},{32,36},... | collective-permute-start | bytes 4616 | tf_op jit(solution)/shard_map/ppermute | solution.py:8
  50.3 38.0 %collective-permute-start.21 = (bf16[1,3,64]{0,2,1:T(8,128)(2,1)S(1)}, bf16[1,3,64]{0,2,1:T(8,128)(2,1)S(1)}, u32[]{:S(2)}, u32[]{:S(2)}) collective-permute-start(bf16[1,3,64]{0,2,1:T(8,128)(2,1)S(1)} %copy.783), channel_id=1, source_target_pairs={{0,4},{4,0},{8,12},{12,8},{16,20},{20,16},{24,28},{28,24},{32,36},... | collective-permute-start | bytes 1160 | tf_op jit(solution)/shard_map/ppermute | solution.py:8
  91.4 49.3 %collective-permute-start.6 = (bf16[8,3,64]{2,0,1:T(8,128)(2,1)S(1)}, bf16[8,3,64]{2,0,1:T(8,128)(2,1)S(1)}, u32[]{:S(2)}, u32[]{:S(2)}) collective-permute-start(bf16[8,3,64]{2,0,1:T(8,128)(2,1)S(1)} %bitcast_reduce_fusion.7), channel_id=1, source_target_pairs={{0,4},{4,0},{8,12},{12,8},{16,20},{20,16},{24,28},{28,24},{32,36},... | collective-permute-start | bytes 9224 | tf_op jit(solution)/shard_map/ppermute | solution.py:8
  93.5 49.3 %collective-permute-start.34 = (bf16[8,3,64]{2,0,1:T(8,128)(2,1)S(1)}, bf16[8,3,64]{2,0,1:T(8,128)(2,1)S(1)}, u32[]{:S(2)}, u32[]{:S(2)}) collective-permute-start(bf16[8,3,64]{2,0,1:T(8,128)(2,1)S(1)} %bitcast_reduce_fusion.2), channel_id=1, source_target_pairs={{0,4},{4,0},{8,12},{12,8},{16,20},{20,16},{24,28},{28,24},{32,36},... | collective-permute-start | bytes 9224 | tf_op jit(solution)/shard_map/ppermute | solution.py:8
  105.8 85.9 %collective-permute-start.3 = (bf16[16,3,64]{0,2,1:T(8,128)(2,1)S(1)}, bf16[16,3,64]{0,2,1:T(8,128)(2,1)S(1)}, u32[]{:S(2)}, u32[]{:S(2)}) collective-permute-start(bf16[16,3,64]{0,2,1:T(8,128)(2,1)S(1)} %copy.774), channel_id=1, source_target_pairs={{0,4},{4,0},{8,12},{12,8},{16,20},{20,16},{24,28},{28,24},{32,36},... | collective-permute-start | bytes 18440 | tf_op jit(solution)/shard_map/ppermute | solution.py:8
  110.3 83.4 %collective-permute-start.31 = (bf16[16,3,64]{0,2,1:T(8,128)(2,1)S(1)}, bf16[16,3,64]{0,2,1:T(8,128)(2,1)S(1)}, u32[]{:S(2)}, u32[]{:S(2)}) collective-permute-start(bf16[16,3,64]{0,2,1:T(8,128)(2,1)S(1)} %copy.795), channel_id=1, source_target_pairs={{0,4},{4,0},{8,12},{12,8},{16,20},{20,16},{24,28},{28,24},{32,36},... | collective-permute-start | bytes 18440 | tf_op jit(solution)/shard_map/ppermute | solution.py:8
  133.6 111.8 %collective-permute-start.1 = (bf16[32,3,64]{0,2,1:T(8,128)(2,1)S(1)}, bf16[32,3,64]{0,2,1:T(8,128)(2,1)S(1)}, u32[]{:S(2)}, u32[]{:S(2)}) collective-permute-start(bf16[32,3,64]{0,2,1:T(8,128)(2,1)S(1)} %copy.771), channel_id=1, source_target_pairs={{0,4},{4,0},{8,12},{12,8},{16,20},{20,16},{24,28},{28,24},{32,36},... | collective-permute-start | bytes 36872 | tf_op jit(solution)/shard_map/ppermute | solution.py:8
  140.7 107.8 %collective-permute-start.29 = (bf16[32,3,64]{0,2,1:T(8,128)(2,1)S(1)}, bf16[32,3,64]{0,2,1:T(8,128)(2,1)S(1)}, u32[]{:S(2)}, u32[]{:S(2)}) collective-permute-start(bf16[32,3,64]{0,2,1:T(8,128)(2,1)S(1)} %copy.790), channel_id=1, source_target_pairs={{0,4},{4,0},{8,12},{12,8},{16,20},{20,16},{24,28},{28,24},{32,36},... | collective-permute-start | bytes 36872 | tf_op jit(solution)/shard_map/ppermute | solution.py:8
  182.6 105.4 %collective-permute-start = (bf16[64,3,64]{2,0,1:T(8,128)(2,1)S(1)}, bf16[64,3,64]{2,0,1:T(8,128)(2,1)S(1)}, u32[]{:S(2)}, u32[]{:S(2)}) collective-permute-start(bf16[64,3,64]{2,0,1:T(8,128)(2,1)S(1)} %get-tuple-element.27), channel_id=1, source_target_pairs={{0,4},{4,0},{8,12},{12,8},{16,20},{20,16},{24,28},{28,24},{32,36},... | collective-permute-start | bytes 73736 | tf_op jit(solution)/shard_map/ppermute | solution.py:8
  191.6 100.0 %collective-permute-start.28 = (bf16[64,3,64]{2,0,1:T(8,128)(2,1)S(1)}, bf16[64,3,64]{2,0,1:T(8,128)(2,1)}, u32[]{:S(2)}, u32[]{:S(2)}) collective-permute-start(bf16[64,3,64]{2,0,1:T(8,128)(2,1)S(1)} %get-tuple-element.34), channel_id=1, source_target_pairs={{0,4},{4,0},{8,12},{12,8},{16,20},{20,16},{24,28},{28,24},{32,36},... | collective-permute-start | bytes 73736 | tf_op jit(solution)/shard_map/ppermute | solution.py:8
  254.9 14.7 collective-permute-start.13
  278.4 27.5 %collective-permute-start.2 = (bf16[64,3,64]{0,2,1:T(8,128)(2,1)S(1)}, bf16[64,3,64]{0,2,1:T(8,128)(2,1)S(1)}, u32[]{:S(2)}, u32[]{:S(2)}) collective-permute-start(bf16[64,3,64]{0,2,1:T(8,128)(2,1)S(1)} %maximum_select_fusion.2), channel_id=1, source_target_pairs={{0,8},{4,12},{8,0},{12,4},{16,24},{20,28},{24,16},{28,20},{32,40},... | collective-permute-start | bytes 73736 | tf_op jit(solution)/shard_map/ppermute | solution.py:8
  281.5 27.1 %collective-permute-start.30 = (bf16[64,3,64]{0,2,1:T(8,128)(2,1)S(1)}, bf16[64,3,64]{0,2,1:T(8,128)(2,1)S(1)}, u32[]{:S(2)}, u32[]{:S(2)}) collective-permute-start(bf16[64,3,64]{0,2,1:T(8,128)(2,1)S(1)} %maximum_select_fusion.26), channel_id=1, source_target_pairs={{0,8},{4,12},{8,0},{12,4},{16,24},{20,28},{24,16},{28,20},{32,40},... | collective-permute-start | bytes 73736 | tf_op jit(solution)/shard_map/ppermute | solution.py:8
  284.5 32.6 %collective-permute-start.5 = (bf16[64,3,64]{0,2,1:T(8,128)(2,1)S(1)}, bf16[64,3,64]{0,2,1:T(8,128)(2,1)}, u32[]{:S(2)}, u32[]{:S(2)}) collective-permute-start(bf16[64,3,64]{0,2,1:T(8,128)(2,1)S(1)} %maximum_select_fusion.5), channel_id=1, source_target_pairs={{0,16},{4,20},{8,24},{12,28},{16,0},{20,4},{24,8},{28,12},{32,48},... | collective-permute-start | bytes 73736 | tf_op jit(solution)/shard_map/ppermute | solution.py:8
  288.0 32.7 %collective-permute-start.33 = (bf16[64,3,64]{0,2,1:T(8,128)(2,1)}, bf16[64,3,64]{0,2,1:T(8,128)(2,1)}, u32[]{:S(2)}, u32[]{:S(2)}) collective-permute-start(bf16[64,3,64]{0,2,1:T(8,128)(2,1)} %maximum_select_fusion.29), channel_id=1, source_target_pairs={{0,16},{4,20},{8,24},{12,28},{16,0},{20,4},{24,8},{28,12},{32,48},... | collective-permute-start | bytes 73736 | tf_op jit(solution)/shard_map/ppermute | solution.py:8
  291.6 38.2 %collective-permute-start.9 = (bf16[64,3,64]{0,2,1:T(8,128)(2,1)}, bf16[64,3,64]{0,2,1:T(8,128)(2,1)}, u32[]{:S(2)}, u32[]{:S(2)}) collective-permute-start(bf16[64,3,64]{0,2,1:T(8,128)(2,1)} %maximum_select_fusion.8), channel_id=1, source_target_pairs={{0,32},{4,36},{8,40},{12,44},{16,48},{20,52},{24,56},{28,60},{32,0... | collective-permute-start | bytes 73736 | tf_op jit(solution)/shard_map/ppermute | solution.py:8
  305.9 27.6 %collective-permute-start.37 = (bf16[64,3,64]{0,2,1:T(8,128)(2,1)}, bf16[64,3,64]{0,2,1:T(8,128)(2,1)}, u32[]{:S(2)}, u32[]{:S(2)}) collective-permute-start(bf16[64,3,64]{0,2,1:T(8,128)(2,1)} %maximum_select_fusion.32), channel_id=1, source_target_pairs={{0,32},{4,36},{8,40},{12,44},{16,48},{20,52},{24,56},{28,60},{32,0... | collective-permute-start | bytes 73736 | tf_op jit(solution)/shard_map/ppermute | solution.py:8
  308.6 35.6 %collective-permute-start.14 = (bf16[64,3,64]{0,2,1:T(8,128)(2,1)}, bf16[64,3,64]{0,2,1:T(8,128)(2,1)}, u32[]{:S(2)}, u32[]{:S(2)}) collective-permute-start(bf16[64,3,64]{0,2,1:T(8,128)(2,1)} %maximum_select_fusion.12), channel_id=1, source_target_pairs={{0,64},{4,68},{8,72},{12,76},{16,80},{20,84},{24,88},{28,92},{32,9... | collective-permute-start | bytes 73736 | tf_op jit(solution)/shard_map/ppermute | solution.py:8
  317.2 30.7 %collective-permute-start.42 = (bf16[64,3,64]{0,2,1:T(8,128)(2,1)S(1)}, bf16[64,3,64]{0,2,1:T(8,128)(2,1)S(1)}, u32[]{:S(2)}, u32[]{:S(2)}) collective-permute-start(bf16[64,3,64]{0,2,1:T(8,128)(2,1)S(1)} %copy-done.120), channel_id=1, source_target_pairs={{0,64},{4,68},{8,72},{12,76},{16,80},{20,84},{24,88},{28,92},{32,9... | collective-permute-start | bytes 73736 | tf_op jit(solution)/shard_map/ppermute | solution.py:8
  320.7 33.9 %collective-permute-start.20 = (bf16[64,3,64]{0,2,1:T(8,128)(2,1)S(1)}, bf16[64,3,64]{0,2,1:T(8,128)(2,1)}, u32[]{:S(2)}, u32[]{:S(2)}) collective-permute-start(bf16[64,3,64]{0,2,1:T(8,128)(2,1)S(1)} %maximum_select_fusion.17), channel_id=1, source_target_pairs={{0,128},{4,132},{8,136},{12,140},{16,144},{20,148},{24,152},{28,15... | collective-permute-start | bytes 73736 | tf_op jit(solution)/shard_map/ppermute | solution.py:8
  329.8 27.0 %collective-permute-start.48 = (bf16[64,3,64]{0,2,1:T(8,128)(2,1)}, bf16[64,3,64]{0,2,1:T(8,128)(2,1)}, u32[]{:S(2)}, u32[]{:S(2)}) collective-permute-start(bf16[64,3,64]{0,2,1:T(8,128)(2,1)} %maximum_select_fusion.41), channel_id=1, source_target_pairs={{0,128},{4,132},{8,136},{12,140},{16,144},{20,148},{24,152},{28,15... | collective-permute-start | bytes 73736 | tf_op jit(solution)/shard_map/ppermute | solution.py:8
  333.5 29.7 %collective-permute-start.27 = (bf16[64,3,64]{0,2,1:T(8,128)(2,1)S(1)}, bf16[64,3,64]{0,2,1:T(8,128)(2,1)}, u32[]{:S(2)}, u32[]{:S(2)}) collective-permute-start(bf16[64,3,64]{0,2,1:T(8,128)(2,1)S(1)} %maximum_select_fusion.24), channel_id=1, source_target_pairs={{0,256},{4,260},{8,264},{12,268},{16,272},{20,276},{24,280},{28,28... | collective-permute-start | bytes 73736 | tf_op jit(solution)/shard_map/ppermute | solution.py:8
  344.3 25.1 %collective-permute-start.55 = (bf16[64,3,64]{0,2,1:T(8,128)(2,1)S(1)}, bf16[64,3,64]{0,2,1:T(8,128)(2,1)}, u32[]{:S(2)}, u32[]{:S(2)}) collective-permute-start(bf16[64,3,64]{0,2,1:T(8,128)(2,1)S(1)} %maximum_select_fusion.48), channel_id=1, source_target_pairs={{0,256},{4,260},{8,264},{12,268},{16,272},{20,276},{24,280},{28,28... | collective-permute-start | bytes 73736 | tf_op jit(solution)/shard_map/ppermute | solution.py:8
  384.1 1083.9 %all-reduce.2.cloned.1.call-start = ((), (), s32[]{:S(2)}) async-start(), calls=%async_computation.2 | async-start | bytes 1179648 | tf_op jit(solution)/shard_map/psum | solution.py:169
  417.1 32.9 %collective-permute-start.71 = (f32[64,3,64]{0,2,1:T(8,128)}, f32[64,3,64]{0,2,1:T(8,128)}, u32[]{:S(2)}, u32[]{:S(2)}) collective-permute-start(f32[64,3,64]{0,2,1:T(8,128)} %slice_select_fusion.28), channel_id=1, source_target_pairs={{0,128},{4,132},{8,136},{12,140},{16,144},{20,148},{24,152},{28,15... | collective-permute-start | bytes 147464 | tf_op jit(solution)/shard_map/ppermute | solution.py:8
  420.4 25.2 %collective-permute-start.77 = (f32[64,3,64]{2,1,0:T(4,128)S(1)}, f32[64,3,64]{2,1,0:T(4,128)S(1)}, u32[]{:S(2)}, u32[]{:S(2)}) collective-permute-start(f32[64,3,64]{2,1,0:T(4,128)S(1)} %slice_select_fusion.1), channel_id=1, source_target_pairs={{0,256},{4,260},{8,264},{12,268},{16,272},{20,276},{24,280},{28,28... | collective-permute-start | bytes 147464 | tf_op jit(solution)/shard_map/ppermute | solution.py:8
  425.6 44.3 %collective-permute-start.66 = (f32[64,3,64]{0,2,1:T(8,128)}, f32[64,3,64]{0,2,1:T(8,128)}, u32[]{:S(2)}, u32[]{:S(2)}) collective-permute-start(f32[64,3,64]{0,2,1:T(8,128)} %slice_select_fusion.33), channel_id=1, source_target_pairs={{0,64},{4,68},{8,72},{12,76},{16,80},{20,84},{24,88},{28,92},{32,9... | collective-permute-start | bytes 147464 | tf_op jit(solution)/shard_map/ppermute | solution.py:8
  429.6 43.9 %collective-permute-start.62 = (f32[64,3,64]{0,2,1:T(8,128)}, f32[64,3,64]{0,2,1:T(8,128)}, u32[]{:S(2)}, u32[]{:S(2)}) collective-permute-start(f32[64,3,64]{0,2,1:T(8,128)} %slice_select_fusion.37), channel_id=1, source_target_pairs={{0,32},{4,36},{8,40},{12,44},{16,48},{20,52},{24,56},{28,60},{32,0... | collective-permute-start | bytes 147464 | tf_op jit(solution)/shard_map/ppermute | solution.py:8
  437.5 41.0 %collective-permute-start.59 = (f32[64,3,64]{0,2,1:T(8,128)}, f32[64,3,64]{0,2,1:T(8,128)}, u32[]{:S(2)}, u32[]{:S(2)}) collective-permute-start(f32[64,3,64]{0,2,1:T(8,128)} %slice_select_fusion.40), channel_id=1, source_target_pairs={{0,16},{4,20},{8,24},{12,28},{16,0},{20,4},{24,8},{28,12},{32,48},... | collective-permute-start | bytes 147464 | tf_op jit(solution)/shard_map/ppermute | solution.py:8
  446.5 35.7 %collective-permute-start.57 = (f32[64,3,64]{0,2,1:T(8,128)S(1)}, f32[64,3,64]{0,2,1:T(8,128)S(1)}, u32[]{:S(2)}, u32[]{:S(2)}) collective-permute-start(f32[64,3,64]{0,2,1:T(8,128)S(1)} %copy-done.29), channel_id=1, source_target_pairs={{0,8},{4,12},{8,0},{12,4},{16,24},{20,28},{24,16},{28,20},{32,40},... | collective-permute-start | bytes 147464 | tf_op jit(solution)/shard_map/ppermute | solution.py:8
  450.0 36.2 %collective-permute-start.56 = (f32[64,3,64]{0,2,1:T(8,128)S(1)}, f32[64,3,64]{0,2,1:T(8,128)S(1)}, u32[]{:S(2)}, u32[]{:S(2)}) collective-permute-start(f32[64,3,64]{0,2,1:T(8,128)S(1)} %slice_select_fusion.43), channel_id=1, source_target_pairs={{0,4},{4,0},{8,12},{12,8},{16,20},{20,16},{24,28},{28,24},{32,36},... | collective-permute-start | bytes 147464 | tf_op jit(solution)/shard_map/ppermute | solution.py:8
  469.9 18.4 %collective-permute-start.99 = (f32[64,3,64]{0,2,1:T(8,128)}, f32[64,3,64]{0,2,1:T(8,128)S(1)}, u32[]{:S(2)}, u32[]{:S(2)}) collective-permute-start(f32[64,3,64]{0,2,1:T(8,128)} %slice_select_fusion.7), channel_id=1, source_target_pairs={{0,128},{4,132},{8,136},{12,140},{16,144},{20,148},{24,152},{28,15... | collective-permute-start | bytes 147464 | tf_op jit(solution)/shard_map/ppermute | solution.py:8
  473.6 23.6 %collective-permute-start.105 = (f32[64,3,64]{2,1,0:T(4,128)S(1)}, f32[64,3,64]{2,1,0:T(4,128)S(1)}, u32[]{:S(2)}, u32[]{:S(2)}) collective-permute-start(f32[64,3,64]{2,1,0:T(4,128)S(1)} %slice_select_fusion), channel_id=1, source_target_pairs={{0,256},{4,260},{8,264},{12,268},{16,272},{20,276},{24,280},{28,28... | collective-permute-start | bytes 147464 | tf_op jit(solution)/shard_map/ppermute | solution.py:8
  482.2 18.4 %collective-permute-start.90 = (f32[64,3,64]{0,2,1:T(8,128)}, f32[64,3,64]{0,2,1:T(8,128)S(1)}, u32[]{:S(2)}, u32[]{:S(2)}) collective-permute-start(f32[64,3,64]{0,2,1:T(8,128)} %slice_select_fusion.16), channel_id=1, source_target_pairs={{0,32},{4,36},{8,40},{12,44},{16,48},{20,52},{24,56},{28,60},{32,0... | collective-permute-start | bytes 147464 | tf_op jit(solution)/shard_map/ppermute | solution.py:8
  486.2 17.2 %collective-permute-start.87 = (f32[64,3,64]{0,2,1:T(8,128)}, f32[64,3,64]{0,2,1:T(8,128)S(1)}, u32[]{:S(2)}, u32[]{:S(2)}) collective-permute-start(f32[64,3,64]{0,2,1:T(8,128)} %slice_select_fusion.19), channel_id=1, source_target_pairs={{0,16},{4,20},{8,24},{12,28},{16,0},{20,4},{24,8},{28,12},{32,48},... | collective-permute-start | bytes 147464 | tf_op jit(solution)/shard_map/ppermute | solution.py:8
  489.1 22.7 %collective-permute-start.85 = (f32[64,3,64]{0,2,1:T(8,128)S(1)}, f32[64,3,64]{0,2,1:T(8,128)S(1)}, u32[]{:S(2)}, u32[]{:S(2)}) collective-permute-start(f32[64,3,64]{0,2,1:T(8,128)S(1)} %copy-done.26), channel_id=1, source_target_pairs={{0,8},{4,12},{8,0},{12,4},{16,24},{20,28},{24,16},{28,20},{32,40},... | collective-permute-start | bytes 147464 | tf_op jit(solution)/shard_map/ppermute | solution.py:8
  493.0 20.8 %collective-permute-start.84 = (f32[64,3,64]{0,2,1:T(8,128)S(1)}, f32[64,3,64]{0,2,1:T(8,128)S(1)}, u32[]{:S(2)}, u32[]{:S(2)}) collective-permute-start(f32[64,3,64]{0,2,1:T(8,128)S(1)} %slice_select_fusion.22), channel_id=1, source_target_pairs={{0,4},{4,0},{8,12},{12,8},{16,20},{20,16},{24,28},{28,24},{32,36},... | collective-permute-start | bytes 147464 | tf_op jit(solution)/shard_map/ppermute | solution.py:8
  497.2 21.4 %collective-permute-start.72 = (f32[32,3,64]{0,2,1:T(8,128)}, f32[32,3,64]{0,2,1:T(8,128)S(1)}, u32[]{:S(2)}, u32[]{:S(2)}) collective-permute-start(f32[32,3,64]{0,2,1:T(8,128)} %slice_select_fusion.27), channel_id=1, source_target_pairs={{0,64},{4,68},{8,72},{12,76},{16,80},{20,84},{24,88},{28,92},{32,9... | collective-permute-start | bytes 73736 | tf_op jit(solution)/shard_map/ppermute | solution.py:8
  500.6 42.2 %collective-permute-start.78 = (f32[32,3,64]{2,1,0:T(4,128)S(1)}, f32[32,3,64]{2,1,0:T(4,128)}, u32[]{:S(2)}, u32[]{:S(2)}) collective-permute-start(f32[32,3,64]{2,1,0:T(4,128)S(1)} %slice_select_fusion.45), channel_id=1, source_target_pairs={{0,128},{4,132},{8,136},{12,140},{16,144},{20,148},{24,152},{28,15... | collective-permute-start | bytes 73736 | tf_op jit(solution)/shard_map/ppermute | solution.py:8
  503.4 18.7 %collective-permute-start.67 = (f32[32,3,64]{0,2,1:T(8,128)}, f32[32,3,64]{0,2,1:T(8,128)S(1)}, u32[]{:S(2)}, u32[]{:S(2)}) collective-permute-start(f32[32,3,64]{0,2,1:T(8,128)} %slice_select_fusion.32), channel_id=1, source_target_pairs={{0,32},{4,36},{8,40},{12,44},{16,48},{20,52},{24,56},{28,60},{32,0... | collective-permute-start | bytes 73736 | tf_op jit(solution)/shard_map/ppermute | solution.py:8
  513.9 14.7 collective-permute-start.60
  518.5 27.7 %collective-permute-start.58 = (f32[32,3,64]{0,2,1:T(8,128)S(1)}, f32[32,3,64]{0,2,1:T(8,128)S(1)}, u32[]{:S(2)}, u32[]{:S(2)}) collective-permute-start(f32[32,3,64]{0,2,1:T(8,128)S(1)} %slice_select_fusion.41), channel_id=1, source_target_pairs={{0,4},{4,0},{8,12},{12,8},{16,20},{20,16},{24,28},{28,24},{32,36},... | collective-permute-start | bytes 73736 | tf_op jit(solution)/shard_map/ppermute | solution.py:8
  525.0 32.6 %collective-permute-start.106 = (f32[32,3,64]{2,1,0:T(4,128)}, f32[32,3,64]{2,1,0:T(4,128)S(1)}, u32[]{:S(2)}, u32[]{:S(2)}) collective-permute-start(f32[32,3,64]{2,1,0:T(4,128)} %slice_select_fusion.44), channel_id=1, source_target_pairs={{0,128},{4,132},{8,136},{12,140},{16,144},{20,148},{24,152},{28,15... | collective-permute-start | bytes 73736 | tf_op jit(solution)/shard_map/ppermute | solution.py:8
  534.2 17.1 %collective-permute-start.91 = (f32[32,3,64]{0,2,1:T(8,128)}, f32[32,3,64]{0,2,1:T(8,128)S(1)}, u32[]{:S(2)}, u32[]{:S(2)}) collective-permute-start(f32[32,3,64]{0,2,1:T(8,128)} %slice_select_fusion.15), channel_id=1, source_target_pairs={{0,16},{4,20},{8,24},{12,28},{16,0},{20,4},{24,8},{28,12},{32,48},... | collective-permute-start | bytes 73736 | tf_op jit(solution)/shard_map/ppermute | solution.py:8
  542.8 18.1 %collective-permute-start.86 = (f32[32,3,64]{0,2,1:T(8,128)S(1)}, f32[32,3,64]{0,2,1:T(8,128)S(1)}, u32[]{:S(2)}, u32[]{:S(2)}) collective-permute-start(f32[32,3,64]{0,2,1:T(8,128)S(1)} %slice_select_fusion.20), channel_id=1, source_target_pairs={{0,4},{4,0},{8,12},{12,8},{16,20},{20,16},{24,28},{28,24},{32,36},... | collective-permute-start | bytes 73736 | tf_op jit(solution)/shard_map/ppermute | solution.py:8
  546.2 29.5 %collective-permute-start.73 = (f32[16,3,64]{0,2,1:T(8,128)S(1)}, f32[16,3,64]{0,2,1:T(8,128)S(1)}, u32[]{:S(2)}, u32[]{:S(2)}) collective-permute-start(f32[16,3,64]{0,2,1:T(8,128)S(1)} %slice_select_fusion.26), channel_id=1, source_target_pairs={{0,32},{4,36},{8,40},{12,44},{16,48},{20,52},{24,56},{28,60},{32,0... | collective-permute-start | bytes 36872 | tf_op jit(solution)/shard_map/ppermute | solution.py:8
  551.2 33.5 %collective-permute-start.79 = (f32[16,3,64]{2,1,0:T(4,128)S(1)}, f32[16,3,64]{2,1,0:T(4,128)}, u32[]{:S(2)}, u32[]{:S(2)}) collective-permute-start(f32[16,3,64]{2,1,0:T(4,128)S(1)} %slice_select_fusion.47), channel_id=1, source_target_pairs={{0,64},{4,68},{8,72},{12,76},{16,80},{20,84},{24,88},{28,92},{32,9... | collective-permute-start | bytes 36872 | tf_op jit(solution)/shard_map/ppermute | solution.py:8
  554.8 23.0 %collective-permute-start.68 = (f32[16,3,64]{0,2,1:T(8,128)S(1)}, f32[16,3,64]{0,2,1:T(8,128)}, u32[]{:S(2)}, u32[]{:S(2)}) collective-permute-start(f32[16,3,64]{0,2,1:T(8,128)S(1)} %slice_select_fusion.31), channel_id=1, source_target_pairs={{0,16},{4,20},{8,24},{12,28},{16,0},{20,4},{24,8},{28,12},{32,48},... | collective-permute-start | bytes 36872 | tf_op jit(solution)/shard_map/ppermute | solution.py:8
  557.6 25.0 %collective-permute-start.64 = (f32[16,3,64]{0,2,1:T(8,128)S(1)}, f32[16,3,64]{0,2,1:T(8,128)S(1)}, u32[]{:S(2)}, u32[]{:S(2)}) collective-permute-start(f32[16,3,64]{0,2,1:T(8,128)S(1)} %slice_select_fusion.35), channel_id=1, source_target_pairs={{0,8},{4,12},{8,0},{12,4},{16,24},{20,28},{24,16},{28,20},{32,40},... | collective-permute-start | bytes 36872 | tf_op jit(solution)/shard_map/ppermute | solution.py:8
  569.3 20.5 %collective-permute-start.101 = (f32[16,3,64]{0,2,1:T(8,128)S(1)}, f32[16,3,64]{0,2,1:T(8,128)}, u32[]{:S(2)}, u32[]{:S(2)}) collective-permute-start(f32[16,3,64]{0,2,1:T(8,128)S(1)} %slice_select_fusion.5), channel_id=1, source_target_pairs={{0,32},{4,36},{8,40},{12,44},{16,48},{20,52},{24,56},{28,60},{32,0... | collective-permute-start | bytes 36872 | tf_op jit(solution)/shard_map/ppermute | solution.py:8
  575.7 25.2 %collective-permute-start.107 = (f32[16,3,64]{2,1,0:T(4,128)}, f32[16,3,64]{2,1,0:T(4,128)S(1)}, u32[]{:S(2)}, u32[]{:S(2)}) collective-permute-start(f32[16,3,64]{2,1,0:T(4,128)} %slice_select_fusion.46), channel_id=1, source_target_pairs={{0,64},{4,68},{8,72},{12,76},{16,80},{20,84},{24,88},{28,92},{32,9... | collective-permute-start | bytes 36872 | tf_op jit(solution)/shard_map/ppermute | solution.py:8
  577.8 15.3 %collective-permute-start.96 = (f32[16,3,64]{0,2,1:T(8,128)S(1)}, f32[16,3,64]{0,2,1:T(8,128)S(1)}, u32[]{:S(2)}, u32[]{:S(2)}) collective-permute-start(f32[16,3,64]{0,2,1:T(8,128)S(1)} %slice_select_fusion.10), channel_id=1, source_target_pairs={{0,16},{4,20},{8,24},{12,28},{16,0},{20,4},{24,8},{28,12},{32,48},... | collective-permute-start | bytes 36872 | tf_op jit(solution)/shard_map/ppermute | solution.py:8
  584.7 19.1 %collective-permute-start.74 = (f32[8,3,64]{0,2,1:T(8,128)S(1)}, f32[8,3,64]{0,2,1:T(8,128)S(1)}, u32[]{:S(2)}, u32[]{:S(2)}) collective-permute-start(f32[8,3,64]{0,2,1:T(8,128)S(1)} %slice_select_fusion.25), channel_id=1, source_target_pairs={{0,16},{4,20},{8,24},{12,28},{16,0},{20,4},{24,8},{28,12},{32,48},... | collective-permute-start | bytes 18440 | tf_op jit(solution)/shard_map/ppermute | solution.py:8
  589.8 23.7 %collective-permute-start.80 = (f32[8,3,64]{2,1,0:T(4,128)S(1)}, f32[8,3,64]{2,1,0:T(4,128)S(1)}, u32[]{:S(2)}, u32[]{:S(2)}) collective-permute-start(f32[8,3,64]{2,1,0:T(4,128)S(1)} %slice_select_fusion.49), channel_id=1, source_target_pairs={{0,32},{4,36},{8,40},{12,44},{16,48},{20,52},{24,56},{28,60},{32,0... | collective-permute-start | bytes 18440 | tf_op jit(solution)/shard_map/ppermute | solution.py:8
  593.1 17.4 %collective-permute-start.69 = (f32[8,3,64]{0,2,1:T(8,128)S(1)}, f32[8,3,64]{0,2,1:T(8,128)}, u32[]{:S(2)}, u32[]{:S(2)}) collective-permute-start(f32[8,3,64]{0,2,1:T(8,128)S(1)} %slice_select_fusion.30), channel_id=1, source_target_pairs={{0,8},{4,12},{8,0},{12,4},{16,24},{20,28},{24,16},{28,20},{32,40},... | collective-permute-start | bytes 18440 | tf_op jit(solution)/shard_map/ppermute | solution.py:8
  596.7 19.4 %collective-permute-start.65 = (f32[8,3,64]{0,2,1:T(8,128)S(1)}, f32[8,3,64]{0,2,1:T(8,128)S(1)}, u32[]{:S(2)}, u32[]{:S(2)}) collective-permute-start(f32[8,3,64]{0,2,1:T(8,128)S(1)} %slice_select_fusion.34), channel_id=1, source_target_pairs={{0,4},{4,0},{8,12},{12,8},{16,20},{20,16},{24,28},{28,24},{32,36},... | collective-permute-start | bytes 18440 | tf_op jit(solution)/shard_map/ppermute | solution.py:8
  600.9 18.9 %collective-permute-start.102 = (f32[8,3,64]{0,2,1:T(8,128)S(1)}, f32[8,3,64]{0,2,1:T(8,128)S(1)}, u32[]{:S(2)}, u32[]{:S(2)}) collective-permute-start(f32[8,3,64]{0,2,1:T(8,128)S(1)} %slice_select_fusion.4), channel_id=1, source_target_pairs={{0,16},{4,20},{8,24},{12,28},{16,0},{20,4},{24,8},{28,12},{32,48},... | collective-permute-start | bytes 18440 | tf_op jit(solution)/shard_map/ppermute | solution.py:8
  603.8 19.0 %collective-permute-start.108 = (f32[8,3,64]{2,1,0:T(4,128)S(1)}, f32[8,3,64]{2,1,0:T(4,128)S(1)}, u32[]{:S(2)}, u32[]{:S(2)}) collective-permute-start(f32[8,3,64]{2,1,0:T(4,128)S(1)} %slice_select_fusion.48), channel_id=1, source_target_pairs={{0,32},{4,36},{8,40},{12,44},{16,48},{20,52},{24,56},{28,60},{32,0... | collective-permute-start | bytes 18440 | tf_op jit(solution)/shard_map/ppermute | solution.py:8
  613.5 15.3 %collective-permute-start.93 = (f32[8,3,64]{0,2,1:T(8,128)S(1)}, f32[8,3,64]{0,2,1:T(8,128)S(1)}, u32[]{:S(2)}, u32[]{:S(2)}) collective-permute-start(f32[8,3,64]{0,2,1:T(8,128)S(1)} %slice_select_fusion.13), channel_id=1, source_target_pairs={{0,4},{4,0},{8,12},{12,8},{16,20},{20,16},{24,28},{28,24},{32,36},... | collective-permute-start | bytes 18440 | tf_op jit(solution)/shard_map/ppermute | solution.py:8
  616.0 15.4 %collective-permute-start.75 = (f32[4,3,64]{0,2,1:T(8,128)S(1)}, f32[4,3,64]{0,2,1:T(8,128)S(1)}, u32[]{:S(2)}, u32[]{:S(2)}) collective-permute-start(f32[4,3,64]{0,2,1:T(8,128)S(1)} %slice_select_fusion.24), channel_id=1, source_target_pairs={{0,8},{4,12},{8,0},{12,4},{16,24},{20,28},{24,16},{28,20},{32,40},... | collective-permute-start | bytes 9224 | tf_op jit(solution)/shard_map/ppermute | solution.py:8
  (314 other events, 6013.4 us)
Sparse Core Ops, SparseCore 0:
  384.2 42.0 reduce-scatter.1
Sparse Core Ops, SparseCore 1:
  445.8 1022.2 all-reduce.1
where the time goes:
time: 1490 us; the launch traced here: 1480 us
  waiting for transfers between devices  850 us (57%)
  starting transfers between devices  389 us (26%)
  local copies, waits for them, and re-layouts  90.1 us (6%)
  other arithmetic  84.4 us (6%)
  matrix products  24.4 us (2%)
  between operations  21.3 us (1%)
  blocking collectives  18.2 us (1%)
    psum x1, waiting for transfers between devices, shards(): weight_grad = lax.psum(weight_term, 'seq')  813 us
    ppermute x112, starting transfers between devices, swapped(): lax.ppermute(shard, axis, [(i, i ^ 1 << bit) for i in range(lax.axis_size...  389 us
    mul x149, local copies, waits for them, and re-layouts, spread(): whole = part[:, None] * mask  40.4 us
    ppermute x112, waiting for transfers between devices, swapped(): lax.ppermute(shard, axis, [(i, i ^ 1 << bit) for i in range(lax.axis_size...  36.8 us
    unnamed x535, local copies, waits for them, and re-layouts  33.5 us
  transfers between devices with their start and end apart: 114, of which 25 were waited for; matrix products, arithmetic and copies ran while one was open for 10% of the time, Pallas kernels for 0%

commit v1 on v0

v1 whole, which is shorter than its diff:
```python
import math

import jax
import jax.numpy as jnp
import numpy as np
from jax import lax
from jax.experimental import pallas as pl
from jax.experimental.pallas import tpu as pltpu
from jax.sharding import PartitionSpec as P

FAR, LINE, CORE = 8, 8, 2
ROWS = 128
LOCAL = 3
SIZE = 64
LANES = LOCAL * 2 * SIZE
WIDTH = 768
HALF = WIDTH // 2
SCALE = SIZE**-0.5
NEAR = 32
PICKED = 16
BLOCK = NEAR + PICKED
REACH = LINE * BLOCK
PARTNER_AT = ROWS + REACH
OTHER_AT = PARTNER_AT + NEAR
KEYS = OTHER_AT + REACH
SHARE = 192
SEND = REACH + NEAR + SHARE
PART = SHARE // LINE
FINAL = PART // FAR

NT = (((1,), (1,)), ((), ()))
TN = (((0,), (0,)), ((), ()))
NN = (((1,), (0,)), ((), ()))
BF16 = jnp.bfloat16
F32 = jnp.float32


def dot(a, b, dims=NN):
    return lax.dot_general(a, b, dims, preferred_element_type=F32)


def depth_of(row):
    return 7 if row == 0 else 7 - row.bit_length()


def far_rows():
    rows = [(1, i) for i in range(4)] + [(d, i) for d in (2, 3) for i in range(2)]
    return rows + [(d, 0) for d in range(4, 8)]


def key_table():
    table = [(-1, depth_of(row)) for row in range(ROWS)]
    for core in range(CORE):
        if core:
            table += [(0, depth_of(NEAR + row)) for row in range(NEAR)]
        for line in range(LINE):
            distance = 2 * line + core
            for row in range(NEAR):
                table.append((distance.bit_length() - 1, depth_of(row)) if distance else None)
            table += [(3 + far.bit_length(), depth_of(row)) for far, row in far_rows()]
            table += [None] * (PICKED - 12)
    return table


def shared_levels():
    table = key_table()
    bias = np.full((KEYS, ROWS), -1e30, np.float32)
    for key, entry in enumerate(table):
        if entry is None:
            continue
        for query in range(ROWS):
            count = min(entry[1], depth_of(query)) - entry[0]
            if count > 0:
                bias[key, query] = math.log(count)
    return bias


def reversed_bits(row):
    out = row * 0
    for bit in range(7):
        out = out | ((row >> bit) & 1) << (6 - bit)
    return out


def token_of(row):
    return jnp.where(row < SIZE, 2 * row, 2 * row - (ROWS - 1))


def one_hot(match):
    return jnp.where(match, 1.0, 0.0).astype(BF16)


def order_from(offset, row_axis):
    row = lax.broadcasted_iota(jnp.int32, (ROWS, ROWS), row_axis)
    token = token_of(lax.broadcasted_iota(jnp.int32, (ROWS, ROWS), 1 - row_axis))
    return one_hot(((reversed_bits(row) + offset) & (ROWS - 1)) == token)


def lane_iota(shape):
    return lax.broadcasted_iota(jnp.int32, shape, len(shape) - 1)


def beside(first, second):
    low = lane_iota(first.shape) < SIZE
    even = jnp.where(low, first, pltpu.roll(second, SIZE, 1))
    odd = jnp.where(low, pltpu.roll(first, SIZE, 1), second)
    return jnp.concatenate([even, odd], axis=0).astype(BF16)


def start_kernel(offsets, keys, values, grad, ordered, far_out, partner_out, grad_out):
    for head in range(LOCAL):
        lanes = pl.ds(head * 2 * SIZE, 2 * SIZE)
        both = beside(keys[:, head, :].astype(F32), values[:, head, :].astype(F32))
        ordered[:, lanes] = dot(order_from(offsets[head], 0), both).astype(BF16)
    for slot in range(FAR):
        far_out[slot] = ordered[0:8, :]
    partner_out[...] = ordered[NEAR : 2 * NEAR, :]
    for slot in range(4):
        grad_out[slot] = grad[...]


def far_place(row, far):
    distance = jnp.where(row < 4, 1, jnp.where(row < 6, 2, jnp.where(row < 8, 3, row - 4)))
    index = jnp.where(row < 4, row, jnp.where(row < 8, row & 1, 0))
    return jnp.where(row < 12, (far ^ distance) * 8 + index, -1)


def line_kernel(rank, ordered, far_in, line_out):
    row = lax.broadcasted_iota(jnp.int32, (PICKED, FAR * 8), 0)
    column = lax.broadcasted_iota(jnp.int32, (PICKED, FAR * 8), 1)
    choose = one_hot(far_place(row, rank[0]) == column)
    picked = dot(choose, far_in[...].reshape(FAR * 8, LANES)).astype(BF16)
    for slot in range(LINE):
        line_out[slot, 0:NEAR, :] = ordered[0:NEAR, :]
        line_out[slot, NEAR:BLOCK, :] = picked


def main_kernel(
    rank, offsets, queries, weight, grads, ordered, line_in, partner_in, other_in, bias,
    output_part, query_grad, send, keep_line, keep_own, keep_weight,
    held, full_grad, attn, weight_term,
):
    line, core = rank[1], rank[2]
    held[0:ROWS, :] = ordered[...]
    held[PARTNER_AT:OTHER_AT, :] = partner_in[...]
    for step in range(LINE):
        slot = line ^ step
        held[ROWS + step * BLOCK : ROWS + (step + 1) * BLOCK, :] = line_in[slot]
        held[OTHER_AT + step * BLOCK : OTHER_AT + (step + 1) * BLOCK, :] = other_in[slot]
    for parity in range(2):
        for half in range(2):
            full_grad[parity * SIZE : (parity + 1) * SIZE, half * HALF : (half + 1) * HALF] = grads[2 * parity + half]
    for head in range(LOCAL):
        lanes = pl.ds(head * 2 * SIZE, 2 * SIZE)
        to_order = order_from(offsets[head], 0)
        to_token = order_from(offsets[head], 1)
        pairs = queries[:, head, :].astype(F32)
        query = dot(to_order, beside(pairs, jnp.zeros_like(pairs))).astype(BF16)
        head_weight = weight[head * SIZE : (head + 1) * SIZE, :]
        grad = dot(full_grad[...], head_weight, NT).astype(BF16)
        grad = dot(to_order, jnp.concatenate([jnp.zeros_like(grad), grad], axis=1)).astype(BF16)
        beside_grad = jnp.concatenate([query, grad], axis=0)
        both = held[:, lanes]
        products = dot(both, beside_grad, NT)
        scores = products[:, :ROWS] * SCALE + bias[...]
        top = jnp.max(scores, axis=0, keepdims=True)
        expd = jnp.exp(scores - top)
        probs = expd / jnp.sum(expd, axis=0, keepdims=True)
        rounded = probs.astype(BF16)
        attn_head = dot(both, rounded, TN)[SIZE:, :].astype(BF16)
        grad_side = grad.astype(F32).T
        delta = jnp.sum(grad_side[SIZE:, :] * attn_head.astype(F32), axis=0, keepdims=True)
        dscore = (probs * (products[:, ROWS:] - delta) * SCALE).astype(BF16)
        dquery = dot(both, dscore, TN)[:SIZE, :].astype(BF16)
        attn[:, head * SIZE : (head + 1) * SIZE] = dot(to_token, attn_head, NT).astype(BF16)
        by_token = dot(to_token, jnp.concatenate([dquery, jnp.zeros_like(dquery)], axis=0), NT)
        query_grad[:, head, :] = (by_token[:SIZE] + pltpu.roll(by_token[SIZE:], SIZE, 1)).astype(BF16)
        dboth = dot(jnp.concatenate([dscore, rounded], axis=1), beside_grad)
        keep_own[:, lanes] = dboth[0:ROWS]
        send[REACH : REACH + NEAR, lanes] = dboth[PARTNER_AT:OTHER_AT].astype(BF16)
        for step in range(LINE):
            slot = line ^ step
            keep_line[slot, :, lanes] = dboth[ROWS + step * BLOCK : ROWS + (step + 1) * BLOCK]
            at = pl.multiple_of(slot * BLOCK, 16)
            send[pl.ds(at, BLOCK), lanes] = dboth[OTHER_AT + step * BLOCK : OTHER_AT + (step + 1) * BLOCK].astype(BF16)
    part = dot(attn[...], weight[...])
    output_part[:, :WIDTH] = part[:SIZE]
    output_part[:, WIDTH:] = part[SIZE:]
    weight_term[...] = dot(attn[...], full_grad[...], TN)
    rows = SHARE // 2
    mine = pl.ds(pl.multiple_of(core * rows, 8), rows)
    theirs = pl.ds(pl.multiple_of((1 - core) * rows, 8), rows)
    for half in range(2):
        columns = pl.ds(half * HALF, HALF)
        keep_weight[half * rows : (half + 1) * rows, :] = weight_term[mine, columns]
        at = REACH + NEAR + half * rows
        send[at : at + rows, :] = weight_term[theirs, columns].astype(BF16)


def line_return_kernel(received, keep_line, keep_weight, line_out):
    for slot in range(LINE):
        rows = slice(slot * BLOCK, (slot + 1) * BLOCK)
        line_out[slot, 0:BLOCK, :] = (keep_line[slot] + received[rows, :].astype(F32)).astype(BF16)
        part = slice(slot * PART, (slot + 1) * PART)
        at = REACH + NEAR + slot * PART
        line_out[slot, BLOCK:, :] = (keep_weight[part, :] + received[at : at + PART, :].astype(F32)).astype(BF16)


def far_return_kernel(rank, line_in, near_sum, far_out):
    total = line_in[0].astype(F32)
    for slot in range(1, LINE):
        total = total + line_in[slot].astype(F32)
    near_sum[...] = total[:NEAR]
    shape = (FAR * 8, PICKED + PART)
    place = lax.broadcasted_iota(jnp.int32, shape, 0)
    column = lax.broadcasted_iota(jnp.int32, shape, 1)
    slot, row = place >> 3, place & 7
    term = PICKED + slot * FINAL + row - 4
    choose = ((row < 4) & (column < 12) & (far_place(column, rank[0]) == place)) | (
        (row >= 4) & (row < 4 + FINAL) & (column == term)
    )
    picked = dot(one_hot(choose), total[NEAR:].astype(BF16)).astype(BF16)
    far_out[...] = picked.reshape(FAR, 8, LANES)


def spread_kernel(far_in, far_sum, spread_out):
    total = far_in[0].astype(F32)
    for slot in range(1, FAR):
        total = total + far_in[slot].astype(F32)
    far_sum[...] = total
    part = total[4:8].astype(BF16)
    spread_out[...] = jnp.broadcast_to(part[None], spread_out.shape)


def finish_kernel(offsets, keep_own, received, near_sum, far_sum, spread_in, key_grad, value_grad, weight_grad, own):
    own[...] = keep_own[...]
    own[NEAR : 2 * NEAR, :] += received[REACH : REACH + NEAR, :].astype(F32)
    own[0:NEAR, :] += near_sum[...]
    row = lax.broadcasted_iota(jnp.int32, (8, LANES), 0)
    own[0:8, :] += jnp.where(row < 4, far_sum[...], 0.0)
    for head in range(LOCAL):
        to_token = order_from(offsets[head], 1)
        both = own[:, head * 2 * SIZE : (head + 1) * 2 * SIZE].astype(BF16)
        both = dot(to_token, both)
        even, odd = both[:SIZE], both[SIZE:]
        low = lane_iota(even.shape) < SIZE
        key_grad[:, head, :] = jnp.where(low, even, pltpu.roll(odd, SIZE, 1)).astype(BF16)
        value_grad[:, head, :] = jnp.where(low, pltpu.roll(even, SIZE, 1), odd).astype(BF16)
    place = lax.broadcasted_iota(jnp.int32, (2 * SHARE, ROWS), 0)
    device = lax.broadcasted_iota(jnp.int32, (2 * SHARE, ROWS), 1)
    start = (device & 1) * SHARE + (device >> 1 & 7) * PART + (device >> 4) * FINAL
    total = jnp.zeros((2 * SHARE, HALF), F32)
    for term in range(FINAL):
        total = total + dot(one_hot(place == start + term), spread_in[:, term, :])
    rows = SHARE // 2
    for core in range(CORE):
        for half in range(2):
            at = core * SHARE + half * rows
            weight_grad[core * rows : (core + 1) * rows, half * HALF : (half + 1) * HALF] = total[at : at + rows]


def call(kernel, outs, args, scalars, scratch=()):
    smem = pl.BlockSpec(memory_space=pltpu.SMEM)
    vmem = pl.BlockSpec(memory_space=pltpu.VMEM)
    return pl.pallas_call(
        kernel,
        out_shape=[jax.ShapeDtypeStruct(shape, dtype) for shape, dtype in outs],
        in_specs=[smem] * scalars + [vmem] * (len(args) - scalars),
        out_specs=[vmem] * len(outs),
        scratch_shapes=list(scratch),
        compiler_params=pltpu.CompilerParams(vmem_limit_bytes=48 * 2**20),
    )(*args)


def start(offsets, keys, values, grad):
    outs = [((ROWS, LANES), BF16), ((FAR, 8, LANES), BF16), ((NEAR, LANES), BF16), ((4, SIZE, HALF), BF16)]
    return call(start_kernel, outs, (offsets, keys, values, grad), 1)


def line_pieces(rank, ordered, far_in):
    return call(line_kernel, [((LINE, BLOCK, LANES), BF16)], (rank, ordered, far_in), 1)[0]


def attention(rank, offsets, queries, weight, grads, ordered, line_in, partner_in, other_in):
    outs = [
        ((SIZE, 2 * WIDTH), F32),
        ((SIZE, LOCAL, 2 * SIZE), BF16),
        ((SEND, LANES), BF16),
        ((LINE, BLOCK, LANES), F32),
        ((ROWS, LANES), F32),
        ((SHARE, HALF), F32),
    ]
    scratch = [
        pltpu.VMEM((KEYS, LANES), BF16),
        pltpu.VMEM((ROWS, WIDTH), BF16),
        pltpu.VMEM((ROWS, LOCAL * SIZE), BF16),
        pltpu.VMEM((SHARE, WIDTH), F32),
    ]
    args = (rank, offsets, queries, weight, grads, ordered, line_in, partner_in, other_in, jnp.asarray(shared_levels()))
    return call(main_kernel, outs, args, 2, scratch)


def line_return(received, keep_line, keep_weight):
    return call(line_return_kernel, [((LINE, BLOCK + PART, LANES), BF16)], (received, keep_line, keep_weight), 0)[0]


def far_return(rank, line_in):
    outs = [((NEAR, LANES), F32), ((FAR, 8, LANES), BF16)]
    return call(far_return_kernel, outs, (rank, line_in), 1)


def spread_pieces(far_in):
    outs = [((8, LANES), F32), ((ROWS, 4, LANES), BF16)]
    return call(spread_kernel, outs, (far_in,), 0)


def finish(offsets, keep_own, received, near_sum, far_sum, spread_in):
    outs = [((SIZE, LOCAL, 2 * SIZE), BF16)] * 2 + [((SHARE, WIDTH), F32)]
    args = (offsets, keep_own, received, near_sum, far_sum, spread_in)
    return call(finish_kernel, outs, args, 1, [pltpu.VMEM((ROWS, LANES), F32)])


def trade(pieces, groups):
    return lax.all_to_all(pieces, "seq", 0, 0, axis_index_groups=groups, tiled=True)


def swap_cores(block):
    return lax.ppermute(block, "seq", [(i, i ^ 1) for i in range(FAR * LINE * CORE)])


def shards(queries, keys, values, out_weight, offsets, out_grad):
    index = lax.axis_index("seq")
    rank = jnp.stack([index >> 4, index >> 1 & 7, index & 1]).astype(jnp.int32)
    far_groups = [[far * 16 + low for far in range(FAR)] for low in range(16)]
    line_groups = [[far * 16 + line * 2 + core for line in range(LINE)] for far in range(FAR) for core in range(CORE)]
    ordered, far_out, partner_out, grad_out = start(offsets, keys, values, out_grad)
    partner_in = swap_cores(partner_out)
    far_in = trade(far_out, far_groups)
    line_in = trade(line_pieces(rank, ordered, far_in), line_groups)
    other_in = swap_cores(line_in)
    grads = lax.all_to_all(grad_out, "head", 0, 0, tiled=True)
    output_part, query_grad, send, keep_line, keep_own, keep_weight = attention(
        rank, offsets, queries, out_weight, grads, ordered, line_in, partner_in, other_in
    )
    output = lax.psum_scatter(output_part, "head", scatter_dimension=1, tiled=True).astype(BF16)
    received = swap_cores(send)
    line_back = trade(line_return(received, keep_line, keep_weight), line_groups)
    near_sum, far_back = far_return(rank, line_back)
    far_sum, spread_out = spread_pieces(trade(far_back, far_groups))
    spread_in = lax.all_to_all(spread_out, "seq", 0, 0, tiled=True)
    key_grad, value_grad, weight_grad = finish(offsets, keep_own, received, near_sum, far_sum, spread_in)
    return (output, query_grad, key_grad, value_grad, weight_grad)


def solution(mesh):
    return jax.shard_map(
        shards,
        mesh=mesh,
        in_specs=(
            P("seq", "head", None),
            P("seq", "head", None),
            P("seq", "head", None),
            P("head", None),
            P("head"),
            P("seq", "head"),
        ),
        out_specs=(
            P("seq", "head"),
            P("seq", "head", None),
            P("seq", "head", None),
            P("seq", "head", None),
            P("head", None),
        ),
        check_vma=False,
    )
```

time: 1490 us -> 136 us (0.09)
  waiting for transfers between devices: 850 us -> 28 us
  starting transfers between devices: 389 us -> 39.4 us
  local copies, waits for them, and re-layouts: 90.1 us -> 3.59 us
  other arithmetic: 84.4 us -> 1.59 us
  matrix products: 24.4 us -> 0 us
  blocking collectives: 18.2 us -> 35.2 us
    psum x1 -> x0, waiting for transfers between devices: 813 us -> none  [shards(): weight_grad = lax.psum(weight_term, 'seq')]
    ppermute x112 -> x3, starting transfers between devices: 389 us -> 13.4 us  [swap_cores(): lax.ppermute(block, 'seq', [(i, i ^ 1) for i in range(FAR * LINE * CORE)])]
    select_n x130 -> x0, other arithmetic: 44.7 us -> none  [the longest x56 18 us: split(): send = jnp.where(lower, buffer[half:], buffer[:half])]
    mul x160 -> x0, local copies, waits for them, and re-layouts: 41.4 us -> none  [the longest x149 40.4 us: spread(): whole = part[:, None] * mask]
    all_to_all x0 -> x2, blocking collectives: none -> 35.2 us  [trade(): lax.all_to_all(pieces, 'seq', 0, 0, axis_index_groups=groups, tiled=True)]
    ppermute x112 -> x3, waiting for transfers between devices: 36.8 us -> 2.53 us  [swap_cores(): lax.ppermute(block, 'seq', [(i, i ^ 1) for i in range(FAR * LINE * CORE)])]
    unnamed x535 -> x18, local copies, waits for them, and re-layouts: 33.5 us -> 3.59 us
    all_to_all x0 -> x4, starting transfers between devices: none -> 25.9 us  [the longest x2 10 us: trade(): lax.all_to_all(pieces, 'seq', 0, 0, axis_index_groups=groups, tiled=True)]
  transfers between devices with their start and end apart: 114 -> 8, of which waited for: 25 -> 6; matrix products, arithmetic and copies ran while one was open for 10% -> 2% of each run, Pallas kernels for 0% -> 1%
where the time goes in v1:
time: 136 us; the launch traced here: 135 us
  starting transfers between devices  39.4 us (29%)
  blocking collectives  35.2 us (26%)
  waiting for transfers between devices  28 us (21%)
  between operations  14.2 us (10%)
  Pallas kernels  13.2 us (10%)
  local copies, waits for them, and re-layouts  3.59 us (3%)
  other arithmetic  1.59 us (1%)
    all_to_all x2, blocking collectives, trade(): lax.all_to_all(pieces, 'seq', 0, 0, axis_index_groups=groups, tiled=True)  35.2 us
    reduce_scatter x1, waiting for transfers between devices, shards(): lax.psum_scatter(output_part, 'head', scatter_dimension=1, tiled=True)  15.1 us
    ppermute x3, starting transfers between devices, swap_cores(): lax.ppermute(block, 'seq', [(i, i ^ 1) for i in range(FAR * LINE * CORE)])  13.4 us
    pallas_call x7, Pallas kernels, call(): pl.pallas_call(kernel, out_shape=[jax.ShapeDtypeStruct(shape, dtype) for...  13.2 us
    all_to_all x2, starting transfers between devices, trade(): lax.all_to_all(pieces, 'seq', 0, 0, axis_index_groups=groups, tiled=True)  10 us
    all_to_all x2, waiting for transfers between devices, trade(): lax.all_to_all(pieces, 'seq', 0, 0, axis_index_groups=groups, tiled=True)  9.52 us
    all_to_all x1, starting transfers between devices, shards(): grads = lax.all_to_all(grad_out, 'head', 0, 0, tiled=True)  9.25 us
    all_to_all x1, starting transfers between devices, shards(): spread_in = lax.all_to_all(spread_out, 'seq', 0, 0, tiled=True)  6.69 us
  transfers between devices with their start and end apart: 8, of which 6 were waited for; matrix products, arithmetic and copies ran while one was open for 2% of the time, Pallas kernels for 1%

profile of v1, /device:TPU:1, one launch (start us, length us, event | category | flops | bytes accessed | tf_op | source)
XLA Modules:
  0.0 135.2 jit_solution(15398806712919739515)
XLA Ops:
  7.2 0.0 copy-start.4
  7.2 0.9 copy.12.keys
  8.0 0.0 copy-done.4
  8.0 0.0 copy-start.2
  8.1 0.0 copy-start.3
  8.1 0.7 copy-done.2
  8.8 0.0 copy-done.3
  8.8 1.5 %shard_map.110 = (bf16[128,384]{1,0:T(8,128)(2,1)S(1)}, bf16[8,8,384]{2,1,0:T(8,128)(2,1)}, bf16[32,384]{1,0:T(8,128)(2,1)S(1)}, bf16[4,64,384]{2,1,0:T(8,128)(2,1)}) custom-call(s32[3]{0:T(128)S(1)} %copy-done.3, bf16[64,3,128]{2,1,0:T(4,128)(2,1)S(1)} %copy.12.keys, bf16[64,3,128]{2,1,0:T(4,128)(2,1)S(1)} %copy.13.values, bf16[64,384]{1,0:T(8,128)(2,1)S(1)} %copy-done.2), custom_call_target="tpu_custom_call" | custom-call | tf_op jit(solution)/shard_map/pallas_call | solution.py:265
  10.4 6.7 %all-to-all-start.1 = ((bf16[8,8,384]{2,1,0:T(8,128)(2,1)}), bf16[8,8,384]{2,1,0:T(8,128)(2,1)S(1)}, u32[]{:S(2)}, u32[]{:S(2)}) async-start(bf16[8,8,384]{2,1,0:T(8,128)(2,1)} %get-tuple-element.24), calls=%async_computation.1 | async-start | bytes 98304 | tf_op jit(solution)/shard_map/all_to_all | solution.py:324
  17.1 0.1 pad_add_fusion.rank
  17.1 5.1 %all-to-all-done.1.far_in = bf16[8,8,384]{2,1,0:T(8,128)(2,1)S(1)} async-done(((bf16[8,8,384]{2,1,0:T(8,128)(2,1)}), bf16[8,8,384]{2,1,0:T(8,128)(2,1)S(1)}, u32[]{:S(2)}, u32[]{:S(2)}) %all-to-all-start.1) | async-done | bytes 49184 | tf_op jit(solution)/shard_map/all_to_all | solution.py:324
  22.2 0.7 shard_map.111
  22.9 0.0 copy-start
  22.9 16.6 %all_to_all.30.line_in = bf16[8,48,384]{2,1,0:T(8,128)(2,1)S(1)} all-to-all(bf16[8,48,384]{2,1,0:T(8,128)(2,1)S(1)} %shard_map.111), channel_id=1, replica_groups={{0,8,16,24,32,40,48,56},{4,12,20,28,36,44,52,60},{64,72,80,88,96,104,11..., dimensions={0} | all-to-all | bytes 589824 | tf_op jit(solution)/shard_map/all_to_all | solution.py:324
  39.5 0.0 copy-start.1
  39.5 0.0 copy-start.5
  39.5 9.3 %all-to-all-start = ((bf16[4,64,384]{2,1,0:T(8,128)(2,1)}), bf16[4,64,384]{2,1,0:T(8,128)(2,1)S(1)}, u32[]{:S(2)}, u32[]{:S(2)}) async-start(bf16[4,64,384]{2,1,0:T(8,128)(2,1)} %get-tuple-element.22), calls=%async_computation | async-start | bytes 393216 | tf_op jit(solution)/shard_map/all_to_all | solution.py:341
  48.7 5.9 %collective-permute-start.1 = (bf16[8,48,384]{2,1,0:T(8,128)(2,1)S(1)}, bf16[8,48,384]{2,1,0:T(8,128)(2,1)S(1)}, u32[]{:S(2)}, u32[]{:S(2)}) collective-permute-start(bf16[8,48,384]{2,1,0:T(8,128)(2,1)S(1)} %all_to_all.30.line_in), channel_id=1, source_target_pairs={{0,4},{4,0},{8,12},{12,8},{16,20},{20,16},{24,28},{28,24},{32,36},... | collective-permute-start | bytes 884744 | tf_op jit(solution)/shard_map/ppermute | solution.py:328
  54.6 1.9 %collective-permute-start = (bf16[32,384]{1,0:T(8,128)(2,1)S(1)}, bf16[32,384]{1,0:T(8,128)(2,1)S(1)}, u32[]{:S(2)}, u32[]{:S(2)}) collective-permute-start(bf16[32,384]{1,0:T(8,128)(2,1)S(1)} %get-tuple-element.25), channel_id=1, source_target_pairs={{0,4},{4,0},{8,12},{12,8},{16,20},{20,16},{24,28},{28,24},{32,36},... | collective-permute-start | bytes 73736 | tf_op jit(solution)/shard_map/ppermute | solution.py:328
  56.5 0.0 copy-done.5
  56.6 1.1 collective-permute-done.partner_in
  57.7 0.0 all-to-all-done.grads
  57.7 0.0 collective-permute-done.1.other_in
  57.7 0.0 copy-done
  57.7 0.0 copy-done.1
  57.7 6.3 %shard_map.112 = (f32[64,1536]{1,0:T(8,128)}, bf16[64,3,128]{2,1,0:T(4,128)(2,1)S(1)}, bf16[608,384]{1,0:T(8,128)(2,1)S(1)}, f32[8,48,384]{2,1,0:T(8,128)S(1)}, ...) custom-call(s32[3]{0:T(128)S(1)} %pad_add_fusion.rank, s32[3]{0:T(128)S(1)} %copy-done.3, ...), custom_call_target="tpu_custom_call" | custom-call | tf_op jit(solution)/shard_map/pallas_call | solution.py:265
  64.0 5.6 %collective-permute-start.2 = (bf16[608,384]{1,0:T(8,128)(2,1)S(1)}, bf16[608,384]{1,0:T(8,128)(2,1)S(1)}, u32[]{:S(2)}, u32[]{:S(2)}) collective-permute-start(bf16[608,384]{1,0:T(8,128)(2,1)S(1)} %get-tuple-element.29), channel_id=1, source_target_pairs={{0,4},{4,0},{8,12},{12,8},{16,20},{20,16},{24,28},{28,24},{32,36},... | collective-permute-start | bytes 1400840 | tf_op jit(solution)/shard_map/ppermute | solution.py:328
  69.6 1.4 %collective-permute-done.2.received = bf16[608,384]{1,0:T(8,128)(2,1)S(1)} collective-permute-done((bf16[608,384]{1,0:T(8,128)(2,1)S(1)}, bf16[608,384]{1,0:T(8,128)(2,1)S(1)}, u32[]{:S(2)}, u32[]{:S(2)}) %collective-permute-start.2) | collective-permute-done | bytes 466976 | tf_op jit(solution)/shard_map/ppermute | solution.py:328
  71.1 0.1 shard_map.113
  71.2 18.6 %all_to_all.31.line_in = bf16[8,72,384]{2,1,0:T(8,128)(2,1)S(1)} all-to-all(bf16[8,72,384]{2,1,0:T(8,128)(2,1)S(1)} %shard_map.113), channel_id=1, replica_groups={{0,8,16,24,32,40,48,56},{4,12,20,28,36,44,52,60},{64,72,80,88,96,104,11..., dimensions={0} | all-to-all | bytes 884736 | tf_op jit(solution)/shard_map/all_to_all | solution.py:324
  89.8 1.4 %shard_map.114 = (f32[32,384]{1,0:T(8,128)S(1)}, bf16[8,8,384]{2,1,0:T(8,128)(2,1)}) custom-call(s32[3]{0:T(128)S(1)} %pad_add_fusion.rank, bf16[8,72,384]{2,1,0:T(8,128)(2,1)S(1)} %all_to_all.31.line_in), custom_call_target="tpu_custom_call" | custom-call | tf_op jit(solution)/shard_map/pallas_call | solution.py:265
  91.1 3.3 %all-to-all-start.4 = ((bf16[8,8,384]{2,1,0:T(8,128)(2,1)}), bf16[8,8,384]{2,1,0:T(8,128)(2,1)S(1)}, u32[]{:S(2)}, u32[]{:S(2)}) async-start(bf16[8,8,384]{2,1,0:T(8,128)(2,1)} %get-tuple-element.33), calls=%async_computation.5 | async-start | bytes 98304 | tf_op jit(solution)/shard_map/all_to_all | solution.py:324
  94.5 0.0 reduce-scatter.2.cloned.1.call-start
  94.5 0.7 reduce-scatter.2.cloned.1.call-update
  95.2 4.4 %all-to-all-done.4.far_in = bf16[8,8,384]{2,1,0:T(8,128)(2,1)S(1)} async-done(((bf16[8,8,384]{2,1,0:T(8,128)(2,1)}), bf16[8,8,384]{2,1,0:T(8,128)(2,1)S(1)}, u32[]{:S(2)}, u32[]{:S(2)}) %all-to-all-start.4) | async-done | bytes 49184 | tf_op jit(solution)/shard_map/all_to_all | solution.py:324
  99.7 0.8 shard_map.115
  100.5 6.7 %all-to-all-start.5 = ((bf16[128,4,384]{2,1,0:T(4,128)(2,1)}), bf16[128,4,384]{2,1,0:T(4,128)(2,1)S(1)}, u32[]{:S(2)}, u32[]{:S(2)}) async-start(bf16[128,4,384]{2,1,0:T(4,128)(2,1)} %get-tuple-element.35), calls=%async_computation.6 | async-start | bytes 786432 | tf_op jit(solution)/shard_map/all_to_all | solution.py:350
  107.2 0.6 copy.15
  107.8 15.1 %reduce-scatter.2.cloned.1.call-done = f32[64,384]{1,0:T(8,128)} async-done(((f32[64,1536]{1,0:T(8,128)}), f32[64,384]{1,0:T(8,128)}) %reduce-scatter.2.cloned.1.call-update) | async-done | bytes 98320 | tf_op jit(solution)/shard_map/reduce_scatter | solution.py:345
  122.9 1.5 %convert_element_type.3 = bf16[64,384]{1,0:T(8,128)(2,1)} convert(f32[64,384]{1,0:T(8,128)} %reduce-scatter.2.cloned.1.call-done) | non-fusion elementwise | flops 24576 | bytes 147456 | tf_op jit(solution)/shard_map/convert_element_type | solution.py:345
  124.4 0.2 all-to-all-done.5.spread_in
  124.6 2.5 %shard_map.116 = (bf16[64,3,128]{2,1,0:T(4,128)(2,1)S(1)}, bf16[64,3,128]{2,1,0:T(4,128)(2,1)S(1)}, f32[192,768]{1,0:T(8,128)}) custom-call(s32[3]{0:T(128)S(1)} %copy-done.3, f32[128,384]{1,0:T(8,128)S(1)} %get-tuple-element.28.keep_own, bf16[608,384]{1,0:T(8,128)(2,1)S(1)} %collective-permute-done.2.received, f32[32,384]{1,0:T(8,128)S(1)} %get-tuple-element.32.near_sum, ...), custom_call_target="tpu_custom_call" | custom-call | tf_op jit(solution)/shard_map/pallas_call | solution.py:265
  127.1 0.6 copy.16
  127.7 0.6 copy.17
  (2 shorter events, 0.1 us)
Async XLA Ops:
  7.2 0.9 copy-start.4
  8.0 0.8 copy-start.2
  8.1 0.8 copy-start.3
  10.4 11.8 %all-to-all-start.1 = ((bf16[8,8,384]{2,1,0:T(8,128)(2,1)}), bf16[8,8,384]{2,1,0:T(8,128)(2,1)S(1)}, u32[]{:S(2)}, u32[]{:S(2)}) async-start(bf16[8,8,384]{2,1,0:T(8,128)(2,1)} %get-tuple-element.24), calls=%async_computation.1 | async-start | bytes 98304 | tf_op jit(solution)/shard_map/all_to_all | solution.py:324
  22.9 34.8 %copy-start = (f32[928,128]{1,0:T(8,128)S(1)}, f32[928,128]{1,0:T(8,128)}, u32[]{:S(2)}) copy-start(f32[928,128]{1,0:T(8,128)} %constant.14.clone.bias) | copy-start | bytes 1425412
  39.5 18.3 %copy-start.1 = (bf16[192,768]{1,0:T(8,128)(2,1)S(1)}, bf16[192,768]{1,0:T(8,128)(2,1)}, u32[]{:S(2)}) copy-start(bf16[192,768]{1,0:T(8,128)(2,1)} %weight.1) | copy-start | bytes 884740
  39.5 17.1 %copy-start.5 = (bf16[64,3,128]{2,0,1:T(8,128)(2,1)S(1)}, bf16[64,3,128]{2,0,1:T(8,128)(2,1)}, u32[]{:S(2)}) copy-start(bf16[64,3,128]{2,0,1:T(8,128)(2,1)} %param.7) | copy-start | bytes 147460
  39.5 18.3 %all-to-all-start = ((bf16[4,64,384]{2,1,0:T(8,128)(2,1)}), bf16[4,64,384]{2,1,0:T(8,128)(2,1)S(1)}, u32[]{:S(2)}, u32[]{:S(2)}) async-start(bf16[4,64,384]{2,1,0:T(8,128)(2,1)} %get-tuple-element.22), calls=%async_computation | async-start | bytes 393216 | tf_op jit(solution)/shard_map/all_to_all | solution.py:341
  48.7 9.0 %collective-permute-start.1 = (bf16[8,48,384]{2,1,0:T(8,128)(2,1)S(1)}, bf16[8,48,384]{2,1,0:T(8,128)(2,1)S(1)}, u32[]{:S(2)}, u32[]{:S(2)}) collective-permute-start(bf16[8,48,384]{2,1,0:T(8,128)(2,1)S(1)} %all_to_all.30.line_in), channel_id=1, source_target_pairs={{0,4},{4,0},{8,12},{12,8},{16,20},{20,16},{24,28},{28,24},{32,36},... | collective-permute-start | bytes 884744 | tf_op jit(solution)/shard_map/ppermute | solution.py:328
  54.6 3.1 %collective-permute-start = (bf16[32,384]{1,0:T(8,128)(2,1)S(1)}, bf16[32,384]{1,0:T(8,128)(2,1)S(1)}, u32[]{:S(2)}, u32[]{:S(2)}) collective-permute-start(bf16[32,384]{1,0:T(8,128)(2,1)S(1)} %get-tuple-element.25), channel_id=1, source_target_pairs={{0,4},{4,0},{8,12},{12,8},{16,20},{20,16},{24,28},{28,24},{32,36},... | collective-permute-start | bytes 73736 | tf_op jit(solution)/shard_map/ppermute | solution.py:328
  64.0 7.1 %collective-permute-start.2 = (bf16[608,384]{1,0:T(8,128)(2,1)S(1)}, bf16[608,384]{1,0:T(8,128)(2,1)S(1)}, u32[]{:S(2)}, u32[]{:S(2)}) collective-permute-start(bf16[608,384]{1,0:T(8,128)(2,1)S(1)} %get-tuple-element.29), channel_id=1, source_target_pairs={{0,4},{4,0},{8,12},{12,8},{16,20},{20,16},{24,28},{28,24},{32,36},... | collective-permute-start | bytes 1400840 | tf_op jit(solution)/shard_map/ppermute | solution.py:328
  91.1 8.5 %all-to-all-start.4 = ((bf16[8,8,384]{2,1,0:T(8,128)(2,1)}), bf16[8,8,384]{2,1,0:T(8,128)(2,1)S(1)}, u32[]{:S(2)}, u32[]{:S(2)}) async-start(bf16[8,8,384]{2,1,0:T(8,128)(2,1)} %get-tuple-element.33), calls=%async_computation.5 | async-start | bytes 98304 | tf_op jit(solution)/shard_map/all_to_all | solution.py:324
  94.5 28.4 %reduce-scatter.2.cloned.1.call-start = ((), (), s32[]{:S(2)}) async-start(), calls=%async_computation.7 | async-start | bytes 491520 | tf_op jit(solution)/shard_map/reduce_scatter | solution.py:345
  100.5 24.1 %all-to-all-start.5 = ((bf16[128,4,384]{2,1,0:T(4,128)(2,1)}), bf16[128,4,384]{2,1,0:T(4,128)(2,1)S(1)}, u32[]{:S(2)}, u32[]{:S(2)}) async-start(bf16[128,4,384]{2,1,0:T(4,128)(2,1)} %get-tuple-element.35), calls=%async_computation.6 | async-start | bytes 786432 | tf_op jit(solution)/shard_map/all_to_all | solution.py:350
Sparse Core Ops, SparseCore 0:
  98.7 24.1 reduce-scatter.1

commit v2 on v1

--- a/solution.py
+++ b/solution.py
@@ -26,7 +26,6 @@
 SHARE = 192
 SEND = REACH + NEAR + SHARE
 PART = SHARE // LINE
-FINAL = PART // FAR
 
 NT = (((1,), (1,)), ((), ()))
 TN = (((0,), (0,)), ((), ()))
@@ -110,7 +109,7 @@
 def start_kernel(offsets, keys, values, grad, ordered, far_out, partner_out, grad_out):
     for head in range(LOCAL):
         lanes = pl.ds(head * 2 * SIZE, 2 * SIZE)
-        both = beside(keys[:, head, :].astype(F32), values[:, head, :].astype(F32))
+        both = beside(keys[head].astype(F32), values[head].astype(F32))
         ordered[:, lanes] = dot(order_from(offsets[head], 0), both).astype(BF16)
     for slot in range(FAR):
         far_out[slot] = ordered[0:8, :]
@@ -154,7 +153,7 @@
         lanes = pl.ds(head * 2 * SIZE, 2 * SIZE)
         to_order = order_from(offsets[head], 0)
         to_token = order_from(offsets[head], 1)
-        pairs = queries[:, head, :].astype(F32)
+        pairs = queries[head].astype(F32)
         query = dot(to_order, beside(pairs, jnp.zeros_like(pairs))).astype(BF16)
         head_weight = weight[head * SIZE : (head + 1) * SIZE, :]
         grad = dot(full_grad[...], head_weight, NT).astype(BF16)
@@ -174,7 +173,7 @@
         dquery = dot(both, dscore, TN)[:SIZE, :].astype(BF16)
         attn[:, head * SIZE : (head + 1) * SIZE] = dot(to_token, attn_head, NT).astype(BF16)
         by_token = dot(to_token, jnp.concatenate([dquery, jnp.zeros_like(dquery)], axis=0), NT)
-        query_grad[:, head, :] = (by_token[:SIZE] + pltpu.roll(by_token[SIZE:], SIZE, 1)).astype(BF16)
+        query_grad[head] = (by_token[:SIZE] + pltpu.roll(by_token[SIZE:], SIZE, 1)).astype(BF16)
         dboth = dot(jnp.concatenate([dscore, rounded], axis=1), beside_grad)
         keep_own[:, lanes] = dboth[0:ROWS]
         send[REACH : REACH + NEAR, lanes] = dboth[PARTNER_AT:OTHER_AT].astype(BF16)
@@ -184,8 +183,10 @@
             at = pl.multiple_of(slot * BLOCK, 16)
             send[pl.ds(at, BLOCK), lanes] = dboth[OTHER_AT + step * BLOCK : OTHER_AT + (step + 1) * BLOCK].astype(BF16)
     part = dot(attn[...], weight[...])
-    output_part[:, :WIDTH] = part[:SIZE]
-    output_part[:, WIDTH:] = part[SIZE:]
+    for parity in range(2):
+        for half in range(2):
+            piece = part[parity * SIZE : (parity + 1) * SIZE, half * HALF : (half + 1) * HALF]
+            output_part[2 * parity + half] = piece.astype(BF16)
     weight_term[...] = dot(attn[...], full_grad[...], TN)
     rows = SHARE // 2
     mine = pl.ds(pl.multiple_of(core * rows, 8), rows)
@@ -211,52 +212,46 @@
     for slot in range(1, LINE):
         total = total + line_in[slot].astype(F32)
     near_sum[...] = total[:NEAR]
-    shape = (FAR * 8, PICKED + PART)
-    place = lax.broadcasted_iota(jnp.int32, shape, 0)
-    column = lax.broadcasted_iota(jnp.int32, shape, 1)
-    slot, row = place >> 3, place & 7
-    term = PICKED + slot * FINAL + row - 4
-    choose = ((row < 4) & (column < 12) & (far_place(column, rank[0]) == place)) | (
-        (row >= 4) & (row < 4 + FINAL) & (column == term)
-    )
-    picked = dot(one_hot(choose), total[NEAR:].astype(BF16)).astype(BF16)
-    far_out[...] = picked.reshape(FAR, 8, LANES)
+    place = lax.broadcasted_iota(jnp.int32, (FAR * 8, PICKED), 0)
+    row = lax.broadcasted_iota(jnp.int32, (FAR * 8, PICKED), 1)
+    choose = one_hot(far_place(row, rank[0]) == place)
+    picked = dot(choose, total[NEAR:BLOCK].astype(BF16))
+    for slot in range(FAR):
+        far_out[slot, 0:8, :] = picked[slot * 8 : (slot + 1) * 8].astype(BF16)
+        far_out[slot, 8:, :] = total[BLOCK:].astype(BF16)
 
 
 def spread_kernel(far_in, far_sum, spread_out):
     total = far_in[0].astype(F32)
     for slot in range(1, FAR):
         total = total + far_in[slot].astype(F32)
-    far_sum[...] = total
-    part = total[4:8].astype(BF16)
-    spread_out[...] = jnp.broadcast_to(part[None], spread_out.shape)
-
-
-def finish_kernel(offsets, keep_own, received, near_sum, far_sum, spread_in, key_grad, value_grad, weight_grad, own):
+    far_sum[...] = total[:8]
+    part = total[8:].astype(BF16)
+    for slot in range(LINE * CORE):
+        spread_out[slot] = part
+
+
+def finish_kernel(offsets, keep_own, received, near_sum, far_sum, key_grad, value_grad, own):
     own[...] = keep_own[...]
     own[NEAR : 2 * NEAR, :] += received[REACH : REACH + NEAR, :].astype(F32)
     own[0:NEAR, :] += near_sum[...]
-    row = lax.broadcasted_iota(jnp.int32, (8, LANES), 0)
-    own[0:8, :] += jnp.where(row < 4, far_sum[...], 0.0)
+    own[0:8, :] += far_sum[...]
     for head in range(LOCAL):
         to_token = order_from(offsets[head], 1)
         both = own[:, head * 2 * SIZE : (head + 1) * 2 * SIZE].astype(BF16)
         both = dot(to_token, both)
         even, odd = both[:SIZE], both[SIZE:]
         low = lane_iota(even.shape) < SIZE
-        key_grad[:, head, :] = jnp.where(low, even, pltpu.roll(odd, SIZE, 1)).astype(BF16)
-        value_grad[:, head, :] = jnp.where(low, pltpu.roll(even, SIZE, 1), odd).astype(BF16)
-    place = lax.broadcasted_iota(jnp.int32, (2 * SHARE, ROWS), 0)
-    device = lax.broadcasted_iota(jnp.int32, (2 * SHARE, ROWS), 1)
-    start = (device & 1) * SHARE + (device >> 1 & 7) * PART + (device >> 4) * FINAL
-    total = jnp.zeros((2 * SHARE, HALF), F32)
-    for term in range(FINAL):
-        total = total + dot(one_hot(place == start + term), spread_in[:, term, :])
-    rows = SHARE // 2
-    for core in range(CORE):
-        for half in range(2):
-            at = core * SHARE + half * rows
-            weight_grad[core * rows : (core + 1) * rows, half * HALF : (half + 1) * HALF] = total[at : at + rows]
+        key_grad[head] = jnp.where(low, even, pltpu.roll(odd, SIZE, 1)).astype(BF16)
+        value_grad[head] = jnp.where(low, pltpu.roll(even, SIZE, 1), odd).astype(BF16)
+
+
+def weight_kernel(spread_in, weight_grad):
+    for line in range(LINE):
+        half, row = line // 4, line % 4 * PART
+        for core in range(CORE):
+            at = core * SHARE // 2 + row
+            weight_grad[at : at + PART, half * HALF : (half + 1) * HALF] = spread_in[2 * line + core].astype(F32)
 
 
 def call(kernel, outs, args, scalars, scratch=()):
@@ -283,8 +278,8 @@
 
 def attention(rank, offsets, queries, weight, grads, ordered, line_in, partner_in, other_in):
     outs = [
-        ((SIZE, 2 * WIDTH), F32),
-        ((SIZE, LOCAL, 2 * SIZE), BF16),
+        ((4, SIZE, HALF), BF16),
+        ((LOCAL, SIZE, 2 * SIZE), BF16),
         ((SEND, LANES), BF16),
         ((LINE, BLOCK, LANES), F32),
         ((ROWS, LANES), F32),
@@ -305,19 +300,23 @@
 
 
 def far_return(rank, line_in):
-    outs = [((NEAR, LANES), F32), ((FAR, 8, LANES), BF16)]
+    outs = [((NEAR, LANES), F32), ((FAR, 8 + PART, LANES), BF16)]
     return call(far_return_kernel, outs, (rank, line_in), 1)
 
 
 def spread_pieces(far_in):
-    outs = [((8, LANES), F32), ((ROWS, 4, LANES), BF16)]
+    outs = [((8, LANES), F32), ((LINE * CORE, PART, LANES), BF16)]
     return call(spread_kernel, outs, (far_in,), 0)
 
 
-def finish(offsets, keep_own, received, near_sum, far_sum, spread_in):
-    outs = [((SIZE, LOCAL, 2 * SIZE), BF16)] * 2 + [((SHARE, WIDTH), F32)]
-    args = (offsets, keep_own, received, near_sum, far_sum, spread_in)
+def finish(offsets, keep_own, received, near_sum, far_sum):
+    outs = [((LOCAL, SIZE, 2 * SIZE), BF16)] * 2
+    args = (offsets, keep_own, received, near_sum, far_sum)
     return call(finish_kernel, outs, args, 1, [pltpu.VMEM((ROWS, LANES), F32)])
+
+
+def weight_rows(spread_in):
+    return call(weight_kernel, [((SHARE, WIDTH), F32)], (spread_in,), 0)[0]
 
 
 def trade(pieces, groups):
@@ -333,6 +332,8 @@
     rank = jnp.stack([index >> 4, index >> 1 & 7, index & 1]).astype(jnp.int32)
     far_groups = [[far * 16 + low for far in range(FAR)] for low in range(16)]
     line_groups = [[far * 16 + line * 2 + core for line in range(LINE)] for far in range(FAR) for core in range(CORE)]
+    near_groups = [[far * 16 + low for low in range(16)] for far in range(FAR)]
+    queries, keys, values = (array.transpose(1, 0, 2) for array in (queries, keys, values))
     ordered, far_out, partner_out, grad_out = start(offsets, keys, values, out_grad)
     partner_in = swap_cores(partner_out)
     far_in = trade(far_out, far_groups)
@@ -342,13 +343,15 @@
     output_part, query_grad, send, keep_line, keep_own, keep_weight = attention(
         rank, offsets, queries, out_weight, grads, ordered, line_in, partner_in, other_in
     )
-    output = lax.psum_scatter(output_part, "head", scatter_dimension=1, tiled=True).astype(BF16)
     received = swap_cores(send)
+    output_terms = lax.all_to_all(output_part, "head", 0, 0, tiled=True)
+    output = jnp.sum(output_terms.astype(F32), axis=0).astype(BF16)
     line_back = trade(line_return(received, keep_line, keep_weight), line_groups)
     near_sum, far_back = far_return(rank, line_back)
     far_sum, spread_out = spread_pieces(trade(far_back, far_groups))
-    spread_in = lax.all_to_all(spread_out, "seq", 0, 0, tiled=True)
-    key_grad, value_grad, weight_grad = finish(offsets, keep_own, received, near_sum, far_sum, spread_in)
+    weight_grad = weight_rows(trade(spread_out, near_groups))
+    key_grad, value_grad = finish(offsets, keep_own, received, near_sum, far_sum)
+    query_grad, key_grad, value_grad = (grad.transpose(1, 0, 2) for grad in (query_grad, key_grad, value_grad))
     return (output, query_grad, key_grad, value_grad, weight_grad)
 
 

time: 136 us -> 126 us (0.926)
  between operations: 14.2 us -> 0.72 us
  blocking collectives: 35.2 us -> 43.5 us
  waiting for transfers between devices: 28 us -> 25 us
    reduce_scatter x1 -> x0, waiting for transfers between devices: 15.1 us -> none  [shards(): lax.psum_scatter(output_part, 'head', scatter_dimension=1, tiled=True)]
    all_to_all x2 -> x3, blocking collectives: 35.2 us -> 43.5 us  [trade(): lax.all_to_all(pieces, 'seq', 0, 0, axis_index_groups=groups, tiled=True)]
    all_to_all x1, waiting for transfers between devices: 0.17 us -> 6.94 us  [shards(): output_terms = lax.all_to_all(output_part, 'head', 0, 0, tiled=True)]
    all_to_all x2, waiting for transfers between devices: 9.52 us -> 15.5 us  [trade(): lax.all_to_all(pieces, 'seq', 0, 0, axis_index_groups=groups, tiled=True)]
    all_to_all x2, starting transfers between devices: 10 us -> 13.8 us  [trade(): lax.all_to_all(pieces, 'seq', 0, 0, axis_index_groups=groups, tiled=True)]
    all_to_all x1, starting transfers between devices: 6.69 us -> 3.77 us  [shards(): output_terms = lax.all_to_all(output_part, 'head', 0, 0, tiled=True)]
    convert_element_type x1 -> x0, other arithmetic: 1.52 us -> none  [shards(): lax.psum_scatter(output_part, 'head', scatter_dimension=1, tiled=True)]
    pallas_call x7 -> x8, Pallas kernels: 13.2 us -> 12.1 us  [call(): pl.pallas_call(kernel, out_shape=[jax.ShapeDtypeStruct(shape, dtype) for...]
  transfers between devices with their start and end apart: 8 -> 7, of which waited for: 6 -> 5; matrix products, arithmetic and copies ran while one was open for 2% -> 1% of each run, Pallas kernels for 1% -> 2%
where the time goes in v2:
time: 126 us; the launch traced here: 125 us
  blocking collectives  43.5 us (35%)
  starting transfers between devices  40.2 us (32%)
  waiting for transfers between devices  25 us (20%)
  Pallas kernels  12.1 us (10%)
  local copies, waits for them, and re-layouts  3.06 us (2%)
    all_to_all x3, blocking collectives, trade(): lax.all_to_all(pieces, 'seq', 0, 0, axis_index_groups=groups, tiled=True)  43.5 us
    all_to_all x2, waiting for transfers between devices, trade(): lax.all_to_all(pieces, 'seq', 0, 0, axis_index_groups=groups, tiled=True)  15.5 us
    all_to_all x2, starting transfers between devices, trade(): lax.all_to_all(pieces, 'seq', 0, 0, axis_index_groups=groups, tiled=True)  13.8 us
    ppermute x3, starting transfers between devices, swap_cores(): lax.ppermute(block, 'seq', [(i, i ^ 1) for i in range(FAR * LINE * CORE)])  13.4 us
    pallas_call x8, Pallas kernels, call(): pl.pallas_call(kernel, out_shape=[jax.ShapeDtypeStruct(shape, dtype) for...  12.1 us
    all_to_all x1, starting transfers between devices, shards(): grads = lax.all_to_all(grad_out, 'head', 0, 0, tiled=True)  9.25 us
    all_to_all x1, waiting for transfers between devices, shards(): output_terms = lax.all_to_all(output_part, 'head', 0, 0, tiled=True)  6.94 us
    all_to_all x1, starting transfers between devices, shards(): output_terms = lax.all_to_all(output_part, 'head', 0, 0, tiled=True)  3.77 us
  transfers between devices with their start and end apart: 7, of which 5 were waited for; matrix products, arithmetic and copies ran while one was open for 1% of the time, Pallas kernels for 2%

profile of v2, /device:TPU:1, one launch (start us, length us, event | category | flops | bytes accessed | tf_op | source)
XLA Modules:
  0.0 125.3 jit_solution(11548545924331720329)
XLA Ops:
  0.6 0.0 copy-start.6
  0.6 0.6 copy-done.6
  1.3 0.0 copy-start.3
  1.3 0.8 copy-done.3
  2.1 0.0 copy-start.4
  2.1 0.8 copy-done.4
  2.9 0.0 copy-start.5
  2.9 0.8 copy-done.5
  3.7 1.4 %shard_map.110 = (bf16[128,384]{1,0:T(8,128)(2,1)S(1)}, bf16[8,8,384]{2,1,0:T(8,128)(2,1)}, bf16[32,384]{1,0:T(8,128)(2,1)S(1)}, bf16[4,64,384]{2,1,0:T(8,128)(2,1)}) custom-call(s32[3]{0:T(128)S(1)} %copy-done.6, bf16[3,64,128]{2,1,0:T(8,128)(2,1)S(1)} %bitcast.10, bf16[3,64,128]{2,1,0:T(8,128)(2,1)S(1)} %bitcast.11, bf16[64,384]{1,0:T(8,128)(2,1)S(1)} %copy-done.5), custom_call_target="tpu_custom_call" | custom-call | tf_op jit(solution)/shard_map/pallas_call | solution.py:260
  5.1 6.7 %all-to-all-start.1 = ((bf16[8,8,384]{2,1,0:T(8,128)(2,1)}), bf16[8,8,384]{2,1,0:T(8,128)(2,1)S(1)}, u32[]{:S(2)}, u32[]{:S(2)}) async-start(bf16[8,8,384]{2,1,0:T(8,128)(2,1)} %get-tuple-element.23), calls=%async_computation.1 | async-start | bytes 98304 | tf_op jit(solution)/shard_map/all_to_all | solution.py:323
  11.8 0.1 pad_add_fusion.rank
  11.8 5.1 %all-to-all-done.1.far_in = bf16[8,8,384]{2,1,0:T(8,128)(2,1)S(1)} async-done(((bf16[8,8,384]{2,1,0:T(8,128)(2,1)}), bf16[8,8,384]{2,1,0:T(8,128)(2,1)S(1)}, u32[]{:S(2)}, u32[]{:S(2)}) %all-to-all-start.1) | async-done | bytes 49184 | tf_op jit(solution)/shard_map/all_to_all | solution.py:323
  16.9 0.7 shard_map.111
  17.6 0.0 copy-start
  17.6 16.6 %all_to_all.35.line_in = bf16[8,48,384]{2,1,0:T(8,128)(2,1)S(1)} all-to-all(bf16[8,48,384]{2,1,0:T(8,128)(2,1)S(1)} %shard_map.111), channel_id=1, replica_groups={{0,8,16,24,32,40,48,56},{4,12,20,28,36,44,52,60},{64,72,80,88,96,104,11..., dimensions={0} | all-to-all | bytes 589824 | tf_op jit(solution)/shard_map/all_to_all | solution.py:323
  34.2 0.0 copy-start.1
  34.2 0.0 copy-start.2
  34.2 9.3 %all-to-all-start = ((bf16[4,64,384]{2,1,0:T(8,128)(2,1)}), bf16[4,64,384]{2,1,0:T(8,128)(2,1)S(1)}, u32[]{:S(2)}, u32[]{:S(2)}) async-start(bf16[4,64,384]{2,1,0:T(8,128)(2,1)} %get-tuple-element.21), calls=%async_computation | async-start | bytes 393216 | tf_op jit(solution)/shard_map/all_to_all | solution.py:342
  43.4 5.9 %collective-permute-start.1 = (bf16[8,48,384]{2,1,0:T(8,128)(2,1)S(1)}, bf16[8,48,384]{2,1,0:T(8,128)(2,1)S(1)}, u32[]{:S(2)}, u32[]{:S(2)}) collective-permute-start(bf16[8,48,384]{2,1,0:T(8,128)(2,1)S(1)} %all_to_all.35.line_in), channel_id=1, source_target_pairs={{0,4},{4,0},{8,12},{12,8},{16,20},{20,16},{24,28},{28,24},{32,36},... | collective-permute-start | bytes 884744 | tf_op jit(solution)/shard_map/ppermute | solution.py:327
  49.3 1.9 %collective-permute-start = (bf16[32,384]{1,0:T(8,128)(2,1)S(1)}, bf16[32,384]{1,0:T(8,128)(2,1)S(1)}, u32[]{:S(2)}, u32[]{:S(2)}) collective-permute-start(bf16[32,384]{1,0:T(8,128)(2,1)S(1)} %get-tuple-element.24), channel_id=1, source_target_pairs={{0,4},{4,0},{8,12},{12,8},{16,20},{20,16},{24,28},{28,24},{32,36},... | collective-permute-start | bytes 73736 | tf_op jit(solution)/shard_map/ppermute | solution.py:327
  51.2 1.2 collective-permute-done.partner_in
  52.4 0.0 all-to-all-done.grads
  52.4 0.0 collective-permute-done.1.other_in
  52.4 0.0 copy-done
  52.4 0.0 copy-done.1
  52.4 0.0 copy-done.2
  52.4 6.2 %shard_map.112 = (bf16[4,64,384]{2,1,0:T(8,128)(2,1)}, bf16[3,64,128]{2,1,0:T(8,128)(2,1)}, bf16[608,384]{1,0:T(8,128)(2,1)S(1)}, f32[8,48,384]{2,1,0:T(8,128)S(...) custom-call(s32[3]{0:T(128)S(1)} %pad_add_fusion.rank, s32[3]{0:T(128)S(1)} %copy-done.6, ...), custom_call_target="tpu_custom_call" | custom-call | tf_op jit(solution)/shard_map/pallas_call | solution.py:260
  58.6 5.6 %collective-permute-start.2 = (bf16[608,384]{1,0:T(8,128)(2,1)S(1)}, bf16[608,384]{1,0:T(8,128)(2,1)S(1)}, u32[]{:S(2)}, u32[]{:S(2)}) collective-permute-start(bf16[608,384]{1,0:T(8,128)(2,1)S(1)} %get-tuple-element.28), channel_id=1, source_target_pairs={{0,4},{4,0},{8,12},{12,8},{16,20},{20,16},{24,28},{28,24},{32,36},... | collective-permute-start | bytes 1400840 | tf_op jit(solution)/shard_map/ppermute | solution.py:327
  64.3 1.4 %collective-permute-done.2.received = bf16[608,384]{1,0:T(8,128)(2,1)S(1)} collective-permute-done((bf16[608,384]{1,0:T(8,128)(2,1)S(1)}, bf16[608,384]{1,0:T(8,128)(2,1)S(1)}, u32[]{:S(2)}, u32[]{:S(2)}) %collective-permute-start.2) | collective-permute-done | bytes 466976 | tf_op jit(solution)/shard_map/ppermute | solution.py:327
  65.7 0.1 shard_map.113
  65.8 18.6 %all_to_all.36.line_in = bf16[8,72,384]{2,1,0:T(8,128)(2,1)S(1)} all-to-all(bf16[8,72,384]{2,1,0:T(8,128)(2,1)S(1)} %shard_map.113), channel_id=1, replica_groups={{0,8,16,24,32,40,48,56},{4,12,20,28,36,44,52,60},{64,72,80,88,96,104,11..., dimensions={0} | all-to-all | bytes 884736 | tf_op jit(solution)/shard_map/all_to_all | solution.py:323
  84.4 0.7 shard_map.114
  85.1 8.3 %all_to_all.37.far_in = bf16[8,32,384]{2,1,0:T(8,128)(2,1)S(1)} all-to-all(bf16[8,32,384]{2,1,0:T(8,128)(2,1)S(1)} %get-tuple-element.32), channel_id=1, replica_groups={{0,64,128,192,256,320,384,448},{4,68,132,196,260,324,388,452},{8,72,136..., dimensions={0} | all-to-all | bytes 393216 | tf_op jit(solution)/shard_map/all_to_all | solution.py:323
  93.4 3.8 %all-to-all-start.3 = ((bf16[4,64,384]{2,1,0:T(8,128)(2,1)}), bf16[4,64,384]{2,1,0:T(8,128)(2,1)S(1)}, u32[]{:S(2)}, u32[]{:S(2)}) async-start(bf16[4,64,384]{2,1,0:T(8,128)(2,1)} %get-tuple-element.25), calls=%async_computation.3 | async-start | bytes 393216 | tf_op jit(solution)/shard_map/all_to_all | solution.py:347
  97.2 0.7 shard_map.115
  97.9 6.9 %all-to-all-done.3 = bf16[4,64,384]{2,1,0:T(8,128)(2,1)S(1)} async-done(((bf16[4,64,384]{2,1,0:T(8,128)(2,1)}), bf16[4,64,384]{2,1,0:T(8,128)(2,1)S(1)}, u32[]{:S(2)}, u32[]{:S(2)}) %all-to-all-start.3) | async-done | bytes 196640 | tf_op jit(solution)/shard_map/all_to_all | solution.py:347
  104.9 7.1 %all-to-all-start.6 = ((bf16[16,24,384]{2,1,0:T(8,128)(2,1)}), bf16[16,24,384]{2,1,0:T(8,128)(2,1)S(1)}, u32[]{:S(2)}, u32[]{:S(2)}) async-start(bf16[16,24,384]{2,1,0:T(8,128)(2,1)} %get-tuple-element.36), calls=%async_computation.6 | async-start | bytes 589824 | tf_op jit(solution)/shard_map/all_to_all | solution.py:323
  112.0 0.7 reduce_sum.12
  112.6 1.4 %shard_map.116 = (bf16[3,64,128]{2,1,0:T(8,128)(2,1)}, bf16[3,64,128]{2,1,0:T(8,128)(2,1)}) custom-call(s32[3]{0:T(128)S(1)} %copy-done.6, f32[128,384]{1,0:T(8,128)S(1)} %get-tuple-element.27.keep_own, bf16[608,384]{1,0:T(8,128)(2,1)S(1)} %collective-permute-done.2.received, f32[32,384]{1,0:T(8,128)S(1)} %get-tuple-element.31.near_sum, ...), custom_call_target="tpu_custom_call" | custom-call | tf_op jit(solution)/shard_map/pallas_call | solution.py:260
  114.1 10.4 %all-to-all-done.6.spread_in = bf16[16,24,384]{2,1,0:T(8,128)(2,1)S(1)} async-done(((bf16[16,24,384]{2,1,0:T(8,128)(2,1)}), bf16[16,24,384]{2,1,0:T(8,128)(2,1)S(1)}, u32[]{:S(2)}, u32[]{:S(2)}) %all-to-all-start.6) | async-done | bytes 294944 | tf_op jit(solution)/shard_map/all_to_all | solution.py:323
  124.4 0.9 shard_map.117
Async XLA Ops:
  0.6 0.7 copy-start.6
  1.3 0.8 copy-start.3
  2.1 0.8 copy-start.4
  2.9 0.8 copy-start.5
  5.1 11.8 %all-to-all-start.1 = ((bf16[8,8,384]{2,1,0:T(8,128)(2,1)}), bf16[8,8,384]{2,1,0:T(8,128)(2,1)S(1)}, u32[]{:S(2)}, u32[]{:S(2)}) async-start(bf16[8,8,384]{2,1,0:T(8,128)(2,1)} %get-tuple-element.23), calls=%async_computation.1 | async-start | bytes 98304 | tf_op jit(solution)/shard_map/all_to_all | solution.py:323
  17.6 34.8 %copy-start = (f32[928,128]{1,0:T(8,128)S(1)}, f32[928,128]{1,0:T(8,128)}, u32[]{:S(2)}) copy-start(f32[928,128]{1,0:T(8,128)} %constant.17.clone.bias) | copy-start | bytes 1425412
  34.2 18.3 %copy-start.1 = (bf16[192,768]{1,0:T(8,128)(2,1)S(1)}, bf16[192,768]{1,0:T(8,128)(2,1)}, u32[]{:S(2)}) copy-start(bf16[192,768]{1,0:T(8,128)(2,1)} %weight.1) | copy-start | bytes 884740
  34.2 18.3 %copy-start.2 = (bf16[64,3,128]{2,0,1:T(8,128)(2,1)S(1)}, bf16[64,3,128]{2,0,1:T(8,128)(2,1)}, u32[]{:S(2)}) copy-start(bf16[64,3,128]{2,0,1:T(8,128)(2,1)} %param.7) | copy-start | bytes 147460
  34.2 18.3 %all-to-all-start = ((bf16[4,64,384]{2,1,0:T(8,128)(2,1)}), bf16[4,64,384]{2,1,0:T(8,128)(2,1)S(1)}, u32[]{:S(2)}, u32[]{:S(2)}) async-start(bf16[4,64,384]{2,1,0:T(8,128)(2,1)} %get-tuple-element.21), calls=%async_computation | async-start | bytes 393216 | tf_op jit(solution)/shard_map/all_to_all | solution.py:342
  43.4 9.0 %collective-permute-start.1 = (bf16[8,48,384]{2,1,0:T(8,128)(2,1)S(1)}, bf16[8,48,384]{2,1,0:T(8,128)(2,1)S(1)}, u32[]{:S(2)}, u32[]{:S(2)}) collective-permute-start(bf16[8,48,384]{2,1,0:T(8,128)(2,1)S(1)} %all_to_all.35.line_in), channel_id=1, source_target_pairs={{0,4},{4,0},{8,12},{12,8},{16,20},{20,16},{24,28},{28,24},{32,36},... | collective-permute-start | bytes 884744 | tf_op jit(solution)/shard_map/ppermute | solution.py:327
  49.3 3.1 %collective-permute-start = (bf16[32,384]{1,0:T(8,128)(2,1)S(1)}, bf16[32,384]{1,0:T(8,128)(2,1)S(1)}, u32[]{:S(2)}, u32[]{:S(2)}) collective-permute-start(bf16[32,384]{1,0:T(8,128)(2,1)S(1)} %get-tuple-element.24), channel_id=1, source_target_pairs={{0,4},{4,0},{8,12},{12,8},{16,20},{20,16},{24,28},{28,24},{32,36},... | collective-permute-start | bytes 73736 | tf_op jit(solution)/shard_map/ppermute | solution.py:327
  58.6 7.1 %collective-permute-start.2 = (bf16[608,384]{1,0:T(8,128)(2,1)S(1)}, bf16[608,384]{1,0:T(8,128)(2,1)S(1)}, u32[]{:S(2)}, u32[]{:S(2)}) collective-permute-start(bf16[608,384]{1,0:T(8,128)(2,1)S(1)} %get-tuple-element.28), channel_id=1, source_target_pairs={{0,4},{4,0},{8,12},{12,8},{16,20},{20,16},{24,28},{28,24},{32,36},... | collective-permute-start | bytes 1400840 | tf_op jit(solution)/shard_map/ppermute | solution.py:327
  93.4 11.5 %all-to-all-start.3 = ((bf16[4,64,384]{2,1,0:T(8,128)(2,1)}), bf16[4,64,384]{2,1,0:T(8,128)(2,1)S(1)}, u32[]{:S(2)}, u32[]{:S(2)}) async-start(bf16[4,64,384]{2,1,0:T(8,128)(2,1)} %get-tuple-element.25), calls=%async_computation.3 | async-start | bytes 393216 | tf_op jit(solution)/shard_map/all_to_all | solution.py:347
  104.9 19.6 %all-to-all-start.6 = ((bf16[16,24,384]{2,1,0:T(8,128)(2,1)}), bf16[16,24,384]{2,1,0:T(8,128)(2,1)S(1)}, u32[]{:S(2)}, u32[]{:S(2)}) async-start(bf16[16,24,384]{2,1,0:T(8,128)(2,1)} %get-tuple-element.36), calls=%async_computation.6 | async-start | bytes 589824 | tf_op jit(solution)/shard_map/all_to_all | solution.py:323

commit v3 on v2

v3 whole, which is shorter than its diff:
```python
import math

import jax
import jax.numpy as jnp
import numpy as np
from jax import lax
from jax.experimental import pallas as pl
from jax.experimental.pallas import tpu as pltpu
from jax.sharding import PartitionSpec as P

FAR, LINE, CORE = 8, 8, 2
ROWS = 128
LOCAL = 3
SIZE = 64
LANES = LOCAL * 2 * SIZE
WIDTH = 768
HALF = WIDTH // 2
SCALE = SIZE**-0.5
NEAR = 32
EACH = 4
PICKED = 96
SLOTS = LINE * NEAR
LINE_AT = ROWS
FAR_AT = LINE_AT + SLOTS - NEAR
PARTNER_AT = FAR_AT + PICKED
OTHER_AT = PARTNER_AT + NEAR
OTHER_FAR_AT = OTHER_AT + SLOTS
KEYS = OTHER_FAR_AT + PICKED
SHARE = 192
PART = SHARE // FAR
SEND_FAR = SLOTS + NEAR
SEND_WEIGHT = SEND_FAR + PICKED
SEND = SEND_WEIGHT + SHARE

NT = (((1,), (1,)), ((), ()))
TN = (((0,), (0,)), ((), ()))
NN = (((1,), (0,)), ((), ()))
BF16 = jnp.bfloat16
F32 = jnp.float32


def dot(a, b, dims=NN):
    return lax.dot_general(a, b, dims, preferred_element_type=F32)


def depth_of(row):
    return 7 if row == 0 else 7 - row.bit_length()


def far_table():
    table = [(1, row) for line in range(LINE) for row in range(4)]
    table += [(far, row) for far in (2, 3) for line in range(LINE) for row in range(2)]
    return table + [(far, 0) for far in range(4, 8) for line in range(LINE)]


def key_table():
    table = [(-1, depth_of(row)) for row in range(ROWS)]
    for core in range(CORE):
        if core:
            table += [(0, depth_of(NEAR + row)) for row in range(NEAR)]
        for line in range(1 - core, LINE):
            table += [(line.bit_length(), depth_of(row)) for row in range(NEAR)]
        table += [(3 + far.bit_length(), depth_of(row)) for far, row in far_table()]
    return table


def shared_levels():
    table = key_table()
    bias = np.full((KEYS, ROWS), -1e30, np.float32)
    for key, entry in enumerate(table):
        for query in range(ROWS):
            count = min(entry[1], depth_of(query)) - entry[0]
            if count > 0:
                bias[key, query] = math.log(count)
    return bias


def reversed_bits(row):
    out = row * 0
    for bit in range(7):
        out = out | ((row >> bit) & 1) << (6 - bit)
    return out


def token_of(row):
    return jnp.where(row < SIZE, 2 * row, 2 * row - (ROWS - 1))


def one_hot(match):
    return jnp.where(match, 1.0, 0.0).astype(BF16)


def order_from(offset, row_axis):
    row = lax.broadcasted_iota(jnp.int32, (ROWS, ROWS), row_axis)
    token = token_of(lax.broadcasted_iota(jnp.int32, (ROWS, ROWS), 1 - row_axis))
    return one_hot(((reversed_bits(row) + offset) & (ROWS - 1)) == token)


def lane_iota(shape):
    return lax.broadcasted_iota(jnp.int32, shape, len(shape) - 1)


def beside(first, second):
    low = lane_iota(first.shape) < SIZE
    even = jnp.where(low, first, pltpu.roll(second, SIZE, 1))
    odd = jnp.where(low, pltpu.roll(first, SIZE, 1), second)
    return jnp.concatenate([even, odd], axis=0).astype(BF16)


def start_kernel(offsets, keys, values, grad, ordered, line_out, partner_out, grad_out, keys_here, values_here, grad_here, done):
    copies = [
        pltpu.make_async_copy(source, target, done.at[at])
        for at, (source, target) in enumerate(((keys, keys_here), (values, values_here), (grad, grad_here)))
    ]
    for copy in copies:
        copy.start()
    orders = [order_from(offsets[head], 0) for head in range(LOCAL)]
    for copy in copies:
        copy.wait()
    for head in range(LOCAL):
        lanes = pl.ds(head * 2 * SIZE, 2 * SIZE)
        both = beside(keys_here[head].astype(F32), values_here[head].astype(F32))
        ordered[:, lanes] = dot(orders[head], both).astype(BF16)
    for slot in range(LINE):
        line_out[slot] = ordered[0:NEAR, :]
    partner_out[...] = ordered[NEAR : 2 * NEAR, :]
    for slot in range(4):
        grad_out[slot] = grad_here[...]


def far_place(row, far):
    second, third = row - 32, row - 64
    distance = jnp.where(row < 32, 1, jnp.where(row < 64, 2 + (second >> 4), 4 + (third >> 3)))
    line = jnp.where(row < 32, row >> 2, jnp.where(row < 64, (second >> 1) & 7, third & 7))
    index = jnp.where(row < 32, row & 3, jnp.where(row < 64, second & 1, 0))
    return ((far ^ distance) * LINE + line) * EACH + index


def far_choice(far, row_axis):
    shape = (PICKED, FAR * NEAR) if row_axis == 0 else (FAR * NEAR, PICKED)
    row = lax.broadcasted_iota(jnp.int32, shape, row_axis)
    return one_hot(far_place(row, far) == lax.broadcasted_iota(jnp.int32, shape, 1 - row_axis))


def far_kernel(line_in, far_out):
    low = lax.broadcasted_iota(jnp.int32, (8, LANES), 0) < EACH
    for pair in range(LINE // 2):
        first, second = (line_in[2 * pair + slot, 0:16, :].astype(F32)[:8] for slot in range(2))
        rows = jnp.where(low, first, pltpu.roll(second, EACH, 0)).astype(BF16)
        for slot in range(FAR):
            far_out[slot, pair * 8 : (pair + 1) * 8, :] = rows


def main_kernel(
    rank, offsets, queries, weight, grads, ordered, line_in, far_in, partner_in, other_in, other_far_in, bias,
    output_part, query_grad, send, keep_line, keep_far, keep_own, keep_weight,
    held, full_grad, attn, weight_term,
):
    far, line, core = rank[0], rank[1], rank[2]
    held[0:ROWS, :] = ordered[...]
    held[PARTNER_AT:OTHER_AT, :] = partner_in[...]
    choice = far_choice(far, 0)
    held[FAR_AT:PARTNER_AT, :] = dot(choice, far_in[...].reshape(FAR * NEAR, LANES)).astype(BF16)
    held[OTHER_FAR_AT:, :] = dot(choice, other_far_in[...].reshape(FAR * NEAR, LANES)).astype(BF16)
    for step in range(LINE):
        slot = line ^ step
        if step:
            at = LINE_AT + (step - 1) * NEAR
            held[at : at + NEAR, :] = line_in[slot]
        at = OTHER_AT + step * NEAR
        held[at : at + NEAR, :] = other_in[slot]
    for parity in range(2):
        for half in range(2):
            full_grad[parity * SIZE : (parity + 1) * SIZE, half * HALF : (half + 1) * HALF] = grads[2 * parity + half]
    for head in range(LOCAL):
        lanes = pl.ds(head * 2 * SIZE, 2 * SIZE)
        to_order = order_from(offsets[head], 0)
        to_token = order_from(offsets[head], 1)
        pairs = queries[head].astype(F32)
        query = dot(to_order, beside(pairs, jnp.zeros_like(pairs))).astype(BF16)
        head_weight = weight[head * SIZE : (head + 1) * SIZE, :]
        grad = dot(full_grad[...], head_weight, NT).astype(BF16)
        grad = dot(to_order, jnp.concatenate([jnp.zeros_like(grad), grad], axis=1)).astype(BF16)
        beside_grad = jnp.concatenate([query, grad], axis=0)
        both = held[:, lanes]
        products = dot(both, beside_grad, NT)
        scores = products[:, :ROWS] * SCALE + bias[...]
        top = jnp.max(scores, axis=0, keepdims=True)
        expd = jnp.exp(scores - top)
        probs = expd / jnp.sum(expd, axis=0, keepdims=True)
        rounded = probs.astype(BF16)
        attn_head = dot(both, rounded, TN)[SIZE:, :].astype(BF16)
        grad_side = grad.astype(F32).T
        delta = jnp.sum(grad_side[SIZE:, :] * attn_head.astype(F32), axis=0, keepdims=True)
        dscore = (probs * (products[:, ROWS:] - delta) * SCALE).astype(BF16)
        dquery = dot(both, dscore, TN)[:SIZE, :].astype(BF16)
        attn[:, head * SIZE : (head + 1) * SIZE] = dot(to_token, attn_head, NT).astype(BF16)
        by_token = dot(to_token, jnp.concatenate([dquery, jnp.zeros_like(dquery)], axis=0), NT)
        query_grad[head] = (by_token[:SIZE] + pltpu.roll(by_token[SIZE:], SIZE, 1)).astype(BF16)
        dboth = dot(jnp.concatenate([dscore, rounded], axis=1), beside_grad)
        keep_own[:, lanes] = dboth[0:ROWS]
        keep_far[:, lanes] = dboth[FAR_AT:PARTNER_AT]
        send[SLOTS:SEND_FAR, lanes] = dboth[PARTNER_AT:OTHER_AT].astype(BF16)
        send[SEND_FAR:SEND_WEIGHT, lanes] = dboth[OTHER_FAR_AT:].astype(BF16)
        for step in range(LINE):
            slot = line ^ step
            at = LINE_AT + (step - 1) * NEAR
            keep_line[slot, :, lanes] = dboth[at : at + NEAR] if step else jnp.zeros((NEAR, 2 * SIZE), F32)
            at = OTHER_AT + step * NEAR
            rows = pl.ds(pl.multiple_of(slot * NEAR, NEAR), NEAR)
            send[rows, lanes] = dboth[at : at + NEAR].astype(BF16)
    part = dot(attn[...], weight[...])
    for parity in range(2):
        for half in range(2):
            piece = part[parity * SIZE : (parity + 1) * SIZE, half * HALF : (half + 1) * HALF]
            output_part[2 * parity + half] = piece.astype(BF16)
    weight_term[...] = dot(attn[...], full_grad[...], TN)
    rows = SHARE // 2
    mine = pl.ds(pl.multiple_of(core * rows, 8), rows)
    theirs = pl.ds(pl.multiple_of((1 - core) * rows, 8), rows)
    for half in range(2):
        columns = pl.ds(half * HALF, HALF)
        keep_weight[half * rows : (half + 1) * rows, :] = weight_term[mine, columns]
        at = SEND_WEIGHT + half * rows
        send[at : at + rows, :] = weight_term[theirs, columns].astype(BF16)


def far_return_kernel(rank, received, keep_far, keep_weight, far_out):
    picked = (keep_far[...] + received[SEND_FAR:SEND_WEIGHT, :].astype(F32)).astype(BF16)
    rows = dot(far_choice(rank[0], 1), picked).astype(BF16)
    weight = (keep_weight[...] + received[SEND_WEIGHT:, :].astype(F32)).astype(BF16)
    for slot in range(FAR):
        far_out[slot, 0:NEAR, :] = rows[slot * NEAR : (slot + 1) * NEAR]
        far_out[slot, NEAR:, :] = weight[slot * PART : (slot + 1) * PART]


def line_return_kernel(received, keep_line, far_in, line_out):
    total = far_in[0].astype(F32)
    for slot in range(1, FAR):
        total = total + far_in[slot].astype(F32)
    low = lax.broadcasted_iota(jnp.int32, (8, LANES), 0) < EACH
    for slot in range(LINE):
        rows = keep_line[slot] + received[slot * NEAR : (slot + 1) * NEAR, :].astype(F32)
        both = total[slot // 2 * 8 : slot // 2 * 8 + 8]
        first = jnp.where(low, pltpu.roll(both, EACH, 0) if slot % 2 else both, 0.0)
        line_out[slot, 0:NEAR, :] = jnp.concatenate([rows[:8] + first, rows[8:]], axis=0).astype(BF16)
        line_out[slot, NEAR:, :] = total[NEAR:].astype(BF16)


def spread_kernel(line_in, near_sum, spread_out):
    total = line_in[0].astype(F32)
    for slot in range(1, LINE):
        total = total + line_in[slot].astype(F32)
    near_sum[...] = total[:NEAR]
    part = total[NEAR:].astype(BF16)
    for slot in range(FAR * CORE):
        spread_out[slot] = part


def finish_kernel(offsets, keep_own, received, near_sum, key_grad, value_grad, own):
    own[...] = keep_own[...]
    own[NEAR : 2 * NEAR, :] += received[SLOTS:SEND_FAR, :].astype(F32)
    own[0:NEAR, :] += near_sum[...]
    for head in range(LOCAL):
        to_token = order_from(offsets[head], 1)
        both = own[:, head * 2 * SIZE : (head + 1) * 2 * SIZE].astype(BF16)
        both = dot(to_token, both)
        even, odd = both[:SIZE], both[SIZE:]
        low = lane_iota(even.shape) < SIZE
        key_grad[head] = jnp.where(low, even, pltpu.roll(odd, SIZE, 1)).astype(BF16)
        value_grad[head] = jnp.where(low, pltpu.roll(even, SIZE, 1), odd).astype(BF16)


def weight_kernel(spread_in, weight_grad):
    for far in range(FAR):
        half, row = far // 4, far % 4 * PART
        for core in range(CORE):
            at = core * SHARE // 2 + row
            weight_grad[at : at + PART, half * HALF : (half + 1) * HALF] = spread_in[CORE * far + core].astype(F32)


def call(kernel, outs, args, scalars, scratch=(), space=pltpu.VMEM):
    return pl.pallas_call(
        kernel,
        out_shape=[jax.ShapeDtypeStruct(shape, dtype) for shape, dtype in outs],
        in_specs=[pl.BlockSpec(memory_space=pltpu.SMEM)] * scalars
        + [pl.BlockSpec(memory_space=space)] * (len(args) - scalars),
        out_specs=[pl.BlockSpec(memory_space=pltpu.VMEM)] * len(outs),
        scratch_shapes=list(scratch),
        compiler_params=pltpu.CompilerParams(vmem_limit_bytes=48 * 2**20),
    )(*args)


def start(offsets, keys, values, grad):
    outs = [((ROWS, LANES), BF16), ((LINE, NEAR, LANES), BF16), ((NEAR, LANES), BF16), ((4, SIZE, HALF), BF16)]
    scratch = [pltpu.VMEM((LOCAL, SIZE, 2 * SIZE), BF16)] * 2 + [pltpu.VMEM((SIZE, HALF), BF16), pltpu.SemaphoreType.DMA((3,))]
    return call(start_kernel, outs, (offsets, keys, values, grad), 1, scratch, pltpu.HBM)


def far_pieces(line_in):
    return call(far_kernel, [((FAR, NEAR, LANES), BF16)], (line_in,), 0)[0]


def attention(rank, offsets, *arrays):
    outs = [
        ((4, SIZE, HALF), BF16),
        ((LOCAL, SIZE, 2 * SIZE), BF16),
        ((SEND, LANES), BF16),
        ((LINE, NEAR, LANES), F32),
        ((PICKED, LANES), F32),
        ((ROWS, LANES), F32),
        ((SHARE, HALF), F32),
    ]
    scratch = [
        pltpu.VMEM((KEYS, LANES), BF16),
        pltpu.VMEM((ROWS, WIDTH), BF16),
        pltpu.VMEM((ROWS, LOCAL * SIZE), BF16),
        pltpu.VMEM((SHARE, WIDTH), F32),
    ]
    return call(main_kernel, outs, (rank, offsets) + arrays + (jnp.asarray(shared_levels()),), 2, scratch)


def far_return(rank, received, keep_far, keep_weight):
    args = (rank, received, keep_far, keep_weight)
    return call(far_return_kernel, [((FAR, NEAR + PART, LANES), BF16)], args, 1)[0]


def line_return(received, keep_line, far_in):
    return call(line_return_kernel, [((LINE, NEAR + PART, LANES), BF16)], (received, keep_line, far_in), 0)[0]


def spread_pieces(line_in):
    outs = [((NEAR, LANES), F32), ((FAR * CORE, PART, LANES), BF16)]
    return call(spread_kernel, outs, (line_in,), 0)


def finish(offsets, keep_own, received, near_sum):
    outs = [((LOCAL, SIZE, 2 * SIZE), BF16)] * 2
    return call(finish_kernel, outs, (offsets, keep_own, received, near_sum), 1, [pltpu.VMEM((ROWS, LANES), F32)])


def weight_rows(spread_in):
    return call(weight_kernel, [((SHARE, WIDTH), F32)], (spread_in,), 0)[0]


def trade(pieces, groups):
    return lax.all_to_all(pieces, "seq", 0, 0, axis_index_groups=groups, tiled=True)


def swap_cores(block):
    return lax.ppermute(block, "seq", [(i, i ^ 1) for i in range(FAR * LINE * CORE)])


def shards(queries, keys, values, out_weight, offsets, out_grad):
    index = lax.axis_index("seq")
    rank = jnp.stack([index >> 4, index >> 1 & 7, index & 1]).astype(jnp.int32)
    far_groups = [[far * 16 + low for far in range(FAR)] for low in range(16)]
    line_groups = [[far * 16 + line * 2 + core for line in range(LINE)] for far in range(FAR) for core in range(CORE)]
    side_groups = [[far * 16 + line * 2 + core for far in range(FAR) for core in range(CORE)] for line in range(LINE)]
    queries, keys, values = (array.transpose(1, 0, 2) for array in (queries, keys, values))
    ordered, line_out, partner_out, grad_out = start(offsets, keys, values, out_grad)
    partner_in = swap_cores(partner_out)
    line_in = trade(line_out, line_groups)
    other_in = swap_cores(line_in)
    far_in = trade(far_pieces(line_in), far_groups)
    other_far_in = swap_cores(far_in)
    grads = lax.all_to_all(grad_out, "head", 0, 0, tiled=True)
    output_part, query_grad, send, keep_line, keep_far, keep_own, keep_weight = attention(
        rank, offsets, queries, out_weight, grads, ordered, line_in, far_in, partner_in, other_in, other_far_in
    )
    received = swap_cores(send)
    output_terms = lax.all_to_all(output_part, "head", 0, 0, tiled=True)
    far_out = far_return(rank, received, keep_far, keep_weight)
    far_out, output_terms = lax.optimization_barrier((far_out, output_terms))
    output = jnp.sum(output_terms.astype(F32), axis=0).astype(BF16)
    line_back = trade(line_return(received, keep_line, trade(far_out, far_groups)), line_groups)
    near_sum, spread_out = spread_pieces(line_back)
    weight_grad = weight_rows(trade(spread_out, side_groups))
    key_grad, value_grad = finish(offsets, keep_own, received, near_sum)
    query_grad, key_grad, value_grad = (grad.transpose(1, 0, 2) for grad in (query_grad, key_grad, value_grad))
    return (output, query_grad, key_grad, value_grad, weight_grad)


def solution(mesh):
    return jax.shard_map(
        shards,
        mesh=mesh,
        in_specs=(
            P("seq", "head", None),
            P("seq", "head", None),
            P("seq", "head", None),
            P("head", None),
            P("head"),
            P("seq", "head"),
        ),
        out_specs=(
            P("seq", "head"),
            P("seq", "head", None),
            P("seq", "head", None),
            P("seq", "head", None),
            P("head", None),
        ),
        check_vma=False,
    )
```

time: 126 us -> 117 us (0.929)
  waiting for transfers between devices: 25 us -> 13.5 us
  blocking collectives: 43.5 us -> 49.5 us
  starting transfers between devices: 40.2 us -> 36.8 us
    all_to_all x2 -> x1, waiting for transfers between devices: 15.5 us -> 5.38 us  [trade(): lax.all_to_all(pieces, 'seq', 0, 0, axis_index_groups=groups, tiled=True)]
    all_to_all x3 -> x4, blocking collectives: 43.5 us -> 49.5 us  [trade(): lax.all_to_all(pieces, 'seq', 0, 0, axis_index_groups=groups, tiled=True)]
    all_to_all x2 -> x1, starting transfers between devices: 13.8 us -> 7.87 us  [trade(): lax.all_to_all(pieces, 'seq', 0, 0, axis_index_groups=groups, tiled=True)]
    all_to_all x1, starting transfers between devices: 3.77 us -> 5.65 us  [shards(): output_terms = lax.all_to_all(output_part, 'head', 0, 0, tiled=True)]
    ppermute x3 -> x4, waiting for transfers between devices: 2.6 us -> 0.75 us  [swap_cores(): lax.ppermute(block, 'seq', [(i, i ^ 1) for i in range(FAR * LINE * CORE)])]
    ppermute x3 -> x4, starting transfers between devices: 13.4 us -> 14.1 us  [swap_cores(): lax.ppermute(block, 'seq', [(i, i ^ 1) for i in range(FAR * LINE * CORE)])]
  transfers between devices with their start and end apart: 7 -> 7, of which waited for: 5 -> 3; matrix products, arithmetic and copies ran while one was open for 1% -> 1% of each run, Pallas kernels for 2% -> 2%
where the time goes in v3:
time: 117 us; the launch traced here: 116 us
  blocking collectives  49.5 us (42%)
  starting transfers between devices  36.8 us (31%)
  waiting for transfers between devices  13.5 us (12%)
  Pallas kernels  11.5 us (10%)
  local copies, waits for them, and re-layouts  3.06 us (3%)
    all_to_all x4, blocking collectives, trade(): lax.all_to_all(pieces, 'seq', 0, 0, axis_index_groups=groups, tiled=True)  49.5 us
    ppermute x4, starting transfers between devices, swap_cores(): lax.ppermute(block, 'seq', [(i, i ^ 1) for i in range(FAR * LINE * CORE)])  14.1 us
    pallas_call x8, Pallas kernels, call(): pl.pallas_call(kernel, out_shape=[jax.ShapeDtypeStruct(shape, dtype) for...  11.5 us
    all_to_all x1, starting transfers between devices, shards(): grads = lax.all_to_all(grad_out, 'head', 0, 0, tiled=True)  9.24 us
    all_to_all x1, starting transfers between devices, trade(): lax.all_to_all(pieces, 'seq', 0, 0, axis_index_groups=groups, tiled=True)  7.87 us
    all_to_all x1, waiting for transfers between devices, shards(): output_terms = lax.all_to_all(output_part, 'head', 0, 0, tiled=True)  7.38 us
    all_to_all x1, starting transfers between devices, shards(): output_terms = lax.all_to_all(output_part, 'head', 0, 0, tiled=True)  5.65 us
    all_to_all x1, waiting for transfers between devices, trade(): lax.all_to_all(pieces, 'seq', 0, 0, axis_index_groups=groups, tiled=True)  5.38 us
  transfers between devices with their start and end apart: 7, of which 3 were waited for; matrix products, arithmetic and copies ran while one was open for 1% of the time, Pallas kernels for 2%

profile of v3, /device:TPU:1, one launch (start us, length us, event | category | flops | bytes accessed | tf_op | source)
XLA Modules:
  0.0 115.9 jit_solution(12243856291245267197)
XLA Ops:
  0.6 0.0 copy-start.6
  0.6 0.6 copy-done.6
  1.3 0.0 copy-start.2
  1.3 0.8 copy-done.2
  2.1 0.0 copy-start.3
  2.1 0.8 copy-done.3
  2.9 0.0 copy-start.4
  2.9 0.8 copy-done.4
  3.7 1.7 %shard_map.110 = (bf16[128,384]{1,0:T(8,128)(2,1)S(1)}, bf16[8,32,384]{2,1,0:T(8,128)(2,1)S(1)}, bf16[32,384]{1,0:T(8,128)(2,1)S(1)}, bf16[4,64,384]{2,1,0:T(8,128)(2,1)}) custom-call(s32[3]{0:T(128)S(1)} %copy-done.6, bf16[3,64,128]{2,1,0:T(8,128)(2,1)S(1)} %bitcast.9, bf16[3,64,128]{2,1,0:T(8,128)(2,1)S(1)} %bitcast.10, bf16[64,384]{1,0:T(8,128)(2,1)S(1)} %copy-done.4), custom_call_target="tpu_custom_call" | custom-call | tf_op jit(solution)/shard_map/pallas_call | solution.py:283
  5.4 16.2 %all_to_all.35.line_in = bf16[8,32,384]{2,1,0:T(8,128)(2,1)S(1)} all-to-all(bf16[8,32,384]{2,1,0:T(8,128)(2,1)S(1)} %get-tuple-element.24), channel_id=1, replica_groups={{0,8,16,24,32,40,48,56},{4,12,20,28,36,44,52,60},{64,72,80,88,96,104,11..., dimensions={0} | all-to-all | bytes 393216 | tf_op jit(solution)/shard_map/all_to_all | solution.py:347
  21.6 0.0 copy-start
  21.6 11.7 %all_to_all.36.far_in = bf16[8,32,384]{2,1,0:T(8,128)(2,1)S(1)} all-to-all(bf16[8,32,384]{2,1,0:T(8,128)(2,1)S(1)} %shard_map.111), channel_id=1, replica_groups={{0,64,128,192,256,320,384,448},{4,68,132,196,260,324,388,452},{8,72,136..., dimensions={0} | all-to-all | bytes 393216 | tf_op jit(solution)/shard_map/all_to_all | solution.py:347
  33.2 0.0 copy-start.1
  33.2 0.0 copy-start.5
  33.2 9.2 %all-to-all-start = ((bf16[4,64,384]{2,1,0:T(8,128)(2,1)}), bf16[4,64,384]{2,1,0:T(8,128)(2,1)S(1)}, u32[]{:S(2)}, u32[]{:S(2)}) async-start(bf16[4,64,384]{2,1,0:T(8,128)(2,1)} %get-tuple-element.22), calls=%async_computation | async-start | bytes 393216 | tf_op jit(solution)/shard_map/all_to_all | solution.py:367
  42.5 6.2 %collective-permute-start.1 = (bf16[8,32,384]{2,1,0:T(8,128)(2,1)S(1)}, bf16[8,32,384]{2,1,0:T(8,128)(2,1)S(1)}, u32[]{:S(2)}, u32[]{:S(2)}) collective-permute-start(bf16[8,32,384]{2,1,0:T(8,128)(2,1)S(1)} %all_to_all.35.line_in), channel_id=1, source_target_pairs={{0,4},{4,0},{8,12},{12,8},{16,20},{20,16},{24,28},{28,24},{32,36},... | collective-permute-start | bytes 589832 | tf_op jit(solution)/shard_map/ppermute | solution.py:351
  48.7 1.9 %collective-permute-start.2 = (bf16[8,32,384]{2,1,0:T(8,128)(2,1)S(1)}, bf16[8,32,384]{2,1,0:T(8,128)(2,1)S(1)}, u32[]{:S(2)}, u32[]{:S(2)}) collective-permute-start(bf16[8,32,384]{2,1,0:T(8,128)(2,1)S(1)} %all_to_all.36.far_in), channel_id=1, source_target_pairs={{0,4},{4,0},{8,12},{12,8},{16,20},{20,16},{24,28},{28,24},{32,36},... | collective-permute-start | bytes 589832 | tf_op jit(solution)/shard_map/ppermute | solution.py:351
  50.6 2.4 %collective-permute-start = (bf16[32,384]{1,0:T(8,128)(2,1)S(1)}, bf16[32,384]{1,0:T(8,128)(2,1)S(1)}, u32[]{:S(2)}, u32[]{:S(2)}) collective-permute-start(bf16[32,384]{1,0:T(8,128)(2,1)S(1)} %get-tuple-element.25), channel_id=1, source_target_pairs={{0,4},{4,0},{8,12},{12,8},{16,20},{20,16},{24,28},{28,24},{32,36},... | collective-permute-start | bytes 73736 | tf_op jit(solution)/shard_map/ppermute | solution.py:351
  53.1 0.1 pad_add_fusion.rank
  53.1 0.7 collective-permute-done.partner_in
  53.9 0.0 all-to-all-done.grads
  53.9 0.0 collective-permute-done.1.other_in
  53.9 0.0 collective-permute-done.2.other_far_in
  53.9 0.0 copy-done
  53.9 0.0 copy-done.1
  53.9 0.0 copy-done.5
  53.9 6.0 %shard_map.112 = (bf16[4,64,384]{2,1,0:T(8,128)(2,1)}, bf16[3,64,128]{2,1,0:T(8,128)(2,1)}, bf16[576,384]{1,0:T(8,128)(2,1)S(1)}, f32[8,32,384]{2,1,0:T(8,128)S(...) custom-call(s32[3]{0:T(128)S(1)} %pad_add_fusion.rank, s32[3]{0:T(128)S(1)} %copy-done.6, ...), custom_call_target="tpu_custom_call" | custom-call | tf_op jit(solution)/shard_map/pallas_call | solution.py:283
  59.9 3.5 %collective-permute-start.3 = (bf16[576,384]{1,0:T(8,128)(2,1)S(1)}, bf16[576,384]{1,0:T(8,128)(2,1)S(1)}, u32[]{:S(2)}, u32[]{:S(2)}) collective-permute-start(bf16[576,384]{1,0:T(8,128)(2,1)S(1)} %get-tuple-element.26), channel_id=1, source_target_pairs={{0,4},{4,0},{8,12},{12,8},{16,20},{20,16},{24,28},{28,24},{32,36},... | collective-permute-start | bytes 1327112 | tf_op jit(solution)/shard_map/ppermute | solution.py:351
  63.5 5.6 %all-to-all-start.3 = ((bf16[4,64,384]{2,1,0:T(8,128)(2,1)}), bf16[4,64,384]{2,1,0:T(8,128)(2,1)S(1)}, u32[]{:S(2)}, u32[]{:S(2)}) async-start(bf16[4,64,384]{2,1,0:T(8,128)(2,1)} %get-tuple-element.29), calls=%async_computation.3 | async-start | bytes 393216 | tf_op jit(solution)/shard_map/all_to_all | solution.py:372
  69.1 0.0 collective-permute-done.3.received
  69.1 0.7 shard_map.113
  69.8 7.4 %all-to-all-done.3 = bf16[4,64,384]{2,1,0:T(8,128)(2,1)S(1)} async-done(((bf16[4,64,384]{2,1,0:T(8,128)(2,1)}), bf16[4,64,384]{2,1,0:T(8,128)(2,1)S(1)}, u32[]{:S(2)}, u32[]{:S(2)}) %all-to-all-start.3) | async-done | bytes 196640 | tf_op jit(solution)/shard_map/all_to_all | solution.py:372
  77.2 9.1 %all_to_all.37.far_in = bf16[8,56,384]{2,1,0:T(8,128)(2,1)S(1)} all-to-all(bf16[8,56,384]{2,1,0:T(8,128)(2,1)S(1)} %shard_map.113), channel_id=1, replica_groups={{0,64,128,192,256,320,384,448},{4,68,132,196,260,324,388,452},{8,72,136..., dimensions={0} | all-to-all | bytes 688128 | tf_op jit(solution)/shard_map/all_to_all | solution.py:347
  86.3 0.1 shard_map.114
  86.4 12.6 %all_to_all.38.line_in = bf16[8,56,384]{2,1,0:T(8,128)(2,1)S(1)} all-to-all(bf16[8,56,384]{2,1,0:T(8,128)(2,1)S(1)} %shard_map.114), channel_id=1, replica_groups={{0,8,16,24,32,40,48,56},{4,12,20,28,36,44,52,60},{64,72,80,88,96,104,11..., dimensions={0} | all-to-all | bytes 688128 | tf_op jit(solution)/shard_map/all_to_all | solution.py:347
  99.0 0.8 shard_map.115
  99.7 7.9 %all-to-all-start.6 = ((bf16[16,24,384]{2,1,0:T(8,128)(2,1)}), bf16[16,24,384]{2,1,0:T(8,128)(2,1)S(1)}, u32[]{:S(2)}, u32[]{:S(2)}) async-start(bf16[16,24,384]{2,1,0:T(8,128)(2,1)} %get-tuple-element.38), calls=%async_computation.6 | async-start | bytes 589824 | tf_op jit(solution)/shard_map/all_to_all | solution.py:347
  107.6 0.7 reduce_sum.12
  108.3 1.4 %shard_map.116 = (bf16[3,64,128]{2,1,0:T(8,128)(2,1)}, bf16[3,64,128]{2,1,0:T(8,128)(2,1)}) custom-call(s32[3]{0:T(128)S(1)} %copy-done.6, f32[128,384]{1,0:T(8,128)S(1)} %get-tuple-element.32.keep_own, bf16[576,384]{1,0:T(8,128)(2,1)S(1)} %collective-permute-done.3.received, f32[32,384]{1,0:T(8,128)S(1)} %get-tuple-element.35.near_sum), custom_call_target="tpu_custom_call" | custom-call | tf_op jit(solution)/shard_map/pallas_call | solution.py:283
  109.7 5.4 %all-to-all-done.6.spread_in = bf16[16,24,384]{2,1,0:T(8,128)(2,1)S(1)} async-done(((bf16[16,24,384]{2,1,0:T(8,128)(2,1)}), bf16[16,24,384]{2,1,0:T(8,128)(2,1)S(1)}, u32[]{:S(2)}, u32[]{:S(2)}) %all-to-all-start.6) | async-done | bytes 294944 | tf_op jit(solution)/shard_map/all_to_all | solution.py:347
  115.1 0.9 shard_map.117
  (1 shorter events, 0.0 us)
Async XLA Ops:
  0.6 0.7 copy-start.6
  1.3 0.8 copy-start.2
  2.1 0.8 copy-start.3
  2.9 0.8 copy-start.4
  21.6 32.3 %copy-start = (f32[832,128]{1,0:T(8,128)S(1)}, f32[832,128]{1,0:T(8,128)}, u32[]{:S(2)}) copy-start(f32[832,128]{1,0:T(8,128)} %constant.17.clone.bias) | copy-start | bytes 1277956
  33.2 20.7 %copy-start.1 = (bf16[192,768]{1,0:T(8,128)(2,1)S(1)}, bf16[192,768]{1,0:T(8,128)(2,1)}, u32[]{:S(2)}) copy-start(bf16[192,768]{1,0:T(8,128)(2,1)} %weight.1) | copy-start | bytes 884740
  33.2 20.7 %copy-start.5 = (bf16[64,3,128]{2,0,1:T(8,128)(2,1)S(1)}, bf16[64,3,128]{2,0,1:T(8,128)(2,1)}, u32[]{:S(2)}) copy-start(bf16[64,3,128]{2,0,1:T(8,128)(2,1)} %param.7) | copy-start | bytes 147460
  33.2 20.6 %all-to-all-start = ((bf16[4,64,384]{2,1,0:T(8,128)(2,1)}), bf16[4,64,384]{2,1,0:T(8,128)(2,1)S(1)}, u32[]{:S(2)}, u32[]{:S(2)}) async-start(bf16[4,64,384]{2,1,0:T(8,128)(2,1)} %get-tuple-element.22), calls=%async_computation | async-start | bytes 393216 | tf_op jit(solution)/shard_map/all_to_all | solution.py:367
  42.5 11.4 %collective-permute-start.1 = (bf16[8,32,384]{2,1,0:T(8,128)(2,1)S(1)}, bf16[8,32,384]{2,1,0:T(8,128)(2,1)S(1)}, u32[]{:S(2)}, u32[]{:S(2)}) collective-permute-start(bf16[8,32,384]{2,1,0:T(8,128)(2,1)S(1)} %all_to_all.35.line_in), channel_id=1, source_target_pairs={{0,4},{4,0},{8,12},{12,8},{16,20},{20,16},{24,28},{28,24},{32,36},... | collective-permute-start | bytes 589832 | tf_op jit(solution)/shard_map/ppermute | solution.py:351
  48.7 5.2 %collective-permute-start.2 = (bf16[8,32,384]{2,1,0:T(8,128)(2,1)S(1)}, bf16[8,32,384]{2,1,0:T(8,128)(2,1)S(1)}, u32[]{:S(2)}, u32[]{:S(2)}) collective-permute-start(bf16[8,32,384]{2,1,0:T(8,128)(2,1)S(1)} %all_to_all.36.far_in), channel_id=1, source_target_pairs={{0,4},{4,0},{8,12},{12,8},{16,20},{20,16},{24,28},{28,24},{32,36},... | collective-permute-start | bytes 589832 | tf_op jit(solution)/shard_map/ppermute | solution.py:351
  50.6 3.2 %collective-permute-start = (bf16[32,384]{1,0:T(8,128)(2,1)S(1)}, bf16[32,384]{1,0:T(8,128)(2,1)S(1)}, u32[]{:S(2)}, u32[]{:S(2)}) collective-permute-start(bf16[32,384]{1,0:T(8,128)(2,1)S(1)} %get-tuple-element.25), channel_id=1, source_target_pairs={{0,4},{4,0},{8,12},{12,8},{16,20},{20,16},{24,28},{28,24},{32,36},... | collective-permute-start | bytes 73736 | tf_op jit(solution)/shard_map/ppermute | solution.py:351
  59.9 9.2 %collective-permute-start.3 = (bf16[576,384]{1,0:T(8,128)(2,1)S(1)}, bf16[576,384]{1,0:T(8,128)(2,1)S(1)}, u32[]{:S(2)}, u32[]{:S(2)}) collective-permute-start(bf16[576,384]{1,0:T(8,128)(2,1)S(1)} %get-tuple-element.26), channel_id=1, source_target_pairs={{0,4},{4,0},{8,12},{12,8},{16,20},{20,16},{24,28},{28,24},{32,36},... | collective-permute-start | bytes 1327112 | tf_op jit(solution)/shard_map/ppermute | solution.py:351
  63.5 13.8 %all-to-all-start.3 = ((bf16[4,64,384]{2,1,0:T(8,128)(2,1)}), bf16[4,64,384]{2,1,0:T(8,128)(2,1)S(1)}, u32[]{:S(2)}, u32[]{:S(2)}) async-start(bf16[4,64,384]{2,1,0:T(8,128)(2,1)} %get-tuple-element.29), calls=%async_computation.3 | async-start | bytes 393216 | tf_op jit(solution)/shard_map/all_to_all | solution.py:372
  99.7 15.3 %all-to-all-start.6 = ((bf16[16,24,384]{2,1,0:T(8,128)(2,1)}), bf16[16,24,384]{2,1,0:T(8,128)(2,1)S(1)}, u32[]{:S(2)}, u32[]{:S(2)}) async-start(bf16[16,24,384]{2,1,0:T(8,128)(2,1)} %get-tuple-element.38), calls=%async_computation.6 | async-start | bytes 589824 | tf_op jit(solution)/shard_map/all_to_all | solution.py:347

commit v4 on v3

--- a/solution.py
+++ b/solution.py
@@ -107,7 +107,7 @@
     return jnp.concatenate([even, odd], axis=0).astype(BF16)
 
 
-def start_kernel(offsets, keys, values, grad, ordered, line_out, partner_out, grad_out, keys_here, values_here, grad_here, done):
+def start_kernel(offsets, keys, values, grad, ordered, line_out, grad_out, keys_here, values_here, grad_here, done):
     copies = [
         pltpu.make_async_copy(source, target, done.at[at])
         for at, (source, target) in enumerate(((keys, keys_here), (values, values_here), (grad, grad_here)))
@@ -123,7 +123,6 @@
         ordered[:, lanes] = dot(orders[head], both).astype(BF16)
     for slot in range(LINE):
         line_out[slot] = ordered[0:NEAR, :]
-    partner_out[...] = ordered[NEAR : 2 * NEAR, :]
     for slot in range(4):
         grad_out[slot] = grad_here[...]
 
@@ -142,7 +141,10 @@
     return one_hot(far_place(row, far) == lax.broadcasted_iota(jnp.int32, shape, 1 - row_axis))
 
 
-def far_kernel(line_in, far_out):
+def far_kernel(ordered, line_in, far_out, partner_out):
+    for slot in range(LINE):
+        partner_out[slot * NEAR : (slot + 1) * NEAR, :] = line_in[slot]
+    partner_out[SLOTS:, :] = ordered[NEAR : 2 * NEAR, :]
     low = lax.broadcasted_iota(jnp.int32, (8, LANES), 0) < EACH
     for pair in range(LINE // 2):
         first, second = (line_in[2 * pair + slot, 0:16, :].astype(F32)[:8] for slot in range(2))
@@ -152,13 +154,13 @@
 
 
 def main_kernel(
-    rank, offsets, queries, weight, grads, ordered, line_in, far_in, partner_in, other_in, other_far_in, bias,
-    output_part, query_grad, send, keep_line, keep_far, keep_own, keep_weight,
-    held, full_grad, attn, weight_term,
+    rank, offsets, queries, weight, grads, ordered, line_in, far_in, other_in, other_far_in, bias,
+    output_keep, output_send, query_grad, send, keep_line, keep_far, keep_own, keep_weight,
+    held, full_grad, attn, weight_term, parts,
 ):
     far, line, core = rank[0], rank[1], rank[2]
     held[0:ROWS, :] = ordered[...]
-    held[PARTNER_AT:OTHER_AT, :] = partner_in[...]
+    held[PARTNER_AT:OTHER_AT, :] = other_in[SLOTS:, :]
     choice = far_choice(far, 0)
     held[FAR_AT:PARTNER_AT, :] = dot(choice, far_in[...].reshape(FAR * NEAR, LANES)).astype(BF16)
     held[OTHER_FAR_AT:, :] = dot(choice, other_far_in[...].reshape(FAR * NEAR, LANES)).astype(BF16)
@@ -168,52 +170,58 @@
             at = LINE_AT + (step - 1) * NEAR
             held[at : at + NEAR, :] = line_in[slot]
         at = OTHER_AT + step * NEAR
-        held[at : at + NEAR, :] = other_in[slot]
+        held[at : at + NEAR, :] = other_in[pl.ds(pl.multiple_of(slot * NEAR, NEAR), NEAR), :]
     for parity in range(2):
         for half in range(2):
             full_grad[parity * SIZE : (parity + 1) * SIZE, half * HALF : (half + 1) * HALF] = grads[2 * parity + half]
-    for head in range(LOCAL):
-        lanes = pl.ds(head * 2 * SIZE, 2 * SIZE)
-        to_order = order_from(offsets[head], 0)
-        to_token = order_from(offsets[head], 1)
-        pairs = queries[head].astype(F32)
-        query = dot(to_order, beside(pairs, jnp.zeros_like(pairs))).astype(BF16)
-        head_weight = weight[head * SIZE : (head + 1) * SIZE, :]
-        grad = dot(full_grad[...], head_weight, NT).astype(BF16)
-        grad = dot(to_order, jnp.concatenate([jnp.zeros_like(grad), grad], axis=1)).astype(BF16)
-        beside_grad = jnp.concatenate([query, grad], axis=0)
-        both = held[:, lanes]
-        products = dot(both, beside_grad, NT)
-        scores = products[:, :ROWS] * SCALE + bias[...]
-        top = jnp.max(scores, axis=0, keepdims=True)
-        expd = jnp.exp(scores - top)
-        probs = expd / jnp.sum(expd, axis=0, keepdims=True)
-        rounded = probs.astype(BF16)
-        attn_head = dot(both, rounded, TN)[SIZE:, :].astype(BF16)
-        grad_side = grad.astype(F32).T
-        delta = jnp.sum(grad_side[SIZE:, :] * attn_head.astype(F32), axis=0, keepdims=True)
-        dscore = (probs * (products[:, ROWS:] - delta) * SCALE).astype(BF16)
-        dquery = dot(both, dscore, TN)[:SIZE, :].astype(BF16)
-        attn[:, head * SIZE : (head + 1) * SIZE] = dot(to_token, attn_head, NT).astype(BF16)
-        by_token = dot(to_token, jnp.concatenate([dquery, jnp.zeros_like(dquery)], axis=0), NT)
+    heads = range(LOCAL)
+    lanes = [pl.ds(head * 2 * SIZE, 2 * SIZE) for head in heads]
+    to_order = [order_from(offsets[head], 0) for head in heads]
+    to_token = [order_from(offsets[head], 1) for head in heads]
+    grad = dot(full_grad[...], weight[...], NT).astype(BF16)
+    pairs = [queries[head].astype(F32) for head in heads]
+    query = [dot(to_order[head], beside(pairs[head], jnp.zeros_like(pairs[head]))).astype(BF16) for head in heads]
+    zeros = jnp.zeros((ROWS, SIZE), BF16)
+    grad = [jnp.concatenate([zeros, grad[:, head * SIZE : (head + 1) * SIZE]], axis=1) for head in heads]
+    grad = [dot(to_order[head], grad[head]).astype(BF16) for head in heads]
+    blocks = [jnp.concatenate([query[head], grad[head]], axis=0) for head in heads]
+    products = [dot(held[:, lanes[head]], blocks[head], NT) for head in heads]
+    scores = [products[head][:, :ROWS] * SCALE + bias[...] for head in heads]
+    top = [jnp.max(scores[head], axis=0, keepdims=True) for head in heads]
+    expd = [jnp.exp(scores[head] - top[head]) for head in heads]
+    share = [1.0 / jnp.sum(expd[head], axis=0, keepdims=True) for head in heads]
+    probs = [expd[head] * share[head] for head in heads]
+    rounded = [probs[head].astype(BF16) for head in heads]
+    attn_head = [dot(held[:, lanes[head]], rounded[head], TN)[SIZE:, :].astype(BF16) for head in heads]
+    grad_side = [grad[head].astype(F32).T[SIZE:, :] for head in heads]
+    delta = [jnp.sum(grad_side[head] * attn_head[head].astype(F32), axis=0, keepdims=True) for head in heads]
+    dscore = [(probs[head] * (products[head][:, ROWS:] - delta[head]) * SCALE).astype(BF16) for head in heads]
+    dquery = [dot(held[:, lanes[head]], dscore[head], TN)[:SIZE, :].astype(BF16) for head in heads]
+    dboth = [dot(jnp.concatenate([dscore[head], rounded[head]], axis=1), blocks[head]) for head in heads]
+    for head in heads:
+        attn[:, head * SIZE : (head + 1) * SIZE] = dot(to_token[head], attn_head[head], NT).astype(BF16)
+        by_token = dot(to_token[head], jnp.concatenate([dquery[head], jnp.zeros_like(dquery[head])], axis=0), NT)
         query_grad[head] = (by_token[:SIZE] + pltpu.roll(by_token[SIZE:], SIZE, 1)).astype(BF16)
-        dboth = dot(jnp.concatenate([dscore, rounded], axis=1), beside_grad)
-        keep_own[:, lanes] = dboth[0:ROWS]
-        keep_far[:, lanes] = dboth[FAR_AT:PARTNER_AT]
-        send[SLOTS:SEND_FAR, lanes] = dboth[PARTNER_AT:OTHER_AT].astype(BF16)
-        send[SEND_FAR:SEND_WEIGHT, lanes] = dboth[OTHER_FAR_AT:].astype(BF16)
+        keep_own[:, lanes[head]] = dboth[head][0:ROWS]
+        keep_far[:, lanes[head]] = dboth[head][FAR_AT:PARTNER_AT]
+        send[SLOTS:SEND_FAR, lanes[head]] = dboth[head][PARTNER_AT:OTHER_AT].astype(BF16)
+        send[SEND_FAR:SEND_WEIGHT, lanes[head]] = dboth[head][OTHER_FAR_AT:].astype(BF16)
         for step in range(LINE):
             slot = line ^ step
             at = LINE_AT + (step - 1) * NEAR
-            keep_line[slot, :, lanes] = dboth[at : at + NEAR] if step else jnp.zeros((NEAR, 2 * SIZE), F32)
+            keep_line[slot, :, lanes[head]] = dboth[head][at : at + NEAR] if step else jnp.zeros((NEAR, 2 * SIZE), F32)
             at = OTHER_AT + step * NEAR
             rows = pl.ds(pl.multiple_of(slot * NEAR, NEAR), NEAR)
-            send[rows, lanes] = dboth[at : at + NEAR].astype(BF16)
+            send[rows, lanes[head]] = dboth[head][at : at + NEAR].astype(BF16)
     part = dot(attn[...], weight[...])
     for parity in range(2):
         for half in range(2):
             piece = part[parity * SIZE : (parity + 1) * SIZE, half * HALF : (half + 1) * HALF]
-            output_part[2 * parity + half] = piece.astype(BF16)
+            parts[2 * parity + half] = piece
+    mine = rank[3]
+    for step, way in ((0, 0), (1, 3)):
+        output_keep[step] = parts[mine ^ way]
+        output_send[step] = parts[mine ^ way ^ 1].astype(BF16)
     weight_term[...] = dot(attn[...], full_grad[...], TN)
     rows = SHARE // 2
     mine = pl.ds(pl.multiple_of(core * rows, 8), rows)
@@ -292,18 +300,20 @@
 
 
 def start(offsets, keys, values, grad):
-    outs = [((ROWS, LANES), BF16), ((LINE, NEAR, LANES), BF16), ((NEAR, LANES), BF16), ((4, SIZE, HALF), BF16)]
+    outs = [((ROWS, LANES), BF16), ((LINE, NEAR, LANES), BF16), ((4, SIZE, HALF), BF16)]
     scratch = [pltpu.VMEM((LOCAL, SIZE, 2 * SIZE), BF16)] * 2 + [pltpu.VMEM((SIZE, HALF), BF16), pltpu.SemaphoreType.DMA((3,))]
+    keys, values, grad = (pltpu.with_memory_space_constraint(array, pltpu.HBM) for array in (keys, values, grad))
     return call(start_kernel, outs, (offsets, keys, values, grad), 1, scratch, pltpu.HBM)
 
 
-def far_pieces(line_in):
-    return call(far_kernel, [((FAR, NEAR, LANES), BF16)], (line_in,), 0)[0]
+def far_pieces(ordered, line_in):
+    return call(far_kernel, [((FAR, NEAR, LANES), BF16), ((SLOTS + NEAR, LANES), BF16)], (ordered, line_in), 0)
 
 
 def attention(rank, offsets, *arrays):
     outs = [
-        ((4, SIZE, HALF), BF16),
+        ((2, SIZE, HALF), F32),
+        ((2, SIZE, HALF), BF16),
         ((LOCAL, SIZE, 2 * SIZE), BF16),
         ((SEND, LANES), BF16),
         ((LINE, NEAR, LANES), F32),
@@ -316,6 +326,7 @@
         pltpu.VMEM((ROWS, WIDTH), BF16),
         pltpu.VMEM((ROWS, LOCAL * SIZE), BF16),
         pltpu.VMEM((SHARE, WIDTH), F32),
+        pltpu.VMEM((4, SIZE, HALF), F32),
     ]
     return call(main_kernel, outs, (rank, offsets) + arrays + (jnp.asarray(shared_levels()),), 2, scratch)
 
@@ -351,29 +362,36 @@
     return lax.ppermute(block, "seq", [(i, i ^ 1) for i in range(FAR * LINE * CORE)])
 
 
+def swap_heads(block, way):
+    return lax.ppermute(block, "head", [(i, i ^ way) for i in range(4)])
+
+
 def shards(queries, keys, values, out_weight, offsets, out_grad):
     index = lax.axis_index("seq")
-    rank = jnp.stack([index >> 4, index >> 1 & 7, index & 1]).astype(jnp.int32)
+    rank = jnp.stack([index >> 4, index >> 1 & 7, index & 1, lax.axis_index("head")]).astype(jnp.int32)
     far_groups = [[far * 16 + low for far in range(FAR)] for low in range(16)]
     line_groups = [[far * 16 + line * 2 + core for line in range(LINE)] for far in range(FAR) for core in range(CORE)]
     side_groups = [[far * 16 + line * 2 + core for far in range(FAR) for core in range(CORE)] for line in range(LINE)]
     queries, keys, values = (array.transpose(1, 0, 2) for array in (queries, keys, values))
-    ordered, line_out, partner_out, grad_out = start(offsets, keys, values, out_grad)
-    partner_in = swap_cores(partner_out)
+    ordered, line_out, grad_out = start(offsets, keys, values, out_grad)
     line_in = trade(line_out, line_groups)
-    other_in = swap_cores(line_in)
-    far_in = trade(far_pieces(line_in), far_groups)
+    far_out, partner_out = far_pieces(ordered, line_in)
+    other_in = swap_cores(partner_out)
+    far_in = trade(far_out, far_groups)
     other_far_in = swap_cores(far_in)
     grads = lax.all_to_all(grad_out, "head", 0, 0, tiled=True)
-    output_part, query_grad, send, keep_line, keep_far, keep_own, keep_weight = attention(
-        rank, offsets, queries, out_weight, grads, ordered, line_in, far_in, partner_in, other_in, other_far_in
+    output_keep, output_send, query_grad, send, keep_line, keep_far, keep_own, keep_weight = attention(
+        rank, offsets, queries, out_weight, grads, ordered, line_in, far_in, other_in, other_far_in
     )
+    first = swap_heads(output_send, 1)
     received = swap_cores(send)
-    output_terms = lax.all_to_all(output_part, "head", 0, 0, tiled=True)
-    far_out = far_return(rank, received, keep_far, keep_weight)
-    far_out, output_terms = lax.optimization_barrier((far_out, output_terms))
-    output = jnp.sum(output_terms.astype(F32), axis=0).astype(BF16)
-    line_back = trade(line_return(received, keep_line, trade(far_out, far_groups)), line_groups)
+    far_back = trade(far_return(rank, received, keep_far, keep_weight), far_groups)
+    far_back, first = lax.optimization_barrier((far_back, first))
+    output_sum = output_keep + first.astype(F32)
+    second = swap_heads(output_sum[1].astype(BF16), 3)
+    line_back = trade(line_return(received, keep_line, far_back), line_groups)
+    line_back, second = lax.optimization_barrier((line_back, second))
+    output = (output_sum[0] + second.astype(F32)).astype(BF16)
     near_sum, spread_out = spread_pieces(line_back)
     weight_grad = weight_rows(trade(spread_out, side_groups))
     key_grad, value_grad = finish(offsets, keep_own, received, near_sum)

time: 117 us -> 107 us (0.915)
  blocking collectives: 49.5 us -> 27.8 us
  starting transfers between devices: 36.8 us -> 46.3 us
  waiting for transfers between devices: 13.5 us -> 19 us
  local copies, waits for them, and re-layouts: 3.06 us -> 0.67 us
    all_to_all x4 -> x2, blocking collectives: 49.5 us -> 27.8 us  [trade(): lax.all_to_all(pieces, 'seq', 0, 0, axis_index_groups=groups, tiled=True)]
    all_to_all x1 -> x3, starting transfers between devices: 7.87 us -> 16.4 us  [trade(): lax.all_to_all(pieces, 'seq', 0, 0, axis_index_groups=groups, tiled=True)]
    all_to_all x1 -> x0, waiting for transfers between devices: 7.38 us -> none  [shards(): output_terms = lax.all_to_all(output_part, 'head', 0, 0, tiled=True)]
    ppermute x0 -> x2, starting transfers between devices: none -> 7.06 us  [swap_heads(): return lax.ppermute(block, 'head', [(i, i ^ way) for i in range(4)])]
    ppermute x0 -> x2, waiting for transfers between devices: none -> 6.86 us  [swap_heads(): return lax.ppermute(block, 'head', [(i, i ^ way) for i in range(4)])]
    all_to_all x1 -> x0, starting transfers between devices: 5.65 us -> none  [shards(): output_terms = lax.all_to_all(output_part, 'head', 0, 0, tiled=True)]
    all_to_all x1 -> x3, waiting for transfers between devices: 5.38 us -> 9.42 us  [trade(): lax.all_to_all(pieces, 'seq', 0, 0, axis_index_groups=groups, tiled=True)]
    unnamed x14 -> x8, local copies, waits for them, and re-layouts: 3.06 us -> 0.66 us
  transfers between devices with their start and end apart: 7 -> 9, of which waited for: 3 -> 7; matrix products, arithmetic and copies ran while one was open for 1% -> 1% of each run, Pallas kernels for 2% -> 1%
where the time goes in v4:
time: 107 us
  starting transfers between devices  46.3 us (43%)
  blocking collectives  27.8 us (26%)
  waiting for transfers between devices  19 us (18%)
  Pallas kernels  11.3 us (11%)
    all_to_all x2, blocking collectives, trade(): lax.all_to_all(pieces, 'seq', 0, 0, axis_index_groups=groups, tiled=True)  27.8 us
    all_to_all x3, starting transfers between devices, trade(): lax.all_to_all(pieces, 'seq', 0, 0, axis_index_groups=groups, tiled=True)  16.4 us
    ppermute x3, starting transfers between devices, swap_cores(): lax.ppermute(block, 'seq', [(i, i ^ 1) for i in range(FAR * LINE * CORE)])  13.5 us
    pallas_call x8, Pallas kernels, call(): pl.pallas_call(kernel, out_shape=[jax.ShapeDtypeStruct(shape, dtype) for...  11.3 us
    all_to_all x3, waiting for transfers between devices, trade(): lax.all_to_all(pieces, 'seq', 0, 0, axis_index_groups=groups, tiled=True)  9.42 us
    all_to_all x1, starting transfers between devices, shards(): grads = lax.all_to_all(grad_out, 'head', 0, 0, tiled=True)  9.26 us
    ppermute x2, starting transfers between devices, swap_heads(): return lax.ppermute(block, 'head', [(i, i ^ way) for i in range(4)])  7.06 us
    ppermute x2, waiting for transfers between devices, swap_heads(): return lax.ppermute(block, 'head', [(i, i ^ way) for i in range(4)])  6.86 us
  transfers between devices with their start and end apart: 9, of which 7 were waited for; matrix products, arithmetic and copies ran while one was open for 1% of the time, Pallas kernels for 1%

profile of v4, /device:TPU:1, one launch (start us, length us, event | category | flops | bytes accessed | tf_op | source)
XLA Modules:
  0.0 106.6 jit_solution(6161247329771413638)
XLA Ops:
  0.6 0.0 copy-start.3
  0.6 0.6 copy-done.3
  1.3 2.2 %shard_map.110 = (bf16[128,384]{1,0:T(8,128)(2,1)S(1)}, bf16[8,32,384]{2,1,0:T(8,128)(2,1)S(1)}, bf16[4,64,384]{2,1,0:T(8,128)(2,1)}) custom-call(s32[3]{0:T(128)S(1)} %copy-done.3, bf16[3,64,128]{2,1,0:T(8,128)(2,1)} %bitcast.19, bf16[3,64,128]{2,1,0:T(8,128)(2,1)} %bitcast.20, bf16[64,384]{1,0:T(8,128)(2,1)} %grad.1), custom_call_target="tpu_custom_call" | custom-call | tf_op jit(solution)/shard_map/pallas_call | solution.py:291
  3.5 16.2 %all_to_all.30.line_in = bf16[8,32,384]{2,1,0:T(8,128)(2,1)S(1)} all-to-all(bf16[8,32,384]{2,1,0:T(8,128)(2,1)S(1)} %get-tuple-element.28), channel_id=1, replica_groups={{0,8,16,24,32,40,48,56},{4,12,20,28,36,44,52,60},{64,72,80,88,96,104,11..., dimensions={0} | all-to-all | bytes 393216 | tf_op jit(solution)/shard_map/all_to_all | solution.py:358
  19.7 0.0 copy-start
  19.7 11.6 %all_to_all.31.far_in = bf16[8,32,384]{2,1,0:T(8,128)(2,1)S(1)} all-to-all(bf16[8,32,384]{2,1,0:T(8,128)(2,1)S(1)} %get-tuple-element.29), channel_id=1, replica_groups={{0,64,128,192,256,320,384,448},{4,68,132,196,260,324,388,452},{8,72,136..., dimensions={0} | all-to-all | bytes 393216 | tf_op jit(solution)/shard_map/all_to_all | solution.py:358
  31.4 0.0 copy-start.1
  31.4 0.0 copy-start.2
  31.4 9.3 %all-to-all-start = ((bf16[4,64,384]{2,1,0:T(8,128)(2,1)}), bf16[4,64,384]{2,1,0:T(8,128)(2,1)S(1)}, u32[]{:S(2)}, u32[]{:S(2)}) async-start(bf16[4,64,384]{2,1,0:T(8,128)(2,1)} %get-tuple-element.26), calls=%async_computation | async-start | bytes 393216 | tf_op jit(solution)/shard_map/all_to_all | solution.py:382
  40.7 6.2 %collective-permute-start = (bf16[288,384]{1,0:T(8,128)(2,1)S(1)}, bf16[288,384]{1,0:T(8,128)(2,1)S(1)}, u32[]{:S(2)}, u32[]{:S(2)}) collective-permute-start(bf16[288,384]{1,0:T(8,128)(2,1)S(1)} %get-tuple-element.30), channel_id=1, source_target_pairs={{0,4},{4,0},{8,12},{12,8},{16,20},{20,16},{24,28},{28,24},{32,36},... | collective-permute-start | bytes 663560 | tf_op jit(solution)/shard_map/ppermute | solution.py:362
  46.9 1.9 %collective-permute-start.1 = (bf16[8,32,384]{2,1,0:T(8,128)(2,1)S(1)}, bf16[8,32,384]{2,1,0:T(8,128)(2,1)S(1)}, u32[]{:S(2)}, u32[]{:S(2)}) collective-permute-start(bf16[8,32,384]{2,1,0:T(8,128)(2,1)S(1)} %all_to_all.31.far_in), channel_id=1, source_target_pairs={{0,4},{4,0},{8,12},{12,8},{16,20},{20,16},{24,28},{28,24},{32,36},... | collective-permute-start | bytes 589832 | tf_op jit(solution)/shard_map/ppermute | solution.py:362
  48.8 0.1 pad_add_fusion.rank
  48.9 0.0 all-to-all-done.grads
  48.9 0.0 collective-permute-done.other_in
  48.9 1.3 %collective-permute-done.1.other_far_in = bf16[8,32,384]{2,1,0:T(8,128)(2,1)S(1)} collective-permute-done((bf16[8,32,384]{2,1,0:T(8,128)(2,1)S(1)}, bf16[8,32,384]{2,1,0:T(8,128)(2,1)S(1)}, u32[]{:S(2)}, u32[]{:S(2)}) %collective-permute-start.1) | collective-permute-done | bytes 196640 | tf_op jit(solution)/shard_map/ppermute | solution.py:362
  50.2 0.0 copy-done
  50.2 0.0 copy-done.1
  50.2 0.0 copy-done.2
  50.2 3.7 %shard_map.112 = (f32[2,64,384]{2,1,0:T(8,128)S(1)}, bf16[2,64,384]{2,1,0:T(8,128)(2,1)S(1)}, bf16[3,64,128]{2,1,0:T(8,128)(2,1)}, bf16[576,384]{1,0:T(8,128)(2,...) custom-call(s32[4]{0:T(128)S(1)} %pad_add_fusion.rank, ...), custom_call_target="tpu_custom_call" | custom-call | tf_op jit(solution)/shard_map/pallas_call | solution.py:291
  54.0 5.4 %collective-permute-start.2 = (bf16[576,384]{1,0:T(8,128)(2,1)S(1)}, bf16[576,384]{1,0:T(8,128)(2,1)S(1)}, u32[]{:S(2)}, u32[]{:S(2)}) collective-permute-start(bf16[576,384]{1,0:T(8,128)(2,1)S(1)} %get-tuple-element.32), channel_id=1, source_target_pairs={{0,4},{4,0},{8,12},{12,8},{16,20},{20,16},{24,28},{28,24},{32,36},... | collective-permute-start | bytes 1327112 | tf_op jit(solution)/shard_map/ppermute | solution.py:362
  59.4 1.4 %collective-permute-done.2.received = bf16[576,384]{1,0:T(8,128)(2,1)S(1)} collective-permute-done((bf16[576,384]{1,0:T(8,128)(2,1)S(1)}, bf16[576,384]{1,0:T(8,128)(2,1)S(1)}, u32[]{:S(2)}, u32[]{:S(2)}) %collective-permute-start.2) | collective-permute-done | bytes 442400 | tf_op jit(solution)/shard_map/ppermute | solution.py:362
  60.8 1.5 %shard_map.113 = bf16[8,56,384]{2,1,0:T(8,128)(2,1)} custom-call(s32[4]{0:T(128)S(1)} %pad_add_fusion.rank, bf16[576,384]{1,0:T(8,128)(2,1)S(1)} %collective-permute-done.2.received, f32[96,384]{1,0:T(8,128)S(1)} %get-tuple-element.33.keep_far, f32[192,384]{1,0:T(8,128)S(1)} %get-tuple-element.34.keep_weight), custom_call_target="tpu_custom_call" | custom-call | tf_op jit(solution)/shard_map/pallas_call | solution.py:291
  62.3 3.4 %all-to-all-start.3 = ((bf16[8,56,384]{2,1,0:T(8,128)(2,1)}), bf16[8,56,384]{2,1,0:T(8,128)(2,1)S(1)}, u32[]{:S(2)}, u32[]{:S(2)}) async-start(bf16[8,56,384]{2,1,0:T(8,128)(2,1)} %shard_map.113), calls=%async_computation.3 | async-start | bytes 688128 | tf_op jit(solution)/shard_map/all_to_all | solution.py:358
  65.7 3.2 %collective-permute-start.3 = (bf16[2,64,384]{2,1,0:T(8,128)(2,1)S(1)}, bf16[2,64,384]{2,1,0:T(8,128)(2,1)S(1)}, u32[]{:S(2)}, u32[]{:S(2)}) collective-permute-start(bf16[2,64,384]{2,1,0:T(8,128)(2,1)S(1)} %get-tuple-element.35), channel_id=1, source_target_pairs={{0,1},{1,0},{2,3},{3,2},{4,5},{5,4},{6,7},{7,6},{8,9},{9,8},{10,11... | collective-permute-start | bytes 294920 | tf_op jit(solution)/shard_map/ppermute | solution.py:366
  69.0 3.7 %collective-permute-done.3 = bf16[2,64,384]{2,1,0:T(8,128)(2,1)S(1)} collective-permute-done((bf16[2,64,384]{2,1,0:T(8,128)(2,1)S(1)}, bf16[2,64,384]{2,1,0:T(8,128)(2,1)S(1)}, u32[]{:S(2)}, u32[]{:S(2)}) %collective-permute-start.3) | collective-permute-done | bytes 98336 | tf_op jit(solution)/shard_map/ppermute | solution.py:366
  72.7 0.9 all-to-all-done.3.far_in
  73.6 0.8 shard_map.114
  74.4 3.4 %all-to-all-start.4 = ((bf16[8,56,384]{2,1,0:T(8,128)(2,1)}), bf16[8,56,384]{2,1,0:T(8,128)(2,1)S(1)}, u32[]{:S(2)}, u32[]{:S(2)}) async-start(bf16[8,56,384]{2,1,0:T(8,128)(2,1)} %shard_map.114), calls=%async_computation.4 | async-start | bytes 688128 | tf_op jit(solution)/shard_map/all_to_all | solution.py:358
  77.9 3.8 %collective-permute-start.4 = (bf16[64,384]{1,0:T(8,128)(2,1)S(1)}, bf16[64,384]{1,0:T(8,128)(2,1)S(1)}, u32[]{:S(2)}, u32[]{:S(2)}) collective-permute-start(bf16[64,384]{1,0:T(8,128)(2,1)S(1)} %fusion.2), channel_id=1, source_target_pairs={{0,3},{1,2},{2,1},{3,0},{4,7},{5,6},{6,5},{7,4},{8,11},{9,10},{10,... | collective-permute-start | bytes 147464 | tf_op jit(solution)/shard_map/ppermute | solution.py:366
  81.7 3.2 %collective-permute-done.4 = bf16[64,384]{1,0:T(8,128)(2,1)S(1)} collective-permute-done((bf16[64,384]{1,0:T(8,128)(2,1)S(1)}, bf16[64,384]{1,0:T(8,128)(2,1)S(1)}, u32[]{:S(2)}, u32[]{:S(2)}) %collective-permute-start.4) | collective-permute-done | bytes 49184 | tf_op jit(solution)/shard_map/ppermute | solution.py:366
  84.9 3.2 %all-to-all-done.4.line_in = bf16[8,56,384]{2,1,0:T(8,128)(2,1)S(1)} async-done(((bf16[8,56,384]{2,1,0:T(8,128)(2,1)}), bf16[8,56,384]{2,1,0:T(8,128)(2,1)S(1)}, u32[]{:S(2)}, u32[]{:S(2)}) %all-to-all-start.4) | async-done | bytes 344096 | tf_op jit(solution)/shard_map/all_to_all | solution.py:358
  88.0 0.8 shard_map.115
  88.8 9.6 %all-to-all-start.5 = ((bf16[16,24,384]{2,1,0:T(8,128)(2,1)}), bf16[16,24,384]{2,1,0:T(8,128)(2,1)S(1)}, u32[]{:S(2)}, u32[]{:S(2)}) async-start(bf16[16,24,384]{2,1,0:T(8,128)(2,1)} %get-tuple-element.46), calls=%async_computation.5 | async-start | bytes 589824 | tf_op jit(solution)/shard_map/all_to_all | solution.py:358
  98.4 1.4 %shard_map.116 = (bf16[3,64,128]{2,1,0:T(8,128)(2,1)}, bf16[3,64,128]{2,1,0:T(8,128)(2,1)}) custom-call(s32[3]{0:T(128)S(1)} %copy-done.3, f32[128,384]{1,0:T(8,128)S(1)} %get-tuple-element.41.keep_own, bf16[576,384]{1,0:T(8,128)(2,1)S(1)} %collective-permute-done.2.received, f32[32,384]{1,0:T(8,128)S(1)} %get-tuple-element.43.near_sum), custom_call_target="tpu_custom_call" | custom-call | tf_op jit(solution)/shard_map/pallas_call | solution.py:291
  99.8 0.6 fusion.1
  100.4 5.3 %all-to-all-done.5.spread_in = bf16[16,24,384]{2,1,0:T(8,128)(2,1)S(1)} async-done(((bf16[16,24,384]{2,1,0:T(8,128)(2,1)}), bf16[16,24,384]{2,1,0:T(8,128)(2,1)S(1)}, u32[]{:S(2)}, u32[]{:S(2)}) %all-to-all-start.5) | async-done | bytes 294944 | tf_op jit(solution)/shard_map/all_to_all | solution.py:358
  105.7 0.9 shard_map.117
  (3 shorter events, 0.1 us)
Async XLA Ops:
  0.6 0.7 copy-start.3
  19.7 30.5 %copy-start = (f32[832,128]{1,0:T(8,128)S(1)}, f32[832,128]{1,0:T(8,128)}, u32[]{:S(2)}) copy-start(f32[832,128]{1,0:T(8,128)} %constant.17.clone.bias) | copy-start | bytes 1277956
  31.4 18.8 %copy-start.1 = (bf16[192,768]{1,0:T(8,128)(2,1)S(1)}, bf16[192,768]{1,0:T(8,128)(2,1)}, u32[]{:S(2)}) copy-start(bf16[192,768]{1,0:T(8,128)(2,1)} %weight.1) | copy-start | bytes 884740
  31.4 18.8 %copy-start.2 = (bf16[64,3,128]{2,0,1:T(8,128)(2,1)S(1)}, bf16[64,3,128]{2,0,1:T(8,128)(2,1)}, u32[]{:S(2)}) copy-start(bf16[64,3,128]{2,0,1:T(8,128)(2,1)} %param.7) | copy-start | bytes 147460
  31.4 17.5 %all-to-all-start = ((bf16[4,64,384]{2,1,0:T(8,128)(2,1)}), bf16[4,64,384]{2,1,0:T(8,128)(2,1)S(1)}, u32[]{:S(2)}, u32[]{:S(2)}) async-start(bf16[4,64,384]{2,1,0:T(8,128)(2,1)} %get-tuple-element.26), calls=%async_computation | async-start | bytes 393216 | tf_op jit(solution)/shard_map/all_to_all | solution.py:382
  40.7 8.2 %collective-permute-start = (bf16[288,384]{1,0:T(8,128)(2,1)S(1)}, bf16[288,384]{1,0:T(8,128)(2,1)S(1)}, u32[]{:S(2)}, u32[]{:S(2)}) collective-permute-start(bf16[288,384]{1,0:T(8,128)(2,1)S(1)} %get-tuple-element.30), channel_id=1, source_target_pairs={{0,4},{4,0},{8,12},{12,8},{16,20},{20,16},{24,28},{28,24},{32,36},... | collective-permute-start | bytes 663560 | tf_op jit(solution)/shard_map/ppermute | solution.py:362
  46.9 3.3 %collective-permute-start.1 = (bf16[8,32,384]{2,1,0:T(8,128)(2,1)S(1)}, bf16[8,32,384]{2,1,0:T(8,128)(2,1)S(1)}, u32[]{:S(2)}, u32[]{:S(2)}) collective-permute-start(bf16[8,32,384]{2,1,0:T(8,128)(2,1)S(1)} %all_to_all.31.far_in), channel_id=1, source_target_pairs={{0,4},{4,0},{8,12},{12,8},{16,20},{20,16},{24,28},{28,24},{32,36},... | collective-permute-start | bytes 589832 | tf_op jit(solution)/shard_map/ppermute | solution.py:362
  54.0 6.8 %collective-permute-start.2 = (bf16[576,384]{1,0:T(8,128)(2,1)S(1)}, bf16[576,384]{1,0:T(8,128)(2,1)S(1)}, u32[]{:S(2)}, u32[]{:S(2)}) collective-permute-start(bf16[576,384]{1,0:T(8,128)(2,1)S(1)} %get-tuple-element.32), channel_id=1, source_target_pairs={{0,4},{4,0},{8,12},{12,8},{16,20},{20,16},{24,28},{28,24},{32,36},... | collective-permute-start | bytes 1327112 | tf_op jit(solution)/shard_map/ppermute | solution.py:362
  62.3 11.3 %all-to-all-start.3 = ((bf16[8,56,384]{2,1,0:T(8,128)(2,1)}), bf16[8,56,384]{2,1,0:T(8,128)(2,1)S(1)}, u32[]{:S(2)}, u32[]{:S(2)}) async-start(bf16[8,56,384]{2,1,0:T(8,128)(2,1)} %shard_map.113), calls=%async_computation.3 | async-start | bytes 688128 | tf_op jit(solution)/shard_map/all_to_all | solution.py:358
  65.7 6.9 %collective-permute-start.3 = (bf16[2,64,384]{2,1,0:T(8,128)(2,1)S(1)}, bf16[2,64,384]{2,1,0:T(8,128)(2,1)S(1)}, u32[]{:S(2)}, u32[]{:S(2)}) collective-permute-start(bf16[2,64,384]{2,1,0:T(8,128)(2,1)S(1)} %get-tuple-element.35), channel_id=1, source_target_pairs={{0,1},{1,0},{2,3},{3,2},{4,5},{5,4},{6,7},{7,6},{8,9},{9,8},{10,11... | collective-permute-start | bytes 294920 | tf_op jit(solution)/shard_map/ppermute | solution.py:366
  74.4 13.7 %all-to-all-start.4 = ((bf16[8,56,384]{2,1,0:T(8,128)(2,1)}), bf16[8,56,384]{2,1,0:T(8,128)(2,1)S(1)}, u32[]{:S(2)}, u32[]{:S(2)}) async-start(bf16[8,56,384]{2,1,0:T(8,128)(2,1)} %shard_map.114), calls=%async_computation.4 | async-start | bytes 688128 | tf_op jit(solution)/shard_map/all_to_all | solution.py:358
  77.9 7.0 %collective-permute-start.4 = (bf16[64,384]{1,0:T(8,128)(2,1)S(1)}, bf16[64,384]{1,0:T(8,128)(2,1)S(1)}, u32[]{:S(2)}, u32[]{:S(2)}) collective-permute-start(bf16[64,384]{1,0:T(8,128)(2,1)S(1)} %fusion.2), channel_id=1, source_target_pairs={{0,3},{1,2},{2,1},{3,0},{4,7},{5,6},{6,5},{7,4},{8,11},{9,10},{10,... | collective-permute-start | bytes 147464 | tf_op jit(solution)/shard_map/ppermute | solution.py:366
  88.8 17.0 %all-to-all-start.5 = ((bf16[16,24,384]{2,1,0:T(8,128)(2,1)}), bf16[16,24,384]{2,1,0:T(8,128)(2,1)S(1)}, u32[]{:S(2)}, u32[]{:S(2)}) async-start(bf16[16,24,384]{2,1,0:T(8,128)(2,1)} %get-tuple-element.46), calls=%async_computation.5 | async-start | bytes 589824 | tf_op jit(solution)/shard_map/all_to_all | solution.py:358

commit v5 on v4

--- a/solution.py
+++ b/solution.py
@@ -107,10 +107,10 @@
     return jnp.concatenate([even, odd], axis=0).astype(BF16)
 
 
-def start_kernel(offsets, keys, values, grad, ordered, line_out, grad_out, keys_here, values_here, grad_here, done):
+def start_kernel(offsets, keys, values, ordered, line_out, keys_here, values_here, done):
     copies = [
         pltpu.make_async_copy(source, target, done.at[at])
-        for at, (source, target) in enumerate(((keys, keys_here), (values, values_here), (grad, grad_here)))
+        for at, (source, target) in enumerate(((keys, keys_here), (values, values_here)))
     ]
     for copy in copies:
         copy.start()
@@ -123,8 +123,6 @@
         ordered[:, lanes] = dot(orders[head], both).astype(BF16)
     for slot in range(LINE):
         line_out[slot] = ordered[0:NEAR, :]
-    for slot in range(4):
-        grad_out[slot] = grad_here[...]
 
 
 def far_place(row, far):
@@ -141,7 +139,20 @@
     return one_hot(far_place(row, far) == lax.broadcasted_iota(jnp.int32, shape, 1 - row_axis))
 
 
-def far_kernel(ordered, line_in, far_out, partner_out):
+def table_kernel(rank, offsets, queries, to_order, to_token, query, choice, choice_back):
+    for head in range(LOCAL):
+        order = order_from(offsets[head], 0)
+        pairs = queries[head].astype(F32)
+        to_order[head] = order
+        to_token[head] = order_from(offsets[head], 1)
+        query[head] = dot(order, beside(pairs, jnp.zeros_like(pairs))).astype(BF16)
+    choice[...] = far_choice(rank[0], 0)
+    choice_back[...] = far_choice(rank[0], 1)
+
+
+def far_kernel(ordered, line_in, grad, grad_in, far_out, partner_out, grads_out):
+    grads_out[0] = grad[...]
+    grads_out[1] = grad_in[...]
     for slot in range(LINE):
         partner_out[slot * NEAR : (slot + 1) * NEAR, :] = line_in[slot]
     partner_out[SLOTS:, :] = ordered[NEAR : 2 * NEAR, :]
@@ -154,16 +165,15 @@
 
 
 def main_kernel(
-    rank, offsets, queries, weight, grads, ordered, line_in, far_in, other_in, other_far_in, bias,
+    rank, to_order, to_token, query, choice, weight, grads, other_grads, ordered, line_in, far_in, other_in, other_far_in, bias,
     output_keep, output_send, query_grad, send, keep_line, keep_far, keep_own, keep_weight,
-    held, full_grad, attn, weight_term, parts,
+    held, full_grad, attn, weight_term, parts, grad_parts,
 ):
-    far, line, core = rank[0], rank[1], rank[2]
+    line, core, mine = rank[1], rank[2], rank[3]
     held[0:ROWS, :] = ordered[...]
     held[PARTNER_AT:OTHER_AT, :] = other_in[SLOTS:, :]
-    choice = far_choice(far, 0)
-    held[FAR_AT:PARTNER_AT, :] = dot(choice, far_in[...].reshape(FAR * NEAR, LANES)).astype(BF16)
-    held[OTHER_FAR_AT:, :] = dot(choice, other_far_in[...].reshape(FAR * NEAR, LANES)).astype(BF16)
+    held[FAR_AT:PARTNER_AT, :] = dot(choice[...], far_in[...].reshape(FAR * NEAR, LANES)).astype(BF16)
+    held[OTHER_FAR_AT:, :] = dot(choice[...], other_far_in[...].reshape(FAR * NEAR, LANES)).astype(BF16)
     for step in range(LINE):
         slot = line ^ step
         if step:
@@ -171,16 +181,15 @@
             held[at : at + NEAR, :] = line_in[slot]
         at = OTHER_AT + step * NEAR
         held[at : at + NEAR, :] = other_in[pl.ds(pl.multiple_of(slot * NEAR, NEAR), NEAR), :]
+    for way, piece in enumerate((grads[0], grads[1], other_grads[1], other_grads[0])):
+        grad_parts[mine ^ way] = piece
     for parity in range(2):
         for half in range(2):
-            full_grad[parity * SIZE : (parity + 1) * SIZE, half * HALF : (half + 1) * HALF] = grads[2 * parity + half]
+            place = (slice(parity * SIZE, (parity + 1) * SIZE), slice(half * HALF, (half + 1) * HALF))
+            full_grad[place] = grad_parts[2 * parity + half]
     heads = range(LOCAL)
     lanes = [pl.ds(head * 2 * SIZE, 2 * SIZE) for head in heads]
-    to_order = [order_from(offsets[head], 0) for head in heads]
-    to_token = [order_from(offsets[head], 1) for head in heads]
     grad = dot(full_grad[...], weight[...], NT).astype(BF16)
-    pairs = [queries[head].astype(F32) for head in heads]
-    query = [dot(to_order[head], beside(pairs[head], jnp.zeros_like(pairs[head]))).astype(BF16) for head in heads]
     zeros = jnp.zeros((ROWS, SIZE), BF16)
     grad = [jnp.concatenate([zeros, grad[:, head * SIZE : (head + 1) * SIZE]], axis=1) for head in heads]
     grad = [dot(to_order[head], grad[head]).astype(BF16) for head in heads]
@@ -218,7 +227,6 @@
         for half in range(2):
             piece = part[parity * SIZE : (parity + 1) * SIZE, half * HALF : (half + 1) * HALF]
             parts[2 * parity + half] = piece
-    mine = rank[3]
     for step, way in ((0, 0), (1, 3)):
         output_keep[step] = parts[mine ^ way]
         output_send[step] = parts[mine ^ way ^ 1].astype(BF16)
@@ -233,9 +241,9 @@
         send[at : at + rows, :] = weight_term[theirs, columns].astype(BF16)
 
 
-def far_return_kernel(rank, received, keep_far, keep_weight, far_out):
+def far_return_kernel(choice_back, received, keep_far, keep_weight, far_out):
     picked = (keep_far[...] + received[SEND_FAR:SEND_WEIGHT, :].astype(F32)).astype(BF16)
-    rows = dot(far_choice(rank[0], 1), picked).astype(BF16)
+    rows = dot(choice_back[...], picked).astype(BF16)
     weight = (keep_weight[...] + received[SEND_WEIGHT:, :].astype(F32)).astype(BF16)
     for slot in range(FAR):
         far_out[slot, 0:NEAR, :] = rows[slot * NEAR : (slot + 1) * NEAR]
@@ -265,14 +273,13 @@
         spread_out[slot] = part
 
 
-def finish_kernel(offsets, keep_own, received, near_sum, key_grad, value_grad, own):
+def finish_kernel(to_token, keep_own, received, near_sum, key_grad, value_grad, own):
     own[...] = keep_own[...]
     own[NEAR : 2 * NEAR, :] += received[SLOTS:SEND_FAR, :].astype(F32)
     own[0:NEAR, :] += near_sum[...]
     for head in range(LOCAL):
-        to_token = order_from(offsets[head], 1)
         both = own[:, head * 2 * SIZE : (head + 1) * 2 * SIZE].astype(BF16)
-        both = dot(to_token, both)
+        both = dot(to_token[head], both)
         even, odd = both[:SIZE], both[SIZE:]
         low = lane_iota(even.shape) < SIZE
         key_grad[head] = jnp.where(low, even, pltpu.roll(odd, SIZE, 1)).astype(BF16)
@@ -299,18 +306,25 @@
     )(*args)
 
 
-def start(offsets, keys, values, grad):
-    outs = [((ROWS, LANES), BF16), ((LINE, NEAR, LANES), BF16), ((4, SIZE, HALF), BF16)]
-    scratch = [pltpu.VMEM((LOCAL, SIZE, 2 * SIZE), BF16)] * 2 + [pltpu.VMEM((SIZE, HALF), BF16), pltpu.SemaphoreType.DMA((3,))]
-    keys, values, grad = (pltpu.with_memory_space_constraint(array, pltpu.HBM) for array in (keys, values, grad))
-    return call(start_kernel, outs, (offsets, keys, values, grad), 1, scratch, pltpu.HBM)
-
-
-def far_pieces(ordered, line_in):
-    return call(far_kernel, [((FAR, NEAR, LANES), BF16), ((SLOTS + NEAR, LANES), BF16)], (ordered, line_in), 0)
-
-
-def attention(rank, offsets, *arrays):
+def start(offsets, keys, values):
+    outs = [((ROWS, LANES), BF16), ((LINE, NEAR, LANES), BF16)]
+    scratch = [pltpu.VMEM((LOCAL, SIZE, 2 * SIZE), BF16)] * 2 + [pltpu.SemaphoreType.DMA((2,))]
+    args = (pltpu.with_memory_space_constraint(array, pltpu.HBM) for array in (offsets, keys, values))
+    return call(start_kernel, outs, tuple(args), 1, scratch, pltpu.HBM)
+
+
+def tables(rank, offsets, queries):
+    square = (LOCAL, ROWS, ROWS)
+    outs = [(square, BF16)] * 3 + [((PICKED, FAR * NEAR), BF16), ((FAR * NEAR, PICKED), BF16)]
+    return call(table_kernel, outs, (rank, offsets, queries), 2)
+
+
+def far_pieces(ordered, line_in, grad, grad_in):
+    outs = [((FAR, NEAR, LANES), BF16), ((SLOTS + NEAR, LANES), BF16), ((2, SIZE, HALF), BF16)]
+    return call(far_kernel, outs, (ordered, line_in, grad, grad_in), 0)
+
+
+def attention(rank, *arrays):
     outs = [
         ((2, SIZE, HALF), F32),
         ((2, SIZE, HALF), BF16),
@@ -327,13 +341,14 @@
         pltpu.VMEM((ROWS, LOCAL * SIZE), BF16),
         pltpu.VMEM((SHARE, WIDTH), F32),
         pltpu.VMEM((4, SIZE, HALF), F32),
+        pltpu.VMEM((4, SIZE, HALF), BF16),
     ]
-    return call(main_kernel, outs, (rank, offsets) + arrays + (jnp.asarray(shared_levels()),), 2, scratch)
-
-
-def far_return(rank, received, keep_far, keep_weight):
-    args = (rank, received, keep_far, keep_weight)
-    return call(far_return_kernel, [((FAR, NEAR + PART, LANES), BF16)], args, 1)[0]
+    return call(main_kernel, outs, (rank,) + arrays + (jnp.asarray(shared_levels()),), 1, scratch)
+
+
+def far_return(choice_back, received, keep_far, keep_weight):
+    args = (choice_back, received, keep_far, keep_weight)
+    return call(far_return_kernel, [((FAR, NEAR + PART, LANES), BF16)], args, 0)[0]
 
 
 def line_return(received, keep_line, far_in):
@@ -345,9 +360,9 @@
     return call(spread_kernel, outs, (line_in,), 0)
 
 
-def finish(offsets, keep_own, received, near_sum):
+def finish(to_token, keep_own, received, near_sum):
     outs = [((LOCAL, SIZE, 2 * SIZE), BF16)] * 2
-    return call(finish_kernel, outs, (offsets, keep_own, received, near_sum), 1, [pltpu.VMEM((ROWS, LANES), F32)])
+    return call(finish_kernel, outs, (to_token, keep_own, received, near_sum), 0, [pltpu.VMEM((ROWS, LANES), F32)])
 
 
 def weight_rows(spread_in):
@@ -373,28 +388,31 @@
     line_groups = [[far * 16 + line * 2 + core for line in range(LINE)] for far in range(FAR) for core in range(CORE)]
     side_groups = [[far * 16 + line * 2 + core for far in range(FAR) for core in range(CORE)] for line in range(LINE)]
     queries, keys, values = (array.transpose(1, 0, 2) for array in (queries, keys, values))
-    ordered, line_out, grad_out = start(offsets, keys, values, out_grad)
+    ordered, line_out = start(offsets, keys, values)
+    grad_in = swap_heads(out_grad, 1)
+    to_order, to_token, query, choice, choice_back = tables(rank, offsets, queries)
     line_in = trade(line_out, line_groups)
-    far_out, partner_out = far_pieces(ordered, line_in)
+    far_out, partner_out, grads = far_pieces(ordered, line_in, out_grad, grad_in)
+    other_grads = swap_heads(grads, 3)
     other_in = swap_cores(partner_out)
     far_in = trade(far_out, far_groups)
     other_far_in = swap_cores(far_in)
-    grads = lax.all_to_all(grad_out, "head", 0, 0, tiled=True)
     output_keep, output_send, query_grad, send, keep_line, keep_far, keep_own, keep_weight = attention(
-        rank, offsets, queries, out_weight, grads, ordered, line_in, far_in, other_in, other_far_in
+        rank, to_order, to_token, query, choice, out_weight, grads, other_grads,
+        ordered, line_in, far_in, other_in, other_far_in,
     )
     first = swap_heads(output_send, 1)
     received = swap_cores(send)
-    far_back = trade(far_return(rank, received, keep_far, keep_weight), far_groups)
-    far_back, first = lax.optimization_barrier((far_back, first))
+    far_back = trade(far_return(choice_back, received, keep_far, keep_weight), far_groups)
+    line_back = trade(line_return(received, keep_line, far_back), line_groups)
+    line_back, first = lax.optimization_barrier((line_back, first))
     output_sum = output_keep + first.astype(F32)
     second = swap_heads(output_sum[1].astype(BF16), 3)
-    line_back = trade(line_return(received, keep_line, far_back), line_groups)
-    line_back, second = lax.optimization_barrier((line_back, second))
+    near_sum, spread_out = spread_pieces(line_back)
+    spread_in = trade(spread_out, side_groups)
+    key_grad, value_grad = finish(to_token, keep_own, received, near_sum)
     output = (output_sum[0] + second.astype(F32)).astype(BF16)
-    near_sum, spread_out = spread_pieces(line_back)
-    weight_grad = weight_rows(trade(spread_out, side_groups))
-    key_grad, value_grad = finish(offsets, keep_own, received, near_sum)
+    weight_grad = weight_rows(spread_in)
     query_grad, key_grad, value_grad = (grad.transpose(1, 0, 2) for grad in (query_grad, key_grad, value_grad))
     return (output, query_grad, key_grad, value_grad, weight_grad)
 

time: 107 us -> 106 us (level)
  blocking collectives: 27.8 us -> 10.6 us
  starting transfers between devices: 46.3 us -> 60.7 us
    all_to_all x2 -> x1, blocking collectives: 27.8 us -> 10.6 us  [trade(): lax.all_to_all(pieces, 'seq', 0, 0, axis_index_groups=groups, tiled=True)]
    ppermute x2 -> x4, starting transfers between devices: 7.06 us -> 23.2 us  [swap_heads(): return lax.ppermute(block, 'head', [(i, i ^ way) for i in range(4)])]
    all_to_all x1 -> x0, starting transfers between devices: 9.26 us -> none  [shards(): grads = lax.all_to_all(grad_out, 'head', 0, 0, tiled=True)]
    all_to_all x3 -> x4, starting transfers between devices: 16.4 us -> 24.2 us  [trade(): lax.all_to_all(pieces, 'seq', 0, 0, axis_index_groups=groups, tiled=True)]
    ppermute x2 -> x4, waiting for transfers between devices: 6.86 us -> 12.4 us  [swap_heads(): return lax.ppermute(block, 'head', [(i, i ^ way) for i in range(4)])]
    all_to_all x3 -> x4, waiting for transfers between devices: 9.42 us -> 6.28 us  [trade(): lax.all_to_all(pieces, 'seq', 0, 0, axis_index_groups=groups, tiled=True)]
    ppermute x3, waiting for transfers between devices: 2.72 us -> 1.4 us  [swap_cores(): lax.ppermute(block, 'seq', [(i, i ^ 1) for i in range(FAR * LINE * CORE)])]
    pallas_call x8 -> x9, Pallas kernels: 11.3 us -> 11.2 us  [call(): pl.pallas_call(kernel, out_shape=[jax.ShapeDtypeStruct(shape, dtype) for...]
  transfers between devices with their start and end apart: 9 -> 11, of which waited for: 7 -> 8; matrix products, arithmetic and copies ran while one was open for 1% -> 1% of each run, Pallas kernels for 1% -> 2%
where the time goes in v5:
time: 106 us; the launch traced here: 105 us
  starting transfers between devices  60.7 us (57%)
  waiting for transfers between devices  20 us (19%)
  Pallas kernels  11.2 us (11%)
  blocking collectives  10.6 us (10%)
    all_to_all x4, starting transfers between devices, trade(): lax.all_to_all(pieces, 'seq', 0, 0, axis_index_groups=groups, tiled=True)  24.2 us
    ppermute x4, starting transfers between devices, swap_heads(): return lax.ppermute(block, 'head', [(i, i ^ way) for i in range(4)])  23.2 us
    ppermute x3, starting transfers between devices, swap_cores(): lax.ppermute(block, 'seq', [(i, i ^ 1) for i in range(FAR * LINE * CORE)])  13.3 us
    ppermute x4, waiting for transfers between devices, swap_heads(): return lax.ppermute(block, 'head', [(i, i ^ way) for i in range(4)])  12.4 us
    pallas_call x9, Pallas kernels, call(): pl.pallas_call(kernel, out_shape=[jax.ShapeDtypeStruct(shape, dtype) for...  11.2 us
    all_to_all x1, blocking collectives, trade(): lax.all_to_all(pieces, 'seq', 0, 0, axis_index_groups=groups, tiled=True)  10.6 us
    all_to_all x4, waiting for transfers between devices, trade(): lax.all_to_all(pieces, 'seq', 0, 0, axis_index_groups=groups, tiled=True)  6.28 us
  transfers between devices with their start and end apart: 11, of which 8 were waited for; matrix products, arithmetic and copies ran while one was open for 1% of the time, Pallas kernels for 2%

profile of v5, /device:TPU:1, one launch (start us, length us, event | category | flops | bytes accessed | tf_op | source)
XLA Modules:
  0.0 104.7 jit_solution(14555335162659299294)
XLA Ops:
  0.6 2.4 %shard_map.111 = (bf16[128,384]{1,0:T(8,128)(2,1)S(1)}, bf16[8,32,384]{2,1,0:T(8,128)(2,1)}) custom-call(s32[3]{0:T(128)} %offsets.3, bf16[3,64,128]{2,1,0:T(8,128)(2,1)} %bitcast.19, bf16[3,64,128]{2,1,0:T(8,128)(2,1)} %bitcast.20), custom_call_target="tpu_custom_call" | custom-call | tf_op jit(solution)/shard_map/pallas_call | solution.py:298
  3.1 0.0 copy-start.2
  3.1 7.8 %all-to-all-start = ((bf16[8,32,384]{2,1,0:T(8,128)(2,1)}), bf16[8,32,384]{2,1,0:T(8,128)(2,1)S(1)}, u32[]{:S(2)}, u32[]{:S(2)}) async-start(bf16[8,32,384]{2,1,0:T(8,128)(2,1)} %get-tuple-element.34), calls=%async_computation | async-start | bytes 393216 | tf_op jit(solution)/shard_map/all_to_all | solution.py:373
  10.9 0.0 copy-done.2
  10.9 5.8 %collective-permute-start = (bf16[64,384]{1,0:T(8,128)(2,1)S(1)}, bf16[64,384]{1,0:T(8,128)(2,1)S(1)}, u32[]{:S(2)}, u32[]{:S(2)}) collective-permute-start(bf16[64,384]{1,0:T(8,128)(2,1)S(1)} %copy-done.2), channel_id=1, source_target_pairs={{0,1},{1,0},{2,3},{3,2},{4,5},{5,4},{6,7},{7,6},{8,9},{9,8},{10,11... | collective-permute-start | bytes 147464 | tf_op jit(solution)/shard_map/ppermute | solution.py:381
  16.7 1.5 %collective-permute-done.grad_in = bf16[64,384]{1,0:T(8,128)(2,1)S(1)} collective-permute-done((bf16[64,384]{1,0:T(8,128)(2,1)S(1)}, bf16[64,384]{1,0:T(8,128)(2,1)S(1)}, u32[]{:S(2)}, u32[]{:S(2)}) %collective-permute-start) | collective-permute-done | bytes 49184 | tf_op jit(solution)/shard_map/ppermute | solution.py:381
  18.2 1.4 %all-to-all-done.line_in = bf16[8,32,384]{2,1,0:T(8,128)(2,1)S(1)} async-done(((bf16[8,32,384]{2,1,0:T(8,128)(2,1)}), bf16[8,32,384]{2,1,0:T(8,128)(2,1)S(1)}, u32[]{:S(2)}, u32[]{:S(2)}) %all-to-all-start) | async-done | bytes 196640 | tf_op jit(solution)/shard_map/all_to_all | solution.py:373
  19.6 0.0 copy-start
  19.6 0.7 shard_map.112
  20.3 0.0 copy-start.1
  20.3 0.0 copy-start.3
  20.3 6.0 %all-to-all-start.1 = ((bf16[8,32,384]{2,1,0:T(8,128)(2,1)}), bf16[8,32,384]{2,1,0:T(8,128)(2,1)S(1)}, u32[]{:S(2)}, u32[]{:S(2)}) async-start(bf16[8,32,384]{2,1,0:T(8,128)(2,1)} %get-tuple-element.36), calls=%async_computation.1 | async-start | bytes 393216 | tf_op jit(solution)/shard_map/all_to_all | solution.py:373
  26.4 4.8 %collective-permute-start.2 = (bf16[288,384]{1,0:T(8,128)(2,1)S(1)}, bf16[288,384]{1,0:T(8,128)(2,1)S(1)}, u32[]{:S(2)}, u32[]{:S(2)}) collective-permute-start(bf16[288,384]{1,0:T(8,128)(2,1)S(1)} %get-tuple-element.37), channel_id=1, source_target_pairs={{0,4},{4,0},{8,12},{12,8},{16,20},{20,16},{24,28},{28,24},{32,36},... | collective-permute-start | bytes 663560 | tf_op jit(solution)/shard_map/ppermute | solution.py:377
  31.2 1.0 all-to-all-done.1.far_in
  32.2 5.9 %collective-permute-start.3 = (bf16[8,32,384]{2,1,0:T(8,128)(2,1)S(1)}, bf16[8,32,384]{2,1,0:T(8,128)(2,1)S(1)}, u32[]{:S(2)}, u32[]{:S(2)}) collective-permute-start(bf16[8,32,384]{2,1,0:T(8,128)(2,1)S(1)} %all-to-all-done.1.far_in), channel_id=1, source_target_pairs={{0,4},{4,0},{8,12},{12,8},{16,20},{20,16},{24,28},{28,24},{32,36},... | collective-permute-start | bytes 589832 | tf_op jit(solution)/shard_map/ppermute | solution.py:377
  38.1 9.8 %collective-permute-start.1 = (bf16[2,64,384]{2,1,0:T(8,128)(2,1)S(1)}, bf16[2,64,384]{2,1,0:T(8,128)(2,1)S(1)}, u32[]{:S(2)}, u32[]{:S(2)}) collective-permute-start(bf16[2,64,384]{2,1,0:T(8,128)(2,1)S(1)} %get-tuple-element.35.grads), channel_id=1, source_target_pairs={{0,3},{1,2},{2,1},{3,0},{4,7},{5,6},{6,5},{7,4},{8,11},{9,10},{10,... | collective-permute-start | bytes 294920 | tf_op jit(solution)/shard_map/ppermute | solution.py:381
  47.9 0.1 pad_add_fusion.rank
  48.0 0.0 copy-start.4
  48.0 0.0 copy-done.3
  48.0 0.7 copy-done.4
  48.6 0.8 shard_map.110
  49.5 2.8 %collective-permute-done.1.other_grads = bf16[2,64,384]{2,1,0:T(8,128)(2,1)S(1)} collective-permute-done((bf16[2,64,384]{2,1,0:T(8,128)(2,1)S(1)}, bf16[2,64,384]{2,1,0:T(8,128)(2,1)S(1)}, u32[]{:S(2)}, u32[]{:S(2)}) %collective-permute-start.1) | collective-permute-done | bytes 98336 | tf_op jit(solution)/shard_map/ppermute | solution.py:381
  52.3 0.0 collective-permute-done.2.other_in
  52.3 0.0 collective-permute-done.3.other_far_in
  52.3 0.0 copy-done
  52.3 0.0 copy-done.1
  52.3 3.6 %shard_map.113 = (f32[2,64,384]{2,1,0:T(8,128)S(1)}, bf16[2,64,384]{2,1,0:T(8,128)(2,1)S(1)}, bf16[3,64,128]{2,1,0:T(8,128)(2,1)}, bf16[576,384]{1,0:T(8,128)(2,...) custom-call(s32[4]{0:T(128)S(1)} %pad_add_fusion.rank, ...), custom_call_target="tpu_custom_call" | custom-call | tf_op jit(solution)/shard_map/pallas_call | solution.py:298
  56.0 2.6 %collective-permute-start.4 = (bf16[576,384]{1,0:T(8,128)(2,1)S(1)}, bf16[576,384]{1,0:T(8,128)(2,1)S(1)}, u32[]{:S(2)}, u32[]{:S(2)}) collective-permute-start(bf16[576,384]{1,0:T(8,128)(2,1)S(1)} %get-tuple-element.39), channel_id=1, source_target_pairs={{0,4},{4,0},{8,12},{12,8},{16,20},{20,16},{24,28},{28,24},{32,36},... | collective-permute-start | bytes 1327112 | tf_op jit(solution)/shard_map/ppermute | solution.py:377
  58.6 1.4 %collective-permute-done.4.received = bf16[576,384]{1,0:T(8,128)(2,1)S(1)} collective-permute-done((bf16[576,384]{1,0:T(8,128)(2,1)S(1)}, bf16[576,384]{1,0:T(8,128)(2,1)S(1)}, u32[]{:S(2)}, u32[]{:S(2)}) %collective-permute-start.4) | collective-permute-done | bytes 442400 | tf_op jit(solution)/shard_map/ppermute | solution.py:377
  60.0 0.2 shard_map.114
  60.2 10.6 %all_to_all.25.far_in = bf16[8,56,384]{2,1,0:T(8,128)(2,1)S(1)} all-to-all(bf16[8,56,384]{2,1,0:T(8,128)(2,1)S(1)} %shard_map.114), channel_id=1, replica_groups={{0,64,128,192,256,320,384,448},{4,68,132,196,260,324,388,452},{8,72,136..., dimensions={0} | all-to-all | bytes 688128 | tf_op jit(solution)/shard_map/all_to_all | solution.py:373
  70.8 0.8 shard_map.115
  71.6 3.8 %all-to-all-start.3 = ((bf16[8,56,384]{2,1,0:T(8,128)(2,1)}), bf16[8,56,384]{2,1,0:T(8,128)(2,1)S(1)}, u32[]{:S(2)}, u32[]{:S(2)}) async-start(bf16[8,56,384]{2,1,0:T(8,128)(2,1)} %shard_map.115), calls=%async_computation.3 | async-start | bytes 688128 | tf_op jit(solution)/shard_map/all_to_all | solution.py:373
  75.4 2.0 %collective-permute-start.5 = (bf16[2,64,384]{2,1,0:T(8,128)(2,1)S(1)}, bf16[2,64,384]{2,1,0:T(8,128)(2,1)S(1)}, u32[]{:S(2)}, u32[]{:S(2)}) collective-permute-start(bf16[2,64,384]{2,1,0:T(8,128)(2,1)S(1)} %get-tuple-element.44), channel_id=1, source_target_pairs={{0,1},{1,0},{2,3},{3,2},{4,5},{5,4},{6,7},{7,6},{8,9},{9,8},{10,11... | collective-permute-start | bytes 294920 | tf_op jit(solution)/shard_map/ppermute | solution.py:381
  77.4 5.5 %collective-permute-done.5 = bf16[2,64,384]{2,1,0:T(8,128)(2,1)S(1)} collective-permute-done((bf16[2,64,384]{2,1,0:T(8,128)(2,1)S(1)}, bf16[2,64,384]{2,1,0:T(8,128)(2,1)S(1)}, u32[]{:S(2)}, u32[]{:S(2)}) %collective-permute-start.5) | collective-permute-done | bytes 98336 | tf_op jit(solution)/shard_map/ppermute | solution.py:381
  82.9 3.9 %all-to-all-done.3.line_in = bf16[8,56,384]{2,1,0:T(8,128)(2,1)S(1)} async-done(((bf16[8,56,384]{2,1,0:T(8,128)(2,1)}), bf16[8,56,384]{2,1,0:T(8,128)(2,1)S(1)}, u32[]{:S(2)}, u32[]{:S(2)}) %all-to-all-start.3) | async-done | bytes 344096 | tf_op jit(solution)/shard_map/all_to_all | solution.py:373
  86.8 0.8 shard_map.116
  87.5 6.6 %all-to-all-start.4 = ((bf16[16,24,384]{2,1,0:T(8,128)(2,1)}), bf16[16,24,384]{2,1,0:T(8,128)(2,1)S(1)}, u32[]{:S(2)}, u32[]{:S(2)}) async-start(bf16[16,24,384]{2,1,0:T(8,128)(2,1)} %get-tuple-element.52), calls=%async_computation.4 | async-start | bytes 589824 | tf_op jit(solution)/shard_map/all_to_all | solution.py:373
  94.1 5.7 %collective-permute-start.6 = (bf16[64,384]{1,0:T(8,128)(2,1)S(1)}, bf16[64,384]{1,0:T(8,128)(2,1)S(1)}, u32[]{:S(2)}, u32[]{:S(2)}) collective-permute-start(bf16[64,384]{1,0:T(8,128)(2,1)S(1)} %fusion.2), channel_id=1, source_target_pairs={{0,3},{1,2},{2,1},{3,0},{4,7},{5,6},{6,5},{7,4},{8,11},{9,10},{10,... | collective-permute-start | bytes 147464 | tf_op jit(solution)/shard_map/ppermute | solution.py:381
  99.8 0.9 shard_map.117
  100.7 2.5 %collective-permute-done.6 = bf16[64,384]{1,0:T(8,128)(2,1)S(1)} collective-permute-done((bf16[64,384]{1,0:T(8,128)(2,1)S(1)}, bf16[64,384]{1,0:T(8,128)(2,1)S(1)}, u32[]{:S(2)}, u32[]{:S(2)}) %collective-permute-start.6) | collective-permute-done | bytes 49184 | tf_op jit(solution)/shard_map/ppermute | solution.py:381
  103.2 0.6 fusion.1
  103.8 0.0 all-to-all-done.4.spread_in
  103.8 0.9 shard_map.118
  (2 shorter events, 0.0 us)
Async XLA Ops:
  3.1 7.8 %copy-start.2 = (bf16[64,384]{1,0:T(8,128)(2,1)S(1)}, bf16[64,384]{1,0:T(8,128)(2,1)}, u32[]{:S(2)}) copy-start(bf16[64,384]{1,0:T(8,128)(2,1)} %grad.1) | copy-start | bytes 147460
  3.1 16.5 %all-to-all-start = ((bf16[8,32,384]{2,1,0:T(8,128)(2,1)}), bf16[8,32,384]{2,1,0:T(8,128)(2,1)S(1)}, u32[]{:S(2)}, u32[]{:S(2)}) async-start(bf16[8,32,384]{2,1,0:T(8,128)(2,1)} %get-tuple-element.34), calls=%async_computation | async-start | bytes 393216 | tf_op jit(solution)/shard_map/all_to_all | solution.py:373
  10.9 7.3 %collective-permute-start = (bf16[64,384]{1,0:T(8,128)(2,1)S(1)}, bf16[64,384]{1,0:T(8,128)(2,1)S(1)}, u32[]{:S(2)}, u32[]{:S(2)}) collective-permute-start(bf16[64,384]{1,0:T(8,128)(2,1)S(1)} %copy-done.2), channel_id=1, source_target_pairs={{0,1},{1,0},{2,3},{3,2},{4,5},{5,4},{6,7},{7,6},{8,9},{9,8},{10,11... | collective-permute-start | bytes 147464 | tf_op jit(solution)/shard_map/ppermute | solution.py:381
  19.6 32.7 %copy-start = (f32[832,128]{1,0:T(8,128)S(1)}, f32[832,128]{1,0:T(8,128)}, u32[]{:S(2)}) copy-start(f32[832,128]{1,0:T(8,128)} %constant.17.clone.bias) | copy-start | bytes 1277956
  20.3 32.0 %copy-start.1 = (bf16[192,768]{1,0:T(8,128)(2,1)S(1)}, bf16[192,768]{1,0:T(8,128)(2,1)}, u32[]{:S(2)}) copy-start(bf16[192,768]{1,0:T(8,128)(2,1)} %weight.1) | copy-start | bytes 884740
  20.3 27.7 %copy-start.3 = (bf16[64,3,128]{2,0,1:T(8,128)(2,1)S(1)}, bf16[64,3,128]{2,0,1:T(8,128)(2,1)}, u32[]{:S(2)}) copy-start(bf16[64,3,128]{2,0,1:T(8,128)(2,1)} %param.7) | copy-start | bytes 147460
  20.3 11.8 %all-to-all-start.1 = ((bf16[8,32,384]{2,1,0:T(8,128)(2,1)}), bf16[8,32,384]{2,1,0:T(8,128)(2,1)S(1)}, u32[]{:S(2)}, u32[]{:S(2)}) async-start(bf16[8,32,384]{2,1,0:T(8,128)(2,1)} %get-tuple-element.36), calls=%async_computation.1 | async-start | bytes 393216 | tf_op jit(solution)/shard_map/all_to_all | solution.py:373
  26.4 25.9 %collective-permute-start.2 = (bf16[288,384]{1,0:T(8,128)(2,1)S(1)}, bf16[288,384]{1,0:T(8,128)(2,1)S(1)}, u32[]{:S(2)}, u32[]{:S(2)}) collective-permute-start(bf16[288,384]{1,0:T(8,128)(2,1)S(1)} %get-tuple-element.37), channel_id=1, source_target_pairs={{0,4},{4,0},{8,12},{12,8},{16,20},{20,16},{24,28},{28,24},{32,36},... | collective-permute-start | bytes 663560 | tf_op jit(solution)/shard_map/ppermute | solution.py:377
  32.2 20.1 %collective-permute-start.3 = (bf16[8,32,384]{2,1,0:T(8,128)(2,1)S(1)}, bf16[8,32,384]{2,1,0:T(8,128)(2,1)S(1)}, u32[]{:S(2)}, u32[]{:S(2)}) collective-permute-start(bf16[8,32,384]{2,1,0:T(8,128)(2,1)S(1)} %all-to-all-done.1.far_in), channel_id=1, source_target_pairs={{0,4},{4,0},{8,12},{12,8},{16,20},{20,16},{24,28},{28,24},{32,36},... | collective-permute-start | bytes 589832 | tf_op jit(solution)/shard_map/ppermute | solution.py:377
  38.1 14.2 %collective-permute-start.1 = (bf16[2,64,384]{2,1,0:T(8,128)(2,1)S(1)}, bf16[2,64,384]{2,1,0:T(8,128)(2,1)S(1)}, u32[]{:S(2)}, u32[]{:S(2)}) collective-permute-start(bf16[2,64,384]{2,1,0:T(8,128)(2,1)S(1)} %get-tuple-element.35.grads), channel_id=1, source_target_pairs={{0,3},{1,2},{2,1},{3,0},{4,7},{5,6},{6,5},{7,4},{8,11},{9,10},{10,... | collective-permute-start | bytes 294920 | tf_op jit(solution)/shard_map/ppermute | solution.py:381
  48.0 0.7 copy-start.4
  56.0 4.0 %collective-permute-start.4 = (bf16[576,384]{1,0:T(8,128)(2,1)S(1)}, bf16[576,384]{1,0:T(8,128)(2,1)S(1)}, u32[]{:S(2)}, u32[]{:S(2)}) collective-permute-start(bf16[576,384]{1,0:T(8,128)(2,1)S(1)} %get-tuple-element.39), channel_id=1, source_target_pairs={{0,4},{4,0},{8,12},{12,8},{16,20},{20,16},{24,28},{28,24},{32,36},... | collective-permute-start | bytes 1327112 | tf_op jit(solution)/shard_map/ppermute | solution.py:377
  71.6 15.2 %all-to-all-start.3 = ((bf16[8,56,384]{2,1,0:T(8,128)(2,1)}), bf16[8,56,384]{2,1,0:T(8,128)(2,1)S(1)}, u32[]{:S(2)}, u32[]{:S(2)}) async-start(bf16[8,56,384]{2,1,0:T(8,128)(2,1)} %shard_map.115), calls=%async_computation.3 | async-start | bytes 688128 | tf_op jit(solution)/shard_map/all_to_all | solution.py:373
  75.4 7.5 %collective-permute-start.5 = (bf16[2,64,384]{2,1,0:T(8,128)(2,1)S(1)}, bf16[2,64,384]{2,1,0:T(8,128)(2,1)S(1)}, u32[]{:S(2)}, u32[]{:S(2)}) collective-permute-start(bf16[2,64,384]{2,1,0:T(8,128)(2,1)S(1)} %get-tuple-element.44), channel_id=1, source_target_pairs={{0,1},{1,0},{2,3},{3,2},{4,5},{5,4},{6,7},{7,6},{8,9},{9,8},{10,11... | collective-permute-start | bytes 294920 | tf_op jit(solution)/shard_map/ppermute | solution.py:381
  87.5 16.3 %all-to-all-start.4 = ((bf16[16,24,384]{2,1,0:T(8,128)(2,1)}), bf16[16,24,384]{2,1,0:T(8,128)(2,1)S(1)}, u32[]{:S(2)}, u32[]{:S(2)}) async-start(bf16[16,24,384]{2,1,0:T(8,128)(2,1)} %get-tuple-element.52), calls=%async_computation.4 | async-start | bytes 589824 | tf_op jit(solution)/shard_map/all_to_all | solution.py:373
  94.1 9.1 %collective-permute-start.6 = (bf16[64,384]{1,0:T(8,128)(2,1)S(1)}, bf16[64,384]{1,0:T(8,128)(2,1)S(1)}, u32[]{:S(2)}, u32[]{:S(2)}) collective-permute-start(bf16[64,384]{1,0:T(8,128)(2,1)S(1)} %fusion.2), channel_id=1, source_target_pairs={{0,3},{1,2},{2,1},{3,0},{4,7},{5,6},{6,5},{7,4},{8,11},{9,10},{10,... | collective-permute-start | bytes 147464 | tf_op jit(solution)/shard_map/ppermute | solution.py:381

commit v6 on v5

--- a/solution.py
+++ b/solution.py
@@ -107,15 +107,16 @@
     return jnp.concatenate([even, odd], axis=0).astype(BF16)
 
 
-def start_kernel(offsets, keys, values, ordered, line_out, keys_here, values_here, done):
+def start_kernel(offsets_far, keys, values, ordered, line_out, offsets, keys_here, values_here, done):
     copies = [
         pltpu.make_async_copy(source, target, done.at[at])
-        for at, (source, target) in enumerate(((keys, keys_here), (values, values_here)))
+        for at, (source, target) in enumerate(((offsets_far, offsets), (keys, keys_here), (values, values_here)))
     ]
     for copy in copies:
         copy.start()
+    copies[0].wait()
     orders = [order_from(offsets[head], 0) for head in range(LOCAL)]
-    for copy in copies:
+    for copy in copies[1:]:
         copy.wait()
     for head in range(LOCAL):
         lanes = pl.ds(head * 2 * SIZE, 2 * SIZE)
@@ -139,7 +140,9 @@
     return one_hot(far_place(row, far) == lax.broadcasted_iota(jnp.int32, shape, 1 - row_axis))
 
 
-def table_kernel(rank, offsets, queries, to_order, to_token, query, choice, choice_back):
+def table_kernel(rank, offsets, queries, grad, to_order, to_token, query, choice, choice_back, grads_out):
+    for slot in range(4):
+        grads_out[slot] = grad[...]
     for head in range(LOCAL):
         order = order_from(offsets[head], 0)
         pairs = queries[head].astype(F32)
@@ -150,9 +153,7 @@
     choice_back[...] = far_choice(rank[0], 1)
 
 
-def far_kernel(ordered, line_in, grad, grad_in, far_out, partner_out, grads_out):
-    grads_out[0] = grad[...]
-    grads_out[1] = grad_in[...]
+def far_kernel(ordered, line_in, far_out, partner_out):
     for slot in range(LINE):
         partner_out[slot * NEAR : (slot + 1) * NEAR, :] = line_in[slot]
     partner_out[SLOTS:, :] = ordered[NEAR : 2 * NEAR, :]
@@ -165,9 +166,9 @@
 
 
 def main_kernel(
-    rank, to_order, to_token, query, choice, weight, grads, other_grads, ordered, line_in, far_in, other_in, other_far_in, bias,
+    rank, to_order, to_token, query, choice, weight, grads, ordered, line_in, far_in, other_in, other_far_in, bias,
     output_keep, output_send, query_grad, send, keep_line, keep_far, keep_own, keep_weight,
-    held, full_grad, attn, weight_term, parts, grad_parts,
+    held, full_grad, attn, weight_term, parts,
 ):
     line, core, mine = rank[1], rank[2], rank[3]
     held[0:ROWS, :] = ordered[...]
@@ -181,12 +182,10 @@
             held[at : at + NEAR, :] = line_in[slot]
         at = OTHER_AT + step * NEAR
         held[at : at + NEAR, :] = other_in[pl.ds(pl.multiple_of(slot * NEAR, NEAR), NEAR), :]
-    for way, piece in enumerate((grads[0], grads[1], other_grads[1], other_grads[0])):
-        grad_parts[mine ^ way] = piece
     for parity in range(2):
         for half in range(2):
             place = (slice(parity * SIZE, (parity + 1) * SIZE), slice(half * HALF, (half + 1) * HALF))
-            full_grad[place] = grad_parts[2 * parity + half]
+            full_grad[place] = grads[2 * parity + half]
     heads = range(LOCAL)
     lanes = [pl.ds(head * 2 * SIZE, 2 * SIZE) for head in heads]
     grad = dot(full_grad[...], weight[...], NT).astype(BF16)
@@ -308,20 +307,20 @@
 
 def start(offsets, keys, values):
     outs = [((ROWS, LANES), BF16), ((LINE, NEAR, LANES), BF16)]
-    scratch = [pltpu.VMEM((LOCAL, SIZE, 2 * SIZE), BF16)] * 2 + [pltpu.SemaphoreType.DMA((2,))]
+    here = pltpu.VMEM((LOCAL, SIZE, 2 * SIZE), BF16)
+    scratch = [pltpu.SMEM((LOCAL,), jnp.int32), here, here, pltpu.SemaphoreType.DMA((3,))]
     args = (pltpu.with_memory_space_constraint(array, pltpu.HBM) for array in (offsets, keys, values))
-    return call(start_kernel, outs, tuple(args), 1, scratch, pltpu.HBM)
-
-
-def tables(rank, offsets, queries):
+    return call(start_kernel, outs, tuple(args), 0, scratch, pltpu.HBM)
+
+
+def tables(rank, offsets, queries, grad):
     square = (LOCAL, ROWS, ROWS)
     outs = [(square, BF16)] * 3 + [((PICKED, FAR * NEAR), BF16), ((FAR * NEAR, PICKED), BF16)]
-    return call(table_kernel, outs, (rank, offsets, queries), 2)
-
-
-def far_pieces(ordered, line_in, grad, grad_in):
-    outs = [((FAR, NEAR, LANES), BF16), ((SLOTS + NEAR, LANES), BF16), ((2, SIZE, HALF), BF16)]
-    return call(far_kernel, outs, (ordered, line_in, grad, grad_in), 0)
+    return call(table_kernel, outs + [((4, SIZE, HALF), BF16)], (rank, offsets, queries, grad), 2)
+
+
+def far_pieces(ordered, line_in):
+    return call(far_kernel, [((FAR, NEAR, LANES), BF16), ((SLOTS + NEAR, LANES), BF16)], (ordered, line_in), 0)
 
 
 def attention(rank, *arrays):
@@ -341,7 +340,6 @@
         pltpu.VMEM((ROWS, LOCAL * SIZE), BF16),
         pltpu.VMEM((SHARE, WIDTH), F32),
         pltpu.VMEM((4, SIZE, HALF), F32),
-        pltpu.VMEM((4, SIZE, HALF), BF16),
     ]
     return call(main_kernel, outs, (rank,) + arrays + (jnp.asarray(shared_levels()),), 1, scratch)
 
@@ -389,17 +387,15 @@
     side_groups = [[far * 16 + line * 2 + core for far in range(FAR) for core in range(CORE)] for line in range(LINE)]
     queries, keys, values = (array.transpose(1, 0, 2) for array in (queries, keys, values))
     ordered, line_out = start(offsets, keys, values)
-    grad_in = swap_heads(out_grad, 1)
-    to_order, to_token, query, choice, choice_back = tables(rank, offsets, queries)
+    to_order, to_token, query, choice, choice_back, grads_out = tables(rank, offsets, queries, out_grad)
     line_in = trade(line_out, line_groups)
-    far_out, partner_out, grads = far_pieces(ordered, line_in, out_grad, grad_in)
-    other_grads = swap_heads(grads, 3)
+    far_out, partner_out = far_pieces(ordered, line_in)
     other_in = swap_cores(partner_out)
     far_in = trade(far_out, far_groups)
     other_far_in = swap_cores(far_in)
+    grads = lax.all_to_all(grads_out, "head", 0, 0, tiled=True)
     output_keep, output_send, query_grad, send, keep_line, keep_far, keep_own, keep_weight = attention(
-        rank, to_order, to_token, query, choice, out_weight, grads, other_grads,
-        ordered, line_in, far_in, other_in, other_far_in,
+        rank, to_order, to_token, query, choice, out_weight, grads, ordered, line_in, far_in, other_in, other_far_in
     )
     first = swap_heads(output_send, 1)
     received = swap_cores(send)

time: 106 us -> 102 us (0.962)
  starting transfers between devices: 60.7 us -> 44.7 us
  blocking collectives: 10.6 us -> 26.3 us
  waiting for transfers between devices: 20 us -> 18.4 us
    ppermute x4 -> x2, starting transfers between devices: 23.2 us -> 6.14 us  [swap_heads(): return lax.ppermute(block, 'head', [(i, i ^ way) for i in range(4)])]
    all_to_all x1 -> x2, blocking collectives: 10.6 us -> 26.3 us  [trade(): lax.all_to_all(pieces, 'seq', 0, 0, axis_index_groups=groups, tiled=True)]
    all_to_all x0 -> x1, starting transfers between devices: none -> 9.12 us  [shards(): grads = lax.all_to_all(grads_out, 'head', 0, 0, tiled=True)]
    all_to_all x4 -> x3, starting transfers between devices: 24.2 us -> 15.9 us  [trade(): lax.all_to_all(pieces, 'seq', 0, 0, axis_index_groups=groups, tiled=True)]
    ppermute x4 -> x2, waiting for transfers between devices: 12.4 us -> 7.6 us  [swap_heads(): return lax.ppermute(block, 'head', [(i, i ^ way) for i in range(4)])]
    all_to_all x4 -> x3, waiting for transfers between devices: 6.28 us -> 8.06 us  [trade(): lax.all_to_all(pieces, 'seq', 0, 0, axis_index_groups=groups, tiled=True)]
    ppermute x3, waiting for transfers between devices: 1.4 us -> 2.79 us  [swap_cores(): lax.ppermute(block, 'seq', [(i, i ^ 1) for i in range(FAR * LINE * CORE)])]
  transfers between devices with their start and end apart: 11 -> 9, of which waited for: 8 -> 7; matrix products, arithmetic and copies ran while one was open for 1% -> 1% of each run, Pallas kernels for 2% -> 2%
where the time goes in v6:
time: 102 us; the launch traced here: 101 us
  starting transfers between devices  44.7 us (44%)
  blocking collectives  26.3 us (26%)
  waiting for transfers between devices  18.4 us (18%)
  Pallas kernels  10.4 us (10%)
    all_to_all x2, blocking collectives, trade(): lax.all_to_all(pieces, 'seq', 0, 0, axis_index_groups=groups, tiled=True)  26.3 us
    all_to_all x3, starting transfers between devices, trade(): lax.all_to_all(pieces, 'seq', 0, 0, axis_index_groups=groups, tiled=True)  15.9 us
    ppermute x3, starting transfers between devices, swap_cores(): lax.ppermute(block, 'seq', [(i, i ^ 1) for i in range(FAR * LINE * CORE)])  13.6 us
    pallas_call x9, Pallas kernels, call(): pl.pallas_call(kernel, out_shape=[jax.ShapeDtypeStruct(shape, dtype) for...  10.4 us
    all_to_all x1, starting transfers between devices, shards(): grads = lax.all_to_all(grads_out, 'head', 0, 0, tiled=True)  9.12 us
    all_to_all x3, waiting for transfers between devices, trade(): lax.all_to_all(pieces, 'seq', 0, 0, axis_index_groups=groups, tiled=True)  8.06 us
    ppermute x2, waiting for transfers between devices, swap_heads(): return lax.ppermute(block, 'head', [(i, i ^ way) for i in range(4)])  7.6 us
    ppermute x2, starting transfers between devices, swap_heads(): return lax.ppermute(block, 'head', [(i, i ^ way) for i in range(4)])  6.14 us
  transfers between devices with their start and end apart: 9, of which 7 were waited for; matrix products, arithmetic and copies ran while one was open for 1% of the time, Pallas kernels for 2%

profile of v6, /device:TPU:1, one launch (start us, length us, event | category | flops | bytes accessed | tf_op | source)
XLA Modules:
  0.0 101.4 jit_solution(1470199726420917664)
XLA Ops:
  0.6 1.1 %shard_map.111 = (bf16[128,384]{1,0:T(8,128)(2,1)S(1)}, bf16[8,32,384]{2,1,0:T(8,128)(2,1)S(1)}) custom-call(s32[3]{0:T(128)} %offsets_far.1, bf16[3,64,128]{2,1,0:T(8,128)(2,1)} %bitcast.19, bf16[3,64,128]{2,1,0:T(8,128)(2,1)} %bitcast.20), custom_call_target="tpu_custom_call" | custom-call | tf_op jit(solution)/shard_map/pallas_call | solution.py:297
  1.7 16.2 %all_to_all.30.line_in = bf16[8,32,384]{2,1,0:T(8,128)(2,1)S(1)} all-to-all(bf16[8,32,384]{2,1,0:T(8,128)(2,1)S(1)} %get-tuple-element.35), channel_id=1, replica_groups={{0,8,16,24,32,40,48,56},{4,12,20,28,36,44,52,60},{64,72,80,88,96,104,11..., dimensions={0} | all-to-all | bytes 393216 | tf_op jit(solution)/shard_map/all_to_all | solution.py:371
  17.9 0.0 copy-start.4
  17.9 0.7 shard_map.112
  18.6 0.0 copy-start.2
  18.6 0.0 copy-start.3
  18.6 0.0 copy-start
  18.6 6.0 %all-to-all-start.2 = ((bf16[8,32,384]{2,1,0:T(8,128)(2,1)}), bf16[8,32,384]{2,1,0:T(8,128)(2,1)S(1)}, u32[]{:S(2)}, u32[]{:S(2)}) async-start(bf16[8,32,384]{2,1,0:T(8,128)(2,1)} %get-tuple-element.36), calls=%async_computation.2 | async-start | bytes 393216 | tf_op jit(solution)/shard_map/all_to_all | solution.py:371
  24.7 0.0 copy-start.1
  24.7 0.1 pad_add_fusion.rank
  24.8 0.0 copy-done.4
  24.8 0.0 copy-done.2
  24.8 0.0 copy-done.3
  24.8 1.4 %shard_map.110 = (bf16[3,128,128]{2,1,0:T(8,128)(2,1)S(1)}, bf16[3,128,128]{2,1,0:T(8,128)(2,1)S(1)}, bf16[3,128,128]{2,1,0:T(8,128)(2,1)S(1)}, bf16[96,256]{1,0...) custom-call(s32[4]{0:T(128)S(1)} %pad_add_fusion.rank, s32[3]{0:T(128)S(1)} %copy-done.4, ...), custom_call_target="tpu_custom_call" | custom-call | tf_op jit(solution)/shard_map/pallas_call | solution.py:297
  26.2 4.3 %all-to-all-done.2.far_in = bf16[8,32,384]{2,1,0:T(8,128)(2,1)S(1)} async-done(((bf16[8,32,384]{2,1,0:T(8,128)(2,1)}), bf16[8,32,384]{2,1,0:T(8,128)(2,1)S(1)}, u32[]{:S(2)}, u32[]{:S(2)}) %all-to-all-start.2) | async-done | bytes 196640 | tf_op jit(solution)/shard_map/all_to_all | solution.py:371
  30.5 9.1 %all-to-all-start = ((bf16[4,64,384]{2,1,0:T(8,128)(2,1)}), bf16[4,64,384]{2,1,0:T(8,128)(2,1)S(1)}, u32[]{:S(2)}, u32[]{:S(2)}) async-start(bf16[4,64,384]{2,1,0:T(8,128)(2,1)} %get-tuple-element.33), calls=%async_computation | async-start | bytes 393216 | tf_op jit(solution)/shard_map/all_to_all | solution.py:396
  39.6 6.2 %collective-permute-start = (bf16[288,384]{1,0:T(8,128)(2,1)S(1)}, bf16[288,384]{1,0:T(8,128)(2,1)S(1)}, u32[]{:S(2)}, u32[]{:S(2)}) collective-permute-start(bf16[288,384]{1,0:T(8,128)(2,1)S(1)} %get-tuple-element.37), channel_id=1, source_target_pairs={{0,4},{4,0},{8,12},{12,8},{16,20},{20,16},{24,28},{28,24},{32,36},... | collective-permute-start | bytes 663560 | tf_op jit(solution)/shard_map/ppermute | solution.py:375
  45.8 1.9 %collective-permute-start.1 = (bf16[8,32,384]{2,1,0:T(8,128)(2,1)S(1)}, bf16[8,32,384]{2,1,0:T(8,128)(2,1)S(1)}, u32[]{:S(2)}, u32[]{:S(2)}) collective-permute-start(bf16[8,32,384]{2,1,0:T(8,128)(2,1)S(1)} %all-to-all-done.2.far_in), channel_id=1, source_target_pairs={{0,4},{4,0},{8,12},{12,8},{16,20},{20,16},{24,28},{28,24},{32,36},... | collective-permute-start | bytes 589832 | tf_op jit(solution)/shard_map/ppermute | solution.py:375
  47.8 0.0 all-to-all-done.grads
  47.8 0.0 collective-permute-done.other_in
  47.8 1.4 %collective-permute-done.1.other_far_in = bf16[8,32,384]{2,1,0:T(8,128)(2,1)S(1)} collective-permute-done((bf16[8,32,384]{2,1,0:T(8,128)(2,1)S(1)}, bf16[8,32,384]{2,1,0:T(8,128)(2,1)S(1)}, u32[]{:S(2)}, u32[]{:S(2)}) %collective-permute-start.1) | collective-permute-done | bytes 196640 | tf_op jit(solution)/shard_map/ppermute | solution.py:375
  49.2 0.0 copy-done
  49.2 0.0 copy-done.1
  49.2 3.6 %shard_map.113 = (f32[2,64,384]{2,1,0:T(8,128)S(1)}, bf16[2,64,384]{2,1,0:T(8,128)(2,1)S(1)}, bf16[3,64,128]{2,1,0:T(8,128)(2,1)}, bf16[576,384]{1,0:T(8,128)(2,...) custom-call(s32[4]{0:T(128)S(1)} %pad_add_fusion.rank, ...), custom_call_target="tpu_custom_call" | custom-call | tf_op jit(solution)/shard_map/pallas_call | solution.py:297
  52.8 5.4 %collective-permute-start.2 = (bf16[576,384]{1,0:T(8,128)(2,1)S(1)}, bf16[576,384]{1,0:T(8,128)(2,1)S(1)}, u32[]{:S(2)}, u32[]{:S(2)}) collective-permute-start(bf16[576,384]{1,0:T(8,128)(2,1)S(1)} %get-tuple-element.39), channel_id=1, source_target_pairs={{0,4},{4,0},{8,12},{12,8},{16,20},{20,16},{24,28},{28,24},{32,36},... | collective-permute-start | bytes 1327112 | tf_op jit(solution)/shard_map/ppermute | solution.py:375
  58.2 1.4 %collective-permute-done.2.received = bf16[576,384]{1,0:T(8,128)(2,1)S(1)} collective-permute-done((bf16[576,384]{1,0:T(8,128)(2,1)S(1)}, bf16[576,384]{1,0:T(8,128)(2,1)S(1)}, u32[]{:S(2)}, u32[]{:S(2)}) %collective-permute-start.2) | collective-permute-done | bytes 442400 | tf_op jit(solution)/shard_map/ppermute | solution.py:375
  59.6 0.2 shard_map.114
  59.9 10.1 %all_to_all.31.far_in = bf16[8,56,384]{2,1,0:T(8,128)(2,1)S(1)} all-to-all(bf16[8,56,384]{2,1,0:T(8,128)(2,1)S(1)} %shard_map.114), channel_id=1, replica_groups={{0,64,128,192,256,320,384,448},{4,68,132,196,260,324,388,452},{8,72,136..., dimensions={0} | all-to-all | bytes 688128 | tf_op jit(solution)/shard_map/all_to_all | solution.py:371
  69.9 0.8 shard_map.115
  70.8 3.4 %all-to-all-start.4 = ((bf16[8,56,384]{2,1,0:T(8,128)(2,1)}), bf16[8,56,384]{2,1,0:T(8,128)(2,1)S(1)}, u32[]{:S(2)}, u32[]{:S(2)}) async-start(bf16[8,56,384]{2,1,0:T(8,128)(2,1)} %shard_map.115), calls=%async_computation.4 | async-start | bytes 688128 | tf_op jit(solution)/shard_map/all_to_all | solution.py:371
  74.2 3.2 %collective-permute-start.3 = (bf16[2,64,384]{2,1,0:T(8,128)(2,1)S(1)}, bf16[2,64,384]{2,1,0:T(8,128)(2,1)S(1)}, u32[]{:S(2)}, u32[]{:S(2)}) collective-permute-start(bf16[2,64,384]{2,1,0:T(8,128)(2,1)S(1)} %get-tuple-element.44), channel_id=1, source_target_pairs={{0,1},{1,0},{2,3},{3,2},{4,5},{5,4},{6,7},{7,6},{8,9},{9,8},{10,11... | collective-permute-start | bytes 294920 | tf_op jit(solution)/shard_map/ppermute | solution.py:379
  77.4 4.5 %collective-permute-done.3 = bf16[2,64,384]{2,1,0:T(8,128)(2,1)S(1)} collective-permute-done((bf16[2,64,384]{2,1,0:T(8,128)(2,1)S(1)}, bf16[2,64,384]{2,1,0:T(8,128)(2,1)S(1)}, u32[]{:S(2)}, u32[]{:S(2)}) %collective-permute-start.3) | collective-permute-done | bytes 98336 | tf_op jit(solution)/shard_map/ppermute | solution.py:379
  81.9 3.7 %all-to-all-done.4.line_in = bf16[8,56,384]{2,1,0:T(8,128)(2,1)S(1)} async-done(((bf16[8,56,384]{2,1,0:T(8,128)(2,1)}), bf16[8,56,384]{2,1,0:T(8,128)(2,1)S(1)}, u32[]{:S(2)}, u32[]{:S(2)}) %all-to-all-start.4) | async-done | bytes 344096 | tf_op jit(solution)/shard_map/all_to_all | solution.py:371
  85.6 0.8 shard_map.116
  86.3 6.4 %all-to-all-start.5 = ((bf16[16,24,384]{2,1,0:T(8,128)(2,1)}), bf16[16,24,384]{2,1,0:T(8,128)(2,1)S(1)}, u32[]{:S(2)}, u32[]{:S(2)}) async-start(bf16[16,24,384]{2,1,0:T(8,128)(2,1)} %get-tuple-element.52), calls=%async_computation.5 | async-start | bytes 589824 | tf_op jit(solution)/shard_map/all_to_all | solution.py:371
  92.8 3.0 %collective-permute-start.4 = (bf16[64,384]{1,0:T(8,128)(2,1)S(1)}, bf16[64,384]{1,0:T(8,128)(2,1)S(1)}, u32[]{:S(2)}, u32[]{:S(2)}) collective-permute-start(bf16[64,384]{1,0:T(8,128)(2,1)S(1)} %fusion.2), channel_id=1, source_target_pairs={{0,3},{1,2},{2,1},{3,0},{4,7},{5,6},{6,5},{7,4},{8,11},{9,10},{10,... | collective-permute-start | bytes 147464 | tf_op jit(solution)/shard_map/ppermute | solution.py:379
  95.8 0.9 shard_map.117
  96.7 3.1 %collective-permute-done.4 = bf16[64,384]{1,0:T(8,128)(2,1)S(1)} collective-permute-done((bf16[64,384]{1,0:T(8,128)(2,1)S(1)}, bf16[64,384]{1,0:T(8,128)(2,1)S(1)}, u32[]{:S(2)}, u32[]{:S(2)}) %collective-permute-start.4) | collective-permute-done | bytes 49184 | tf_op jit(solution)/shard_map/ppermute | solution.py:379
  99.8 0.6 fusion.1
  100.4 0.1 all-to-all-done.5.spread_in
  100.5 0.9 shard_map.118
  (2 shorter events, 0.0 us)
Async XLA Ops:
  17.9 6.8 %copy-start.4 = (s32[3]{0:T(128)S(1)}, s32[3]{0:T(128)}, u32[]{:S(2)}) copy-start(s32[3]{0:T(128)} %offsets_far.1) | copy-start | bytes 40
  18.6 6.1 %copy-start.2 = (bf16[64,3,128]{2,0,1:T(8,128)(2,1)S(1)}, bf16[64,3,128]{2,0,1:T(8,128)(2,1)}, u32[]{:S(2)}) copy-start(bf16[64,3,128]{2,0,1:T(8,128)(2,1)} %param.7) | copy-start | bytes 147460
  18.6 6.1 %copy-start.3 = (bf16[64,384]{1,0:T(8,128)(2,1)S(1)}, bf16[64,384]{1,0:T(8,128)(2,1)}, u32[]{:S(2)}) copy-start(bf16[64,384]{1,0:T(8,128)(2,1)} %grad.1) | copy-start | bytes 147460
  18.6 30.5 %copy-start = (f32[832,128]{1,0:T(8,128)S(1)}, f32[832,128]{1,0:T(8,128)}, u32[]{:S(2)}) copy-start(f32[832,128]{1,0:T(8,128)} %constant.17.clone.bias) | copy-start | bytes 1277956
  18.6 11.8 %all-to-all-start.2 = ((bf16[8,32,384]{2,1,0:T(8,128)(2,1)}), bf16[8,32,384]{2,1,0:T(8,128)(2,1)S(1)}, u32[]{:S(2)}, u32[]{:S(2)}) async-start(bf16[8,32,384]{2,1,0:T(8,128)(2,1)} %get-tuple-element.36), calls=%async_computation.2 | async-start | bytes 393216 | tf_op jit(solution)/shard_map/all_to_all | solution.py:371
  24.7 24.5 %copy-start.1 = (bf16[192,768]{1,0:T(8,128)(2,1)S(1)}, bf16[192,768]{1,0:T(8,128)(2,1)}, u32[]{:S(2)}) copy-start(bf16[192,768]{1,0:T(8,128)(2,1)} %weight.1) | copy-start | bytes 884740
  30.5 17.3 %all-to-all-start = ((bf16[4,64,384]{2,1,0:T(8,128)(2,1)}), bf16[4,64,384]{2,1,0:T(8,128)(2,1)S(1)}, u32[]{:S(2)}, u32[]{:S(2)}) async-start(bf16[4,64,384]{2,1,0:T(8,128)(2,1)} %get-tuple-element.33), calls=%async_computation | async-start | bytes 393216 | tf_op jit(solution)/shard_map/all_to_all | solution.py:396
  39.6 8.2 %collective-permute-start = (bf16[288,384]{1,0:T(8,128)(2,1)S(1)}, bf16[288,384]{1,0:T(8,128)(2,1)S(1)}, u32[]{:S(2)}, u32[]{:S(2)}) collective-permute-start(bf16[288,384]{1,0:T(8,128)(2,1)S(1)} %get-tuple-element.37), channel_id=1, source_target_pairs={{0,4},{4,0},{8,12},{12,8},{16,20},{20,16},{24,28},{28,24},{32,36},... | collective-permute-start | bytes 663560 | tf_op jit(solution)/shard_map/ppermute | solution.py:375
  45.8 3.3 %collective-permute-start.1 = (bf16[8,32,384]{2,1,0:T(8,128)(2,1)S(1)}, bf16[8,32,384]{2,1,0:T(8,128)(2,1)S(1)}, u32[]{:S(2)}, u32[]{:S(2)}) collective-permute-start(bf16[8,32,384]{2,1,0:T(8,128)(2,1)S(1)} %all-to-all-done.2.far_in), channel_id=1, source_target_pairs={{0,4},{4,0},{8,12},{12,8},{16,20},{20,16},{24,28},{28,24},{32,36},... | collective-permute-start | bytes 589832 | tf_op jit(solution)/shard_map/ppermute | solution.py:375
  52.8 6.8 %collective-permute-start.2 = (bf16[576,384]{1,0:T(8,128)(2,1)S(1)}, bf16[576,384]{1,0:T(8,128)(2,1)S(1)}, u32[]{:S(2)}, u32[]{:S(2)}) collective-permute-start(bf16[576,384]{1,0:T(8,128)(2,1)S(1)} %get-tuple-element.39), channel_id=1, source_target_pairs={{0,4},{4,0},{8,12},{12,8},{16,20},{20,16},{24,28},{28,24},{32,36},... | collective-permute-start | bytes 1327112 | tf_op jit(solution)/shard_map/ppermute | solution.py:375
  70.8 14.8 %all-to-all-start.4 = ((bf16[8,56,384]{2,1,0:T(8,128)(2,1)}), bf16[8,56,384]{2,1,0:T(8,128)(2,1)S(1)}, u32[]{:S(2)}, u32[]{:S(2)}) async-start(bf16[8,56,384]{2,1,0:T(8,128)(2,1)} %shard_map.115), calls=%async_computation.4 | async-start | bytes 688128 | tf_op jit(solution)/shard_map/all_to_all | solution.py:371
  74.2 7.7 %collective-permute-start.3 = (bf16[2,64,384]{2,1,0:T(8,128)(2,1)S(1)}, bf16[2,64,384]{2,1,0:T(8,128)(2,1)S(1)}, u32[]{:S(2)}, u32[]{:S(2)}) collective-permute-start(bf16[2,64,384]{2,1,0:T(8,128)(2,1)S(1)} %get-tuple-element.44), channel_id=1, source_target_pairs={{0,1},{1,0},{2,3},{3,2},{4,5},{5,4},{6,7},{7,6},{8,9},{9,8},{10,11... | collective-permute-start | bytes 294920 | tf_op jit(solution)/shard_map/ppermute | solution.py:379
  86.3 14.2 %all-to-all-start.5 = ((bf16[16,24,384]{2,1,0:T(8,128)(2,1)}), bf16[16,24,384]{2,1,0:T(8,128)(2,1)S(1)}, u32[]{:S(2)}, u32[]{:S(2)}) async-start(bf16[16,24,384]{2,1,0:T(8,128)(2,1)} %get-tuple-element.52), calls=%async_computation.5 | async-start | bytes 589824 | tf_op jit(solution)/shard_map/all_to_all | solution.py:371
  92.8 7.0 %collective-permute-start.4 = (bf16[64,384]{1,0:T(8,128)(2,1)S(1)}, bf16[64,384]{1,0:T(8,128)(2,1)S(1)}, u32[]{:S(2)}, u32[]{:S(2)}) collective-permute-start(bf16[64,384]{1,0:T(8,128)(2,1)S(1)} %fusion.2), channel_id=1, source_target_pairs={{0,3},{1,2},{2,1},{3,0},{4,7},{5,6},{6,5},{7,4},{8,11},{9,10},{10,... | collective-permute-start | bytes 147464 | tf_op jit(solution)/shard_map/ppermute | solution.py:379

commit v7 on v6

--- a/solution.py
+++ b/solution.py
@@ -90,6 +90,11 @@
     return jnp.where(match, 1.0, 0.0).astype(BF16)
 
 
+def here():
+    index = lax.axis_index("seq")
+    return index >> 4, (index >> 1) & 7, index & 1, lax.axis_index("head")
+
+
 def order_from(offset, row_axis):
     row = lax.broadcasted_iota(jnp.int32, (ROWS, ROWS), row_axis)
     token = token_of(lax.broadcasted_iota(jnp.int32, (ROWS, ROWS), 1 - row_axis))
@@ -140,7 +145,7 @@
     return one_hot(far_place(row, far) == lax.broadcasted_iota(jnp.int32, shape, 1 - row_axis))
 
 
-def table_kernel(rank, offsets, queries, grad, to_order, to_token, query, choice, choice_back, grads_out):
+def table_kernel(offsets, queries, grad, to_order, to_token, query, choice, choice_back, grads_out):
     for slot in range(4):
         grads_out[slot] = grad[...]
     for head in range(LOCAL):
@@ -149,30 +154,29 @@
         to_order[head] = order
         to_token[head] = order_from(offsets[head], 1)
         query[head] = dot(order, beside(pairs, jnp.zeros_like(pairs))).astype(BF16)
-    choice[...] = far_choice(rank[0], 0)
-    choice_back[...] = far_choice(rank[0], 1)
-
-
-def far_kernel(ordered, line_in, far_out, partner_out):
-    for slot in range(LINE):
-        partner_out[slot * NEAR : (slot + 1) * NEAR, :] = line_in[slot]
-    partner_out[SLOTS:, :] = ordered[NEAR : 2 * NEAR, :]
+    far = here()[0]
+    choice[...] = far_choice(far, 0)
+    choice_back[...] = far_choice(far, 1)
+
+
+def far_kernel(ordered, line_in, far_out):
     low = lax.broadcasted_iota(jnp.int32, (8, LANES), 0) < EACH
     for pair in range(LINE // 2):
         first, second = (line_in[2 * pair + slot, 0:16, :].astype(F32)[:8] for slot in range(2))
         rows = jnp.where(low, first, pltpu.roll(second, EACH, 0)).astype(BF16)
         for slot in range(FAR):
             far_out[slot, pair * 8 : (pair + 1) * 8, :] = rows
+    far_out[here()[0]] = ordered[NEAR : 2 * NEAR, :]
 
 
 def main_kernel(
-    rank, to_order, to_token, query, choice, weight, grads, ordered, line_in, far_in, other_in, other_far_in, bias,
+    to_order, to_token, query, choice, weight, grads, ordered, line_in, far_in, other_in, other_far_in, bias,
     output_keep, output_send, query_grad, send, keep_line, keep_far, keep_own, keep_weight,
     held, full_grad, attn, weight_term, parts,
 ):
-    line, core, mine = rank[1], rank[2], rank[3]
+    far, line, core, mine = here()
     held[0:ROWS, :] = ordered[...]
-    held[PARTNER_AT:OTHER_AT, :] = other_in[SLOTS:, :]
+    held[PARTNER_AT:OTHER_AT, :] = other_far_in[far]
     held[FAR_AT:PARTNER_AT, :] = dot(choice[...], far_in[...].reshape(FAR * NEAR, LANES)).astype(BF16)
     held[OTHER_FAR_AT:, :] = dot(choice[...], other_far_in[...].reshape(FAR * NEAR, LANES)).astype(BF16)
     for step in range(LINE):
@@ -181,7 +185,7 @@
             at = LINE_AT + (step - 1) * NEAR
             held[at : at + NEAR, :] = line_in[slot]
         at = OTHER_AT + step * NEAR
-        held[at : at + NEAR, :] = other_in[pl.ds(pl.multiple_of(slot * NEAR, NEAR), NEAR), :]
+        held[at : at + NEAR, :] = other_in[slot]
     for parity in range(2):
         for half in range(2):
             place = (slice(parity * SIZE, (parity + 1) * SIZE), slice(half * HALF, (half + 1) * HALF))
@@ -285,7 +289,8 @@
         value_grad[head] = jnp.where(low, pltpu.roll(even, SIZE, 1), odd).astype(BF16)
 
 
-def weight_kernel(spread_in, weight_grad):
+def weight_kernel(spread_in, output_sum, second, weight_grad, output):
+    output[...] = (output_sum[0] + second[...].astype(F32)).astype(BF16)
     for far in range(FAR):
         half, row = far // 4, far % 4 * PART
         for core in range(CORE):
@@ -313,17 +318,17 @@
     return call(start_kernel, outs, tuple(args), 0, scratch, pltpu.HBM)
 
 
-def tables(rank, offsets, queries, grad):
+def tables(offsets, queries, grad):
     square = (LOCAL, ROWS, ROWS)
     outs = [(square, BF16)] * 3 + [((PICKED, FAR * NEAR), BF16), ((FAR * NEAR, PICKED), BF16)]
-    return call(table_kernel, outs + [((4, SIZE, HALF), BF16)], (rank, offsets, queries, grad), 2)
+    return call(table_kernel, outs + [((4, SIZE, HALF), BF16)], (offsets, queries, grad), 1)
 
 
 def far_pieces(ordered, line_in):
-    return call(far_kernel, [((FAR, NEAR, LANES), BF16), ((SLOTS + NEAR, LANES), BF16)], (ordered, line_in), 0)
-
-
-def attention(rank, *arrays):
+    return call(far_kernel, [((FAR, NEAR, LANES), BF16)], (ordered, line_in), 0)[0]
+
+
+def attention(*arrays):
     outs = [
         ((2, SIZE, HALF), F32),
         ((2, SIZE, HALF), BF16),
@@ -341,7 +346,7 @@
         pltpu.VMEM((SHARE, WIDTH), F32),
         pltpu.VMEM((4, SIZE, HALF), F32),
     ]
-    return call(main_kernel, outs, (rank,) + arrays + (jnp.asarray(shared_levels()),), 1, scratch)
+    return call(main_kernel, outs, arrays + (jnp.asarray(shared_levels()),), 0, scratch)
 
 
 def far_return(choice_back, received, keep_far, keep_weight):
@@ -363,8 +368,8 @@
     return call(finish_kernel, outs, (to_token, keep_own, received, near_sum), 0, [pltpu.VMEM((ROWS, LANES), F32)])
 
 
-def weight_rows(spread_in):
-    return call(weight_kernel, [((SHARE, WIDTH), F32)], (spread_in,), 0)[0]
+def weight_rows(spread_in, output_sum, second):
+    return call(weight_kernel, [((SHARE, WIDTH), F32), ((SIZE, HALF), BF16)], (spread_in, output_sum, second), 0)
 
 
 def trade(pieces, groups):
@@ -380,22 +385,20 @@
 
 
 def shards(queries, keys, values, out_weight, offsets, out_grad):
-    index = lax.axis_index("seq")
-    rank = jnp.stack([index >> 4, index >> 1 & 7, index & 1, lax.axis_index("head")]).astype(jnp.int32)
     far_groups = [[far * 16 + low for far in range(FAR)] for low in range(16)]
     line_groups = [[far * 16 + line * 2 + core for line in range(LINE)] for far in range(FAR) for core in range(CORE)]
     side_groups = [[far * 16 + line * 2 + core for far in range(FAR) for core in range(CORE)] for line in range(LINE)]
     queries, keys, values = (array.transpose(1, 0, 2) for array in (queries, keys, values))
     ordered, line_out = start(offsets, keys, values)
-    to_order, to_token, query, choice, choice_back, grads_out = tables(rank, offsets, queries, out_grad)
+    to_order, to_token, query, choice, choice_back, grads_out = tables(offsets, queries, out_grad)
     line_in = trade(line_out, line_groups)
-    far_out, partner_out = far_pieces(ordered, line_in)
-    other_in = swap_cores(partner_out)
+    far_out = far_pieces(ordered, line_in)
+    other_in = swap_cores(line_in)
     far_in = trade(far_out, far_groups)
     other_far_in = swap_cores(far_in)
     grads = lax.all_to_all(grads_out, "head", 0, 0, tiled=True)
     output_keep, output_send, query_grad, send, keep_line, keep_far, keep_own, keep_weight = attention(
-        rank, to_order, to_token, query, choice, out_weight, grads, ordered, line_in, far_in, other_in, other_far_in
+        to_order, to_token, query, choice, out_weight, grads, ordered, line_in, far_in, other_in, other_far_in
     )
     first = swap_heads(output_send, 1)
     received = swap_cores(send)
@@ -407,8 +410,7 @@
     near_sum, spread_out = spread_pieces(line_back)
     spread_in = trade(spread_out, side_groups)
     key_grad, value_grad = finish(to_token, keep_own, received, near_sum)
-    output = (output_sum[0] + second.astype(F32)).astype(BF16)
-    weight_grad = weight_rows(spread_in)
+    weight_grad, output = weight_rows(spread_in, output_sum, second)
     query_grad, key_grad, value_grad = (grad.transpose(1, 0, 2) for grad in (query_grad, key_grad, value_grad))
     return (output, query_grad, key_grad, value_grad, weight_grad)
 

time: 102 us -> 102 us (level)
  transfers between devices with their start and end apart: 9 -> 9, of which waited for: 7 -> 7; matrix products, arithmetic and copies ran while one was open for 1% -> 0% of each run, Pallas kernels for 2% -> 2%
where the time goes in v7:
time: 102 us; the launch traced here: 101 us
  starting transfers between devices  44.7 us (44%)
  blocking collectives  26.3 us (26%)
  waiting for transfers between devices  19.2 us (19%)
  Pallas kernels  9.84 us (10%)
    all_to_all x2, blocking collectives, trade(): lax.all_to_all(pieces, 'seq', 0, 0, axis_index_groups=groups, tiled=True)  26.3 us
    all_to_all x3, starting transfers between devices, trade(): lax.all_to_all(pieces, 'seq', 0, 0, axis_index_groups=groups, tiled=True)  15.9 us
    ppermute x3, starting transfers between devices, swap_cores(): lax.ppermute(block, 'seq', [(i, i ^ 1) for i in range(FAR * LINE * CORE)])  13.6 us
    pallas_call x9, Pallas kernels, call(): pl.pallas_call(kernel, out_shape=[jax.ShapeDtypeStruct(shape, dtype) for...  9.84 us
    all_to_all x1, starting transfers between devices, shards(): grads = lax.all_to_all(grads_out, 'head', 0, 0, tiled=True)  9.12 us
    all_to_all x3, waiting for transfers between devices, trade(): lax.all_to_all(pieces, 'seq', 0, 0, axis_index_groups=groups, tiled=True)  8.77 us
    ppermute x2, waiting for transfers between devices, swap_heads(): return lax.ppermute(block, 'head', [(i, i ^ way) for i in range(4)])  7.63 us
    ppermute x2, starting transfers between devices, swap_heads(): return lax.ppermute(block, 'head', [(i, i ^ way) for i in range(4)])  6.11 us
  transfers between devices with their start and end apart: 9, of which 7 were waited for; matrix products, arithmetic and copies ran while one was open for 0% of the time, Pallas kernels for 2%

profile of v7, /device:TPU:1, one launch (start us, length us, event | category | flops | bytes accessed | tf_op | source)
XLA Modules:
  0.0 100.8 jit_solution(11665029582903725646)
XLA Ops:
  0.6 1.1 %shard_map.111 = (bf16[128,384]{1,0:T(8,128)(2,1)S(1)}, bf16[8,32,384]{2,1,0:T(8,128)(2,1)S(1)}) custom-call(s32[3]{0:T(128)} %offsets_far.1, bf16[3,64,128]{2,1,0:T(8,128)(2,1)} %bitcast.9, bf16[3,64,128]{2,1,0:T(8,128)(2,1)} %bitcast.10), custom_call_target="tpu_custom_call" | custom-call | tf_op jit(solution)/shard_map/pallas_call | solution.py:302
  1.7 16.2 %all_to_all.30.line_in = bf16[8,32,384]{2,1,0:T(8,128)(2,1)S(1)} all-to-all(bf16[8,32,384]{2,1,0:T(8,128)(2,1)S(1)} %get-tuple-element.35), channel_id=1, replica_groups={{0,8,16,24,32,40,48,56},{4,12,20,28,36,44,52,60},{64,72,80,88,96,104,11..., dimensions={0} | all-to-all | bytes 393216 | tf_op jit(solution)/shard_map/all_to_all | solution.py:376
  17.9 0.0 copy-start.2
  17.9 0.0 copy-start.3
  17.9 0.0 copy-start.4
  17.9 0.7 shard_map.112
  18.6 0.0 copy-start
  18.6 6.0 %all-to-all-start.2 = ((bf16[8,32,384]{2,1,0:T(8,128)(2,1)}), bf16[8,32,384]{2,1,0:T(8,128)(2,1)S(1)}, u32[]{:S(2)}, u32[]{:S(2)}) async-start(bf16[8,32,384]{2,1,0:T(8,128)(2,1)} %shard_map.112), calls=%async_computation.2 | async-start | bytes 393216 | tf_op jit(solution)/shard_map/all_to_all | solution.py:376
  24.7 0.0 copy-start.1
  24.7 0.0 copy-done.2
  24.7 0.0 copy-done.3
  24.7 0.0 copy-done.4
  24.7 1.4 %shard_map.110 = (bf16[3,128,128]{2,1,0:T(8,128)(2,1)S(1)}, bf16[3,128,128]{2,1,0:T(8,128)(2,1)S(1)}, bf16[3,128,128]{2,1,0:T(8,128)(2,1)S(1)}, bf16[96,256]{1,0...) custom-call(s32[3]{0:T(128)S(1)} %copy-done.4, bf16[3,64,128]{2,1,0:T(8,128)(2,1)S(1)} %bitcast.8, ...), custom_call_target="tpu_custom_call" | custom-call | tf_op jit(solution)/shard_map/pallas_call | solution.py:302
  26.1 4.4 %all-to-all-done.2.far_in = bf16[8,32,384]{2,1,0:T(8,128)(2,1)S(1)} async-done(((bf16[8,32,384]{2,1,0:T(8,128)(2,1)}), bf16[8,32,384]{2,1,0:T(8,128)(2,1)S(1)}, u32[]{:S(2)}, u32[]{:S(2)}) %all-to-all-start.2) | async-done | bytes 196640 | tf_op jit(solution)/shard_map/all_to_all | solution.py:376
  30.5 9.1 %all-to-all-start = ((bf16[4,64,384]{2,1,0:T(8,128)(2,1)}), bf16[4,64,384]{2,1,0:T(8,128)(2,1)S(1)}, u32[]{:S(2)}, u32[]{:S(2)}) async-start(bf16[4,64,384]{2,1,0:T(8,128)(2,1)} %get-tuple-element.33), calls=%async_computation | async-start | bytes 393216 | tf_op jit(solution)/shard_map/all_to_all | solution.py:399
  39.6 6.2 %collective-permute-start = (bf16[8,32,384]{2,1,0:T(8,128)(2,1)S(1)}, bf16[8,32,384]{2,1,0:T(8,128)(2,1)S(1)}, u32[]{:S(2)}, u32[]{:S(2)}) collective-permute-start(bf16[8,32,384]{2,1,0:T(8,128)(2,1)S(1)} %all_to_all.30.line_in), channel_id=1, source_target_pairs={{0,4},{4,0},{8,12},{12,8},{16,20},{20,16},{24,28},{28,24},{32,36},... | collective-permute-start | bytes 589832 | tf_op jit(solution)/shard_map/ppermute | solution.py:380
  45.8 1.9 %collective-permute-start.1 = (bf16[8,32,384]{2,1,0:T(8,128)(2,1)S(1)}, bf16[8,32,384]{2,1,0:T(8,128)(2,1)S(1)}, u32[]{:S(2)}, u32[]{:S(2)}) collective-permute-start(bf16[8,32,384]{2,1,0:T(8,128)(2,1)S(1)} %all-to-all-done.2.far_in), channel_id=1, source_target_pairs={{0,4},{4,0},{8,12},{12,8},{16,20},{20,16},{24,28},{28,24},{32,36},... | collective-permute-start | bytes 589832 | tf_op jit(solution)/shard_map/ppermute | solution.py:380
  47.8 0.0 all-to-all-done.grads
  47.8 0.0 collective-permute-done.other_in
  47.8 1.4 %collective-permute-done.1.other_far_in = bf16[8,32,384]{2,1,0:T(8,128)(2,1)S(1)} collective-permute-done((bf16[8,32,384]{2,1,0:T(8,128)(2,1)S(1)}, bf16[8,32,384]{2,1,0:T(8,128)(2,1)S(1)}, u32[]{:S(2)}, u32[]{:S(2)}) %collective-permute-start.1) | collective-permute-done | bytes 196640 | tf_op jit(solution)/shard_map/ppermute | solution.py:380
  49.2 0.0 copy-done
  49.2 0.0 copy-done.1
  49.2 3.1 %shard_map.113 = (f32[2,64,384]{2,1,0:T(8,128)S(1)}, bf16[2,64,384]{2,1,0:T(8,128)(2,1)S(1)}, bf16[3,64,128]{2,1,0:T(8,128)(2,1)}, bf16[576,384]{1,0:T(8,128)(2,...) custom-call(bf16[3,128,128]{2,1,0:T(8,128)(2,1)S(1)} %get-tuple-elem, ...), custom_call_target="tpu_custom_call" | custom-call | tf_op jit(solution)/shard_map/pallas_call | solution.py:302
  52.2 5.4 %collective-permute-start.2 = (bf16[576,384]{1,0:T(8,128)(2,1)S(1)}, bf16[576,384]{1,0:T(8,128)(2,1)S(1)}, u32[]{:S(2)}, u32[]{:S(2)}) collective-permute-start(bf16[576,384]{1,0:T(8,128)(2,1)S(1)} %get-tuple-element.36), channel_id=1, source_target_pairs={{0,4},{4,0},{8,12},{12,8},{16,20},{20,16},{24,28},{28,24},{32,36},... | collective-permute-start | bytes 1327112 | tf_op jit(solution)/shard_map/ppermute | solution.py:380
  57.7 1.4 %collective-permute-done.2.received = bf16[576,384]{1,0:T(8,128)(2,1)S(1)} collective-permute-done((bf16[576,384]{1,0:T(8,128)(2,1)S(1)}, bf16[576,384]{1,0:T(8,128)(2,1)S(1)}, u32[]{:S(2)}, u32[]{:S(2)}) %collective-permute-start.2) | collective-permute-done | bytes 442400 | tf_op jit(solution)/shard_map/ppermute | solution.py:380
  59.1 0.2 shard_map.114
  59.3 10.1 %all_to_all.31.far_in = bf16[8,56,384]{2,1,0:T(8,128)(2,1)S(1)} all-to-all(bf16[8,56,384]{2,1,0:T(8,128)(2,1)S(1)} %shard_map.114), channel_id=1, replica_groups={{0,64,128,192,256,320,384,448},{4,68,132,196,260,324,388,452},{8,72,136..., dimensions={0} | all-to-all | bytes 688128 | tf_op jit(solution)/shard_map/all_to_all | solution.py:376
  69.4 0.8 shard_map.115
  70.2 3.4 %all-to-all-start.4 = ((bf16[8,56,384]{2,1,0:T(8,128)(2,1)}), bf16[8,56,384]{2,1,0:T(8,128)(2,1)S(1)}, u32[]{:S(2)}, u32[]{:S(2)}) async-start(bf16[8,56,384]{2,1,0:T(8,128)(2,1)} %shard_map.115), calls=%async_computation.4 | async-start | bytes 688128 | tf_op jit(solution)/shard_map/all_to_all | solution.py:376
  73.6 3.2 %collective-permute-start.3 = (bf16[2,64,384]{2,1,0:T(8,128)(2,1)S(1)}, bf16[2,64,384]{2,1,0:T(8,128)(2,1)S(1)}, u32[]{:S(2)}, u32[]{:S(2)}) collective-permute-start(bf16[2,64,384]{2,1,0:T(8,128)(2,1)S(1)} %get-tuple-element.41), channel_id=1, source_target_pairs={{0,1},{1,0},{2,3},{3,2},{4,5},{5,4},{6,7},{7,6},{8,9},{9,8},{10,11... | collective-permute-start | bytes 294920 | tf_op jit(solution)/shard_map/ppermute | solution.py:384
  76.8 4.5 %collective-permute-done.3 = bf16[2,64,384]{2,1,0:T(8,128)(2,1)S(1)} collective-permute-done((bf16[2,64,384]{2,1,0:T(8,128)(2,1)S(1)}, bf16[2,64,384]{2,1,0:T(8,128)(2,1)S(1)}, u32[]{:S(2)}, u32[]{:S(2)}) %collective-permute-start.3) | collective-permute-done | bytes 98336 | tf_op jit(solution)/shard_map/ppermute | solution.py:384
  81.3 3.7 %all-to-all-done.4.line_in = bf16[8,56,384]{2,1,0:T(8,128)(2,1)S(1)} async-done(((bf16[8,56,384]{2,1,0:T(8,128)(2,1)}), bf16[8,56,384]{2,1,0:T(8,128)(2,1)S(1)}, u32[]{:S(2)}, u32[]{:S(2)}) %all-to-all-start.4) | async-done | bytes 344096 | tf_op jit(solution)/shard_map/all_to_all | solution.py:376
  85.0 0.8 shard_map.116
  85.8 6.4 %all-to-all-start.5 = ((bf16[16,24,384]{2,1,0:T(8,128)(2,1)}), bf16[16,24,384]{2,1,0:T(8,128)(2,1)S(1)}, u32[]{:S(2)}, u32[]{:S(2)}) async-start(bf16[16,24,384]{2,1,0:T(8,128)(2,1)} %get-tuple-element.43), calls=%async_computation.5 | async-start | bytes 589824 | tf_op jit(solution)/shard_map/all_to_all | solution.py:376
  92.3 3.0 %collective-permute-start.4 = (bf16[64,384]{1,0:T(8,128)(2,1)S(1)}, bf16[64,384]{1,0:T(8,128)(2,1)S(1)}, u32[]{:S(2)}, u32[]{:S(2)}) collective-permute-start(bf16[64,384]{1,0:T(8,128)(2,1)S(1)} %fusion), channel_id=1, source_target_pairs={{0,3},{1,2},{2,1},{3,0},{4,7},{5,6},{6,5},{7,4},{8,11},{9,10},{10,... | collective-permute-start | bytes 147464 | tf_op jit(solution)/shard_map/ppermute | solution.py:384
  95.2 0.9 shard_map.118
  96.1 3.1 %collective-permute-done.4.second = bf16[64,384]{1,0:T(8,128)(2,1)S(1)} collective-permute-done((bf16[64,384]{1,0:T(8,128)(2,1)S(1)}, bf16[64,384]{1,0:T(8,128)(2,1)S(1)}, u32[]{:S(2)}, u32[]{:S(2)}) %collective-permute-start.4) | collective-permute-done | bytes 49184 | tf_op jit(solution)/shard_map/ppermute | solution.py:384
  99.2 0.7 all-to-all-done.5.spread_in
  99.9 0.9 shard_map.117
  (2 shorter events, 0.0 us)
Async XLA Ops:
  17.9 6.7 %copy-start.2 = (bf16[64,3,128]{2,0,1:T(8,128)(2,1)S(1)}, bf16[64,3,128]{2,0,1:T(8,128)(2,1)}, u32[]{:S(2)}) copy-start(bf16[64,3,128]{2,0,1:T(8,128)(2,1)} %param.7) | copy-start | bytes 147460
  17.9 6.8 %copy-start.3 = (bf16[64,384]{1,0:T(8,128)(2,1)S(1)}, bf16[64,384]{1,0:T(8,128)(2,1)}, u32[]{:S(2)}) copy-start(bf16[64,384]{1,0:T(8,128)(2,1)} %grad.1) | copy-start | bytes 147460
  17.9 6.8 %copy-start.4 = (s32[3]{0:T(128)S(1)}, s32[3]{0:T(128)}, u32[]{:S(2)}) copy-start(s32[3]{0:T(128)} %offsets_far.1) | copy-start | bytes 40
  18.6 30.5 %copy-start = (f32[832,128]{1,0:T(8,128)S(1)}, f32[832,128]{1,0:T(8,128)}, u32[]{:S(2)}) copy-start(f32[832,128]{1,0:T(8,128)} %constant.2.clone.bias) | copy-start | bytes 1277956
  18.6 11.8 %all-to-all-start.2 = ((bf16[8,32,384]{2,1,0:T(8,128)(2,1)}), bf16[8,32,384]{2,1,0:T(8,128)(2,1)S(1)}, u32[]{:S(2)}, u32[]{:S(2)}) async-start(bf16[8,32,384]{2,1,0:T(8,128)(2,1)} %shard_map.112), calls=%async_computation.2 | async-start | bytes 393216 | tf_op jit(solution)/shard_map/all_to_all | solution.py:376
  24.7 24.5 %copy-start.1 = (bf16[192,768]{1,0:T(8,128)(2,1)S(1)}, bf16[192,768]{1,0:T(8,128)(2,1)}, u32[]{:S(2)}) copy-start(bf16[192,768]{1,0:T(8,128)(2,1)} %weight.1) | copy-start | bytes 884740
  30.5 17.3 %all-to-all-start = ((bf16[4,64,384]{2,1,0:T(8,128)(2,1)}), bf16[4,64,384]{2,1,0:T(8,128)(2,1)S(1)}, u32[]{:S(2)}, u32[]{:S(2)}) async-start(bf16[4,64,384]{2,1,0:T(8,128)(2,1)} %get-tuple-element.33), calls=%async_computation | async-start | bytes 393216 | tf_op jit(solution)/shard_map/all_to_all | solution.py:399
  39.6 8.2 %collective-permute-start = (bf16[8,32,384]{2,1,0:T(8,128)(2,1)S(1)}, bf16[8,32,384]{2,1,0:T(8,128)(2,1)S(1)}, u32[]{:S(2)}, u32[]{:S(2)}) collective-permute-start(bf16[8,32,384]{2,1,0:T(8,128)(2,1)S(1)} %all_to_all.30.line_in), channel_id=1, source_target_pairs={{0,4},{4,0},{8,12},{12,8},{16,20},{20,16},{24,28},{28,24},{32,36},... | collective-permute-start | bytes 589832 | tf_op jit(solution)/shard_map/ppermute | solution.py:380
  45.8 3.3 %collective-permute-start.1 = (bf16[8,32,384]{2,1,0:T(8,128)(2,1)S(1)}, bf16[8,32,384]{2,1,0:T(8,128)(2,1)S(1)}, u32[]{:S(2)}, u32[]{:S(2)}) collective-permute-start(bf16[8,32,384]{2,1,0:T(8,128)(2,1)S(1)} %all-to-all-done.2.far_in), channel_id=1, source_target_pairs={{0,4},{4,0},{8,12},{12,8},{16,20},{20,16},{24,28},{28,24},{32,36},... | collective-permute-start | bytes 589832 | tf_op jit(solution)/shard_map/ppermute | solution.py:380
  52.2 6.8 %collective-permute-start.2 = (bf16[576,384]{1,0:T(8,128)(2,1)S(1)}, bf16[576,384]{1,0:T(8,128)(2,1)S(1)}, u32[]{:S(2)}, u32[]{:S(2)}) collective-permute-start(bf16[576,384]{1,0:T(8,128)(2,1)S(1)} %get-tuple-element.36), channel_id=1, source_target_pairs={{0,4},{4,0},{8,12},{12,8},{16,20},{20,16},{24,28},{28,24},{32,36},... | collective-permute-start | bytes 1327112 | tf_op jit(solution)/shard_map/ppermute | solution.py:380
  70.2 14.8 %all-to-all-start.4 = ((bf16[8,56,384]{2,1,0:T(8,128)(2,1)}), bf16[8,56,384]{2,1,0:T(8,128)(2,1)S(1)}, u32[]{:S(2)}, u32[]{:S(2)}) async-start(bf16[8,56,384]{2,1,0:T(8,128)(2,1)} %shard_map.115), calls=%async_computation.4 | async-start | bytes 688128 | tf_op jit(solution)/shard_map/all_to_all | solution.py:376
  73.6 7.7 %collective-permute-start.3 = (bf16[2,64,384]{2,1,0:T(8,128)(2,1)S(1)}, bf16[2,64,384]{2,1,0:T(8,128)(2,1)S(1)}, u32[]{:S(2)}, u32[]{:S(2)}) collective-permute-start(bf16[2,64,384]{2,1,0:T(8,128)(2,1)S(1)} %get-tuple-element.41), channel_id=1, source_target_pairs={{0,1},{1,0},{2,3},{3,2},{4,5},{5,4},{6,7},{7,6},{8,9},{9,8},{10,11... | collective-permute-start | bytes 294920 | tf_op jit(solution)/shard_map/ppermute | solution.py:384
  85.8 14.2 %all-to-all-start.5 = ((bf16[16,24,384]{2,1,0:T(8,128)(2,1)}), bf16[16,24,384]{2,1,0:T(8,128)(2,1)S(1)}, u32[]{:S(2)}, u32[]{:S(2)}) async-start(bf16[16,24,384]{2,1,0:T(8,128)(2,1)} %get-tuple-element.43), calls=%async_computation.5 | async-start | bytes 589824 | tf_op jit(solution)/shard_map/all_to_all | solution.py:376
  92.3 7.0 %collective-permute-start.4 = (bf16[64,384]{1,0:T(8,128)(2,1)S(1)}, bf16[64,384]{1,0:T(8,128)(2,1)S(1)}, u32[]{:S(2)}, u32[]{:S(2)}) collective-permute-start(bf16[64,384]{1,0:T(8,128)(2,1)S(1)} %fusion), channel_id=1, source_target_pairs={{0,3},{1,2},{2,1},{3,0},{4,7},{5,6},{6,5},{7,4},{8,11},{9,10},{10,... | collective-permute-start | bytes 147464 | tf_op jit(solution)/shard_map/ppermute | solution.py:384

commit v8 on v7

--- a/solution.py
+++ b/solution.py
@@ -9,6 +9,8 @@
 from jax.sharding import PartitionSpec as P
 
 FAR, LINE, CORE = 8, 8, 2
+FAR_FIRST, LINE_FIRST, HEAD_FIRST = 3, 7, 3
+FAR_BACK, LINE_BACK, SPREAD_FIRST, SPREAD_CORE = 3, 7, 3, 1
 ROWS = 128
 LOCAL = 3
 SIZE = 64
@@ -92,7 +94,7 @@
 
 def here():
     index = lax.axis_index("seq")
-    return index >> 4, (index >> 1) & 7, index & 1, lax.axis_index("head")
+    return (index >> 4) ^ FAR_FIRST, ((index >> 1) & 7) ^ LINE_FIRST, index & 1, lax.axis_index("head")
 
 
 def order_from(offset, row_axis):
@@ -153,10 +155,10 @@
         pairs = queries[head].astype(F32)
         to_order[head] = order
         to_token[head] = order_from(offsets[head], 1)
-        query[head] = dot(order, beside(pairs, jnp.zeros_like(pairs))).astype(BF16)
+        query[head] = (dot(order, beside(pairs, jnp.zeros_like(pairs))) * SCALE).astype(BF16)
     far = here()[0]
     choice[...] = far_choice(far, 0)
-    choice_back[...] = far_choice(far, 1)
+    choice_back[...] = far_choice(far ^ FAR_FIRST ^ FAR_BACK, 1)
 
 
 def far_kernel(ordered, line_in, far_out):
@@ -189,7 +191,7 @@
     for parity in range(2):
         for half in range(2):
             place = (slice(parity * SIZE, (parity + 1) * SIZE), slice(half * HALF, (half + 1) * HALF))
-            full_grad[place] = grads[2 * parity + half]
+            full_grad[place] = grads[HEAD_FIRST ^ (2 * parity + half)]
     heads = range(LOCAL)
     lanes = [pl.ds(head * 2 * SIZE, 2 * SIZE) for head in heads]
     grad = dot(full_grad[...], weight[...], NT).astype(BF16)
@@ -197,18 +199,19 @@
     grad = [jnp.concatenate([zeros, grad[:, head * SIZE : (head + 1) * SIZE]], axis=1) for head in heads]
     grad = [dot(to_order[head], grad[head]).astype(BF16) for head in heads]
     blocks = [jnp.concatenate([query[head], grad[head]], axis=0) for head in heads]
-    products = [dot(held[:, lanes[head]], blocks[head], NT) for head in heads]
-    scores = [products[head][:, :ROWS] * SCALE + bias[...] for head in heads]
+    sides = [held[:, lanes[head]].T for head in heads]
+    scores = [dot(held[:, lanes[head]], query[head], NT) + bias[...] for head in heads]
     top = [jnp.max(scores[head], axis=0, keepdims=True) for head in heads]
     expd = [jnp.exp(scores[head] - top[head]) for head in heads]
     share = [1.0 / jnp.sum(expd[head], axis=0, keepdims=True) for head in heads]
     probs = [expd[head] * share[head] for head in heads]
     rounded = [probs[head].astype(BF16) for head in heads]
-    attn_head = [dot(held[:, lanes[head]], rounded[head], TN)[SIZE:, :].astype(BF16) for head in heads]
+    attn_head = [dot(sides[head][SIZE:], rounded[head]).astype(BF16) for head in heads]
     grad_side = [grad[head].astype(F32).T[SIZE:, :] for head in heads]
     delta = [jnp.sum(grad_side[head] * attn_head[head].astype(F32), axis=0, keepdims=True) for head in heads]
-    dscore = [(probs[head] * (products[head][:, ROWS:] - delta[head]) * SCALE).astype(BF16) for head in heads]
-    dquery = [dot(held[:, lanes[head]], dscore[head], TN)[:SIZE, :].astype(BF16) for head in heads]
+    dprob = [dot(held[:, lanes[head]], grad[head], NT) for head in heads]
+    dscore = [(probs[head] * (dprob[head] - delta[head])).astype(BF16) for head in heads]
+    dquery = [(dot(sides[head][:SIZE], dscore[head]) * SCALE).astype(BF16) for head in heads]
     dboth = [dot(jnp.concatenate([dscore[head], rounded[head]], axis=1), blocks[head]) for head in heads]
     for head in heads:
         attn[:, head * SIZE : (head + 1) * SIZE] = dot(to_token[head], attn_head[head], NT).astype(BF16)
@@ -262,11 +265,14 @@
         rows = keep_line[slot] + received[slot * NEAR : (slot + 1) * NEAR, :].astype(F32)
         both = total[slot // 2 * 8 : slot // 2 * 8 + 8]
         first = jnp.where(low, pltpu.roll(both, EACH, 0) if slot % 2 else both, 0.0)
-        line_out[slot, 0:NEAR, :] = jnp.concatenate([rows[:8] + first, rows[8:]], axis=0).astype(BF16)
-        line_out[slot, NEAR:, :] = total[NEAR:].astype(BF16)
-
-
-def spread_kernel(line_in, near_sum, spread_out):
+        back = slot ^ LINE_FIRST ^ LINE_BACK
+        line_out[back, 0:NEAR, :] = jnp.concatenate([rows[:8] + first, rows[8:]], axis=0).astype(BF16)
+        line_out[back, NEAR:, :] = total[NEAR:].astype(BF16)
+
+
+def spread_kernel(line_in, output_keep, first, near_sum, spread_out, output_sum, second_out):
+    output_sum[...] = output_keep[0] + first[0].astype(F32)
+    second_out[...] = (output_keep[1] + first[1].astype(F32)).astype(BF16)
     total = line_in[0].astype(F32)
     for slot in range(1, LINE):
         total = total + line_in[slot].astype(F32)
@@ -290,12 +296,13 @@
 
 
 def weight_kernel(spread_in, output_sum, second, weight_grad, output):
-    output[...] = (output_sum[0] + second[...].astype(F32)).astype(BF16)
-    for far in range(FAR):
-        half, row = far // 4, far % 4 * PART
+    output[...] = (output_sum[...] + second[...].astype(F32)).astype(BF16)
+    for share in range(FAR):
+        half, row = share // 4, share % 4 * PART
         for core in range(CORE):
             at = core * SHARE // 2 + row
-            weight_grad[at : at + PART, half * HALF : (half + 1) * HALF] = spread_in[CORE * far + core].astype(F32)
+            slot = CORE * (share ^ FAR_BACK ^ SPREAD_FIRST) + (core ^ SPREAD_CORE)
+            weight_grad[at : at + PART, half * HALF : (half + 1) * HALF] = spread_in[slot].astype(F32)
 
 
 def call(kernel, outs, args, scalars, scratch=(), space=pltpu.VMEM):
@@ -358,9 +365,9 @@
     return call(line_return_kernel, [((LINE, NEAR + PART, LANES), BF16)], (received, keep_line, far_in), 0)[0]
 
 
-def spread_pieces(line_in):
-    outs = [((NEAR, LANES), F32), ((FAR * CORE, PART, LANES), BF16)]
-    return call(spread_kernel, outs, (line_in,), 0)
+def spread_pieces(line_in, output_keep, first):
+    outs = [((NEAR, LANES), F32), ((FAR * CORE, PART, LANES), BF16), ((SIZE, HALF), F32), ((SIZE, HALF), BF16)]
+    return call(spread_kernel, outs, (line_in, output_keep, first), 0)
 
 
 def finish(to_token, keep_own, received, near_sum):
@@ -385,9 +392,18 @@
 
 
 def shards(queries, keys, values, out_weight, offsets, out_grad):
-    far_groups = [[far * 16 + low for far in range(FAR)] for low in range(16)]
-    line_groups = [[far * 16 + line * 2 + core for line in range(LINE)] for far in range(FAR) for core in range(CORE)]
-    side_groups = [[far * 16 + line * 2 + core for far in range(FAR) for core in range(CORE)] for line in range(LINE)]
+    head_group = [HEAD_FIRST ^ slot for slot in range(4)]
+    far_groups, far_back_groups = (
+        [[(first ^ slot) * 16 + low for slot in range(FAR)] for low in range(16)] for first in (FAR_FIRST, FAR_BACK)
+    )
+    line_groups, line_back_groups = (
+        [[far * 16 + (first ^ slot) * 2 + core for slot in range(LINE)] for far in range(FAR) for core in range(CORE)]
+        for first in (LINE_FIRST, LINE_BACK)
+    )
+    spread_groups = [
+        [(SPREAD_FIRST ^ slot) * 16 + line * 2 + (SPREAD_CORE ^ core) for slot in range(FAR) for core in range(CORE)]
+        for line in range(LINE)
+    ]
     queries, keys, values = (array.transpose(1, 0, 2) for array in (queries, keys, values))
     ordered, line_out = start(offsets, keys, values)
     to_order, to_token, query, choice, choice_back, grads_out = tables(offsets, queries, out_grad)
@@ -396,19 +412,17 @@
     other_in = swap_cores(line_in)
     far_in = trade(far_out, far_groups)
     other_far_in = swap_cores(far_in)
-    grads = lax.all_to_all(grads_out, "head", 0, 0, tiled=True)
+    grads = lax.all_to_all(grads_out, "head", 0, 0, axis_index_groups=[head_group], tiled=True)
     output_keep, output_send, query_grad, send, keep_line, keep_far, keep_own, keep_weight = attention(
         to_order, to_token, query, choice, out_weight, grads, ordered, line_in, far_in, other_in, other_far_in
     )
     first = swap_heads(output_send, 1)
     received = swap_cores(send)
-    far_back = trade(far_return(choice_back, received, keep_far, keep_weight), far_groups)
-    line_back = trade(line_return(received, keep_line, far_back), line_groups)
-    line_back, first = lax.optimization_barrier((line_back, first))
-    output_sum = output_keep + first.astype(F32)
-    second = swap_heads(output_sum[1].astype(BF16), 3)
-    near_sum, spread_out = spread_pieces(line_back)
-    spread_in = trade(spread_out, side_groups)
+    far_back = trade(far_return(choice_back, received, keep_far, keep_weight), far_back_groups)
+    line_back = trade(line_return(received, keep_line, far_back), line_back_groups)
+    near_sum, spread_out, output_sum, second_out = spread_pieces(line_back, output_keep, first)
+    second = swap_heads(second_out, 3)
+    spread_in = trade(spread_out, spread_groups)
     key_grad, value_grad = finish(to_token, keep_own, received, near_sum)
     weight_grad, output = weight_rows(spread_in, output_sum, second)
     query_grad, key_grad, value_grad = (grad.transpose(1, 0, 2) for grad in (query_grad, key_grad, value_grad))

time: 102 us -> 97.3 us (0.954)
  waiting for transfers between devices: 19.2 us -> 14.1 us
  starting transfers between devices: 44.7 us -> 47.4 us
  blocking collectives: 26.3 us -> 23.8 us
    all_to_all x3, waiting for transfers between devices: 8.77 us -> 3.11 us  [trade(): lax.all_to_all(pieces, 'seq', 0, 0, axis_index_groups=groups, tiled=True)]
    ppermute x3, starting transfers between devices: 13.6 us -> 9.88 us  [swap_cores(): lax.ppermute(block, 'seq', [(i, i ^ 1) for i in range(FAR * LINE * CORE)])]
    all_to_all x2, blocking collectives: 26.3 us -> 23.8 us  [trade(): lax.all_to_all(pieces, 'seq', 0, 0, axis_index_groups=groups, tiled=True)]
    all_to_all x3, starting transfers between devices: 15.9 us -> 18.1 us  [trade(): lax.all_to_all(pieces, 'seq', 0, 0, axis_index_groups=groups, tiled=True)]
    ppermute x2, starting transfers between devices: 6.11 us -> 8.22 us  [swap_heads(): return lax.ppermute(block, 'head', [(i, i ^ way) for i in range(4)])]
    all_to_all x1, starting transfers between devices: 9.12 us -> 11.2 us  [shards(): lax.all_to_all(grads_out, 'head', 0, 0, axis_index_groups=[head_group], t...]
  transfers between devices with their start and end apart: 9 -> 9, of which waited for: 7 -> 5; matrix products, arithmetic and copies ran while one was open for 0% -> 0% of each run, Pallas kernels for 2% -> 2%
where the time goes in v8:
time: 97.3 us; the launch traced here: 95.8 us
  starting transfers between devices  47.4 us (49%)
  blocking collectives  23.8 us (24%)
  waiting for transfers between devices  14.1 us (14%)
  Pallas kernels  9.72 us (10%)
    all_to_all x2, blocking collectives, trade(): lax.all_to_all(pieces, 'seq', 0, 0, axis_index_groups=groups, tiled=True)  23.8 us
    all_to_all x3, starting transfers between devices, trade(): lax.all_to_all(pieces, 'seq', 0, 0, axis_index_groups=groups, tiled=True)  18.1 us
    all_to_all x1, starting transfers between devices, shards(): lax.all_to_all(grads_out, 'head', 0, 0, axis_index_groups=[head_group], t...  11.2 us
    ppermute x3, starting transfers between devices, swap_cores(): lax.ppermute(block, 'seq', [(i, i ^ 1) for i in range(FAR * LINE * CORE)])  9.88 us
    pallas_call x9, Pallas kernels, call(): pl.pallas_call(kernel, out_shape=[jax.ShapeDtypeStruct(shape, dtype) for...  9.72 us
    ppermute x2, starting transfers between devices, swap_heads(): return lax.ppermute(block, 'head', [(i, i ^ way) for i in range(4)])  8.22 us
    ppermute x2, waiting for transfers between devices, swap_heads(): return lax.ppermute(block, 'head', [(i, i ^ way) for i in range(4)])  8.19 us
    all_to_all x3, waiting for transfers between devices, trade(): lax.all_to_all(pieces, 'seq', 0, 0, axis_index_groups=groups, tiled=True)  3.11 us
  transfers between devices with their start and end apart: 9, of which 5 were waited for; matrix products, arithmetic and copies ran while one was open for 0% of the time, Pallas kernels for 2%

profile of v8, /device:TPU:1, one launch (start us, length us, event | category | flops | bytes accessed | tf_op | source)
XLA Modules:
  0.0 95.8 jit_solution(4405599743660870093)
XLA Ops:
  0.6 1.1 %shard_map.111 = (bf16[128,384]{1,0:T(8,128)(2,1)S(1)}, bf16[8,32,384]{2,1,0:T(8,128)(2,1)S(1)}) custom-call(s32[3]{0:T(128)} %offsets_far.1, bf16[3,64,128]{2,1,0:T(8,128)(2,1)} %bitcast.7, bf16[3,64,128]{2,1,0:T(8,128)(2,1)} %bitcast.8), custom_call_target="tpu_custom_call" | custom-call | tf_op jit(solution)/shard_map/pallas_call | solution.py:309
  1.7 13.0 %all_to_all.30.line_in = bf16[8,32,384]{2,1,0:T(8,128)(2,1)S(1)} all-to-all(bf16[8,32,384]{2,1,0:T(8,128)(2,1)S(1)} %get-tuple-element.35), channel_id=1, replica_groups={{56,48,40,32,24,16,8,0},{60,52,44,36,28,20,12,4},{120,112,104,96,88,80,..., dimensions={0} | all-to-all | bytes 393216 | tf_op jit(solution)/shard_map/all_to_all | solution.py:383
  14.8 0.0 copy-start.2
  14.8 0.0 copy-start.3
  14.8 0.0 copy-start.4
  14.8 0.7 shard_map.112
  15.5 0.0 copy-start
  15.5 6.5 %all-to-all-start.2 = ((bf16[8,32,384]{2,1,0:T(8,128)(2,1)}), bf16[8,32,384]{2,1,0:T(8,128)(2,1)S(1)}, u32[]{:S(2)}, u32[]{:S(2)}) async-start(bf16[8,32,384]{2,1,0:T(8,128)(2,1)} %shard_map.112), calls=%async_computation.2 | async-start | bytes 393216 | tf_op jit(solution)/shard_map/all_to_all | solution.py:383
  21.9 0.0 copy-start.1
  21.9 0.0 copy-done.2
  21.9 0.0 copy-done.3
  21.9 0.0 copy-done.4
  21.9 1.4 %shard_map.110 = (bf16[3,128,128]{2,1,0:T(8,128)(2,1)S(1)}, bf16[3,128,128]{2,1,0:T(8,128)(2,1)S(1)}, bf16[3,128,128]{2,1,0:T(8,128)(2,1)S(1)}, bf16[96,256]{1,0...) custom-call(s32[3]{0:T(128)S(1)} %copy-done.4, bf16[3,64,128]{2,1,0:T(8,128)(2,1)S(1)} %bitcast.6, ...), custom_call_target="tpu_custom_call" | custom-call | tf_op jit(solution)/shard_map/pallas_call | solution.py:309
  23.4 3.1 %all-to-all-done.2.far_in = bf16[8,32,384]{2,1,0:T(8,128)(2,1)S(1)} async-done(((bf16[8,32,384]{2,1,0:T(8,128)(2,1)}), bf16[8,32,384]{2,1,0:T(8,128)(2,1)S(1)}, u32[]{:S(2)}, u32[]{:S(2)}) %all-to-all-start.2) | async-done | bytes 196640 | tf_op jit(solution)/shard_map/all_to_all | solution.py:383
  26.5 11.2 %all-to-all-start = ((bf16[4,64,384]{2,1,0:T(8,128)(2,1)}), bf16[4,64,384]{2,1,0:T(8,128)(2,1)S(1)}, u32[]{:S(2)}, u32[]{:S(2)}) async-start(bf16[4,64,384]{2,1,0:T(8,128)(2,1)} %get-tuple-element.33), calls=%async_computation | async-start | bytes 393216 | tf_op jit(solution)/shard_map/all_to_all | solution.py:415
  37.6 5.6 %collective-permute-start = (bf16[8,32,384]{2,1,0:T(8,128)(2,1)S(1)}, bf16[8,32,384]{2,1,0:T(8,128)(2,1)S(1)}, u32[]{:S(2)}, u32[]{:S(2)}) collective-permute-start(bf16[8,32,384]{2,1,0:T(8,128)(2,1)S(1)} %all_to_all.30.line_in), channel_id=1, source_target_pairs={{0,4},{4,0},{8,12},{12,8},{16,20},{20,16},{24,28},{28,24},{32,36},... | collective-permute-start | bytes 589832 | tf_op jit(solution)/shard_map/ppermute | solution.py:387
  43.2 1.9 %collective-permute-start.1 = (bf16[8,32,384]{2,1,0:T(8,128)(2,1)S(1)}, bf16[8,32,384]{2,1,0:T(8,128)(2,1)S(1)}, u32[]{:S(2)}, u32[]{:S(2)}) collective-permute-start(bf16[8,32,384]{2,1,0:T(8,128)(2,1)S(1)} %all-to-all-done.2.far_in), channel_id=1, source_target_pairs={{0,4},{4,0},{8,12},{12,8},{16,20},{20,16},{24,28},{28,24},{32,36},... | collective-permute-start | bytes 589832 | tf_op jit(solution)/shard_map/ppermute | solution.py:387
  45.2 0.0 all-to-all-done.grads
  45.2 0.0 collective-permute-done.other_in
  45.2 1.4 %collective-permute-done.1.other_far_in = bf16[8,32,384]{2,1,0:T(8,128)(2,1)S(1)} collective-permute-done((bf16[8,32,384]{2,1,0:T(8,128)(2,1)S(1)}, bf16[8,32,384]{2,1,0:T(8,128)(2,1)S(1)}, u32[]{:S(2)}, u32[]{:S(2)}) %collective-permute-start.1) | collective-permute-done | bytes 196640 | tf_op jit(solution)/shard_map/ppermute | solution.py:387
  46.6 0.0 copy-done
  46.6 0.0 copy-done.1
  46.6 3.0 %shard_map.113 = (f32[2,64,384]{2,1,0:T(8,128)S(1)}, bf16[2,64,384]{2,1,0:T(8,128)(2,1)S(1)}, bf16[3,64,128]{2,1,0:T(8,128)(2,1)}, bf16[576,384]{1,0:T(8,128)(2,...) custom-call(bf16[3,128,128]{2,1,0:T(8,128)(2,1)S(1)} %get-tuple-elem, ...), custom_call_target="tpu_custom_call" | custom-call | tf_op jit(solution)/shard_map/pallas_call | solution.py:309
  49.5 2.4 %collective-permute-start.2 = (bf16[576,384]{1,0:T(8,128)(2,1)S(1)}, bf16[576,384]{1,0:T(8,128)(2,1)S(1)}, u32[]{:S(2)}, u32[]{:S(2)}) collective-permute-start(bf16[576,384]{1,0:T(8,128)(2,1)S(1)} %get-tuple-element.36), channel_id=1, source_target_pairs={{0,4},{4,0},{8,12},{12,8},{16,20},{20,16},{24,28},{28,24},{32,36},... | collective-permute-start | bytes 1327112 | tf_op jit(solution)/shard_map/ppermute | solution.py:387
  51.9 1.4 %collective-permute-done.2.received = bf16[576,384]{1,0:T(8,128)(2,1)S(1)} collective-permute-done((bf16[576,384]{1,0:T(8,128)(2,1)S(1)}, bf16[576,384]{1,0:T(8,128)(2,1)S(1)}, u32[]{:S(2)}, u32[]{:S(2)}) %collective-permute-start.2) | collective-permute-done | bytes 442400 | tf_op jit(solution)/shard_map/ppermute | solution.py:387
  53.3 0.2 shard_map.114
  53.6 10.8 %all_to_all.31.far_in = bf16[8,56,384]{2,1,0:T(8,128)(2,1)S(1)} all-to-all(bf16[8,56,384]{2,1,0:T(8,128)(2,1)S(1)} %shard_map.114), channel_id=1, replica_groups={{192,128,64,0,448,384,320,256},{196,132,68,4,452,388,324,260},{200,136,..., dimensions={0} | all-to-all | bytes 688128 | tf_op jit(solution)/shard_map/all_to_all | solution.py:383
  64.4 0.8 shard_map.115
  65.2 7.5 %all-to-all-start.4 = ((bf16[8,56,384]{2,1,0:T(8,128)(2,1)}), bf16[8,56,384]{2,1,0:T(8,128)(2,1)S(1)}, u32[]{:S(2)}, u32[]{:S(2)}) async-start(bf16[8,56,384]{2,1,0:T(8,128)(2,1)} %shard_map.115), calls=%async_computation.4 | async-start | bytes 688128 | tf_op jit(solution)/shard_map/all_to_all | solution.py:383
  72.7 3.7 %collective-permute-start.3 = (bf16[2,64,384]{2,1,0:T(8,128)(2,1)S(1)}, bf16[2,64,384]{2,1,0:T(8,128)(2,1)S(1)}, u32[]{:S(2)}, u32[]{:S(2)}) collective-permute-start(bf16[2,64,384]{2,1,0:T(8,128)(2,1)S(1)} %get-tuple-element.42), channel_id=1, source_target_pairs={{0,1},{1,0},{2,3},{3,2},{4,5},{5,4},{6,7},{7,6},{8,9},{9,8},{10,11... | collective-permute-start | bytes 294920 | tf_op jit(solution)/shard_map/ppermute | solution.py:391
  76.4 5.8 %collective-permute-done.3.first = bf16[2,64,384]{2,1,0:T(8,128)(2,1)S(1)} collective-permute-done((bf16[2,64,384]{2,1,0:T(8,128)(2,1)S(1)}, bf16[2,64,384]{2,1,0:T(8,128)(2,1)S(1)}, u32[]{:S(2)}, u32[]{:S(2)}) %collective-permute-start.3) | collective-permute-done | bytes 98336 | tf_op jit(solution)/shard_map/ppermute | solution.py:391
  82.2 0.0 all-to-all-done.4.line_in
  82.2 0.8 shard_map.116
  82.9 4.1 %all-to-all-start.5 = ((bf16[16,24,384]{2,1,0:T(8,128)(2,1)}), bf16[16,24,384]{2,1,0:T(8,128)(2,1)S(1)}, u32[]{:S(2)}, u32[]{:S(2)}) async-start(bf16[16,24,384]{2,1,0:T(8,128)(2,1)} %get-tuple-element.43), calls=%async_computation.5 | async-start | bytes 589824 | tf_op jit(solution)/shard_map/all_to_all | solution.py:383
  87.1 4.5 %collective-permute-start.4 = (bf16[64,384]{1,0:T(8,128)(2,1)S(1)}, bf16[64,384]{1,0:T(8,128)(2,1)S(1)}, u32[]{:S(2)}, u32[]{:S(2)}) collective-permute-start(bf16[64,384]{1,0:T(8,128)(2,1)S(1)} %get-tuple-element.45), channel_id=1, source_target_pairs={{0,3},{1,2},{2,1},{3,0},{4,7},{5,6},{6,5},{7,4},{8,11},{9,10},{10,... | collective-permute-start | bytes 147464 | tf_op jit(solution)/shard_map/ppermute | solution.py:391
  91.6 0.9 shard_map.118
  92.5 2.4 %collective-permute-done.4.second = bf16[64,384]{1,0:T(8,128)(2,1)S(1)} collective-permute-done((bf16[64,384]{1,0:T(8,128)(2,1)S(1)}, bf16[64,384]{1,0:T(8,128)(2,1)S(1)}, u32[]{:S(2)}, u32[]{:S(2)}) %collective-permute-start.4) | collective-permute-done | bytes 49184 | tf_op jit(solution)/shard_map/ppermute | solution.py:391
  94.9 0.0 all-to-all-done.5.spread_in
  94.9 0.9 shard_map.117
Async XLA Ops:
  14.8 7.2 %copy-start.2 = (bf16[64,3,128]{2,0,1:T(8,128)(2,1)S(1)}, bf16[64,3,128]{2,0,1:T(8,128)(2,1)}, u32[]{:S(2)}) copy-start(bf16[64,3,128]{2,0,1:T(8,128)(2,1)} %param.7) | copy-start | bytes 147460
  14.8 7.2 %copy-start.3 = (bf16[64,384]{1,0:T(8,128)(2,1)S(1)}, bf16[64,384]{1,0:T(8,128)(2,1)}, u32[]{:S(2)}) copy-start(bf16[64,384]{1,0:T(8,128)(2,1)} %grad.1) | copy-start | bytes 147460
  14.8 7.2 %copy-start.4 = (s32[3]{0:T(128)S(1)}, s32[3]{0:T(128)}, u32[]{:S(2)}) copy-start(s32[3]{0:T(128)} %offsets_far.1) | copy-start | bytes 40
  15.5 31.1 %copy-start = (f32[832,128]{1,0:T(8,128)S(1)}, f32[832,128]{1,0:T(8,128)}, u32[]{:S(2)}) copy-start(f32[832,128]{1,0:T(8,128)} %constant.2.clone.bias) | copy-start | bytes 1277956
  15.5 11.0 %all-to-all-start.2 = ((bf16[8,32,384]{2,1,0:T(8,128)(2,1)}), bf16[8,32,384]{2,1,0:T(8,128)(2,1)S(1)}, u32[]{:S(2)}, u32[]{:S(2)}) async-start(bf16[8,32,384]{2,1,0:T(8,128)(2,1)} %shard_map.112), calls=%async_computation.2 | async-start | bytes 393216 | tf_op jit(solution)/shard_map/all_to_all | solution.py:383
  21.9 24.7 %copy-start.1 = (bf16[192,768]{1,0:T(8,128)(2,1)S(1)}, bf16[192,768]{1,0:T(8,128)(2,1)}, u32[]{:S(2)}) copy-start(bf16[192,768]{1,0:T(8,128)(2,1)} %weight.1) | copy-start | bytes 884740
  26.5 18.7 %all-to-all-start = ((bf16[4,64,384]{2,1,0:T(8,128)(2,1)}), bf16[4,64,384]{2,1,0:T(8,128)(2,1)S(1)}, u32[]{:S(2)}, u32[]{:S(2)}) async-start(bf16[4,64,384]{2,1,0:T(8,128)(2,1)} %get-tuple-element.33), calls=%async_computation | async-start | bytes 393216 | tf_op jit(solution)/shard_map/all_to_all | solution.py:415
  37.6 7.5 %collective-permute-start = (bf16[8,32,384]{2,1,0:T(8,128)(2,1)S(1)}, bf16[8,32,384]{2,1,0:T(8,128)(2,1)S(1)}, u32[]{:S(2)}, u32[]{:S(2)}) collective-permute-start(bf16[8,32,384]{2,1,0:T(8,128)(2,1)S(1)} %all_to_all.30.line_in), channel_id=1, source_target_pairs={{0,4},{4,0},{8,12},{12,8},{16,20},{20,16},{24,28},{28,24},{32,36},... | collective-permute-start | bytes 589832 | tf_op jit(solution)/shard_map/ppermute | solution.py:387
  43.2 3.3 %collective-permute-start.1 = (bf16[8,32,384]{2,1,0:T(8,128)(2,1)S(1)}, bf16[8,32,384]{2,1,0:T(8,128)(2,1)S(1)}, u32[]{:S(2)}, u32[]{:S(2)}) collective-permute-start(bf16[8,32,384]{2,1,0:T(8,128)(2,1)S(1)} %all-to-all-done.2.far_in), channel_id=1, source_target_pairs={{0,4},{4,0},{8,12},{12,8},{16,20},{20,16},{24,28},{28,24},{32,36},... | collective-permute-start | bytes 589832 | tf_op jit(solution)/shard_map/ppermute | solution.py:387
  49.5 3.8 %collective-permute-start.2 = (bf16[576,384]{1,0:T(8,128)(2,1)S(1)}, bf16[576,384]{1,0:T(8,128)(2,1)S(1)}, u32[]{:S(2)}, u32[]{:S(2)}) collective-permute-start(bf16[576,384]{1,0:T(8,128)(2,1)S(1)} %get-tuple-element.36), channel_id=1, source_target_pairs={{0,4},{4,0},{8,12},{12,8},{16,20},{20,16},{24,28},{28,24},{32,36},... | collective-permute-start | bytes 1327112 | tf_op jit(solution)/shard_map/ppermute | solution.py:387
  65.2 17.0 %all-to-all-start.4 = ((bf16[8,56,384]{2,1,0:T(8,128)(2,1)}), bf16[8,56,384]{2,1,0:T(8,128)(2,1)S(1)}, u32[]{:S(2)}, u32[]{:S(2)}) async-start(bf16[8,56,384]{2,1,0:T(8,128)(2,1)} %shard_map.115), calls=%async_computation.4 | async-start | bytes 688128 | tf_op jit(solution)/shard_map/all_to_all | solution.py:383
  72.7 9.5 %collective-permute-start.3 = (bf16[2,64,384]{2,1,0:T(8,128)(2,1)S(1)}, bf16[2,64,384]{2,1,0:T(8,128)(2,1)S(1)}, u32[]{:S(2)}, u32[]{:S(2)}) collective-permute-start(bf16[2,64,384]{2,1,0:T(8,128)(2,1)S(1)} %get-tuple-element.42), channel_id=1, source_target_pairs={{0,1},{1,0},{2,3},{3,2},{4,5},{5,4},{6,7},{7,6},{8,9},{9,8},{10,11... | collective-permute-start | bytes 294920 | tf_op jit(solution)/shard_map/ppermute | solution.py:391
  82.9 12.0 %all-to-all-start.5 = ((bf16[16,24,384]{2,1,0:T(8,128)(2,1)}), bf16[16,24,384]{2,1,0:T(8,128)(2,1)S(1)}, u32[]{:S(2)}, u32[]{:S(2)}) async-start(bf16[16,24,384]{2,1,0:T(8,128)(2,1)} %get-tuple-element.43), calls=%async_computation.5 | async-start | bytes 589824 | tf_op jit(solution)/shard_map/all_to_all | solution.py:383
  87.1 7.8 %collective-permute-start.4 = (bf16[64,384]{1,0:T(8,128)(2,1)S(1)}, bf16[64,384]{1,0:T(8,128)(2,1)S(1)}, u32[]{:S(2)}, u32[]{:S(2)}) collective-permute-start(bf16[64,384]{1,0:T(8,128)(2,1)S(1)} %get-tuple-element.45), channel_id=1, source_target_pairs={{0,3},{1,2},{2,1},{3,0},{4,7},{5,6},{6,5},{7,4},{8,11},{9,10},{10,... | collective-permute-start | bytes 147464 | tf_op jit(solution)/shard_map/ppermute | solution.py:391

commit v9 on v8

--- a/solution.py
+++ b/solution.py
@@ -9,8 +9,8 @@
 from jax.sharding import PartitionSpec as P
 
 FAR, LINE, CORE = 8, 8, 2
-FAR_FIRST, LINE_FIRST, HEAD_FIRST = 3, 7, 3
-FAR_BACK, LINE_BACK, SPREAD_FIRST, SPREAD_CORE = 3, 7, 3, 1
+FAR_FIRST, LINE_FIRST, HEAD_FIRST = 3, 6, 3
+FAR_BACK, LINE_BACK, SPREAD_FIRST, SPREAD_CORE = 3, 7, 2, 1
 ROWS = 128
 LOCAL = 3
 SIZE = 64

time: 97.3 us -> 95.6 us (0.983)
  waiting for transfers between devices: 14.1 us -> 11.7 us
  starting transfers between devices: 47.4 us -> 48.6 us
    ppermute x2, waiting for transfers between devices: 8.19 us -> 5.58 us  [swap_heads(): return lax.ppermute(block, 'head', [(i, i ^ way) for i in range(4)])]
where the time goes in v9:
time: 95.6 us; the launch traced here: 94.2 us
  starting transfers between devices  48.6 us (51%)
  blocking collectives  23.4 us (24%)
  waiting for transfers between devices  11.7 us (12%)
  Pallas kernels  9.73 us (10%)
    all_to_all x2, blocking collectives, trade(): lax.all_to_all(pieces, 'seq', 0, 0, axis_index_groups=groups, tiled=True)  23.4 us
    all_to_all x3, starting transfers between devices, trade(): lax.all_to_all(pieces, 'seq', 0, 0, axis_index_groups=groups, tiled=True)  18.5 us
    all_to_all x1, starting transfers between devices, shards(): lax.all_to_all(grads_out, 'head', 0, 0, axis_index_groups=[head_group], t...  11.2 us
    ppermute x3, starting transfers between devices, swap_cores(): lax.ppermute(block, 'seq', [(i, i ^ 1) for i in range(FAR * LINE * CORE)])  10.2 us
    pallas_call x9, Pallas kernels, call(): pl.pallas_call(kernel, out_shape=[jax.ShapeDtypeStruct(shape, dtype) for...  9.73 us
    ppermute x2, starting transfers between devices, swap_heads(): return lax.ppermute(block, 'head', [(i, i ^ way) for i in range(4)])  8.7 us
    ppermute x2, waiting for transfers between devices, swap_heads(): return lax.ppermute(block, 'head', [(i, i ^ way) for i in range(4)])  5.58 us
    all_to_all x3, waiting for transfers between devices, trade(): lax.all_to_all(pieces, 'seq', 0, 0, axis_index_groups=groups, tiled=True)  3.11 us
  transfers between devices with their start and end apart: 9, of which 5 were waited for; matrix products, arithmetic and copies ran while one was open for 0% of the time, Pallas kernels for 2%

profile of v9, /device:TPU:1, one launch (start us, length us, event | category | flops | bytes accessed | tf_op | source)
XLA Modules:
  0.0 94.2 jit_solution(9006422139708259511)
XLA Ops:
  0.6 1.1 %shard_map.111 = (bf16[128,384]{1,0:T(8,128)(2,1)S(1)}, bf16[8,32,384]{2,1,0:T(8,128)(2,1)S(1)}) custom-call(s32[3]{0:T(128)} %offsets_far.1, bf16[3,64,128]{2,1,0:T(8,128)(2,1)} %bitcast.7, bf16[3,64,128]{2,1,0:T(8,128)(2,1)} %bitcast.8), custom_call_target="tpu_custom_call" | custom-call | tf_op jit(solution)/shard_map/pallas_call | solution.py:309
  1.7 12.0 %all_to_all.30.line_in = bf16[8,32,384]{2,1,0:T(8,128)(2,1)S(1)} all-to-all(bf16[8,32,384]{2,1,0:T(8,128)(2,1)S(1)} %get-tuple-element.35), channel_id=1, replica_groups={{48,56,32,40,16,24,0,8},{52,60,36,44,20,28,4,12},{112,120,96,104,80,88,..., dimensions={0} | all-to-all | bytes 393216 | tf_op jit(solution)/shard_map/all_to_all | solution.py:383
  13.8 0.0 copy-start.2
  13.8 0.0 copy-start.3
  13.8 0.0 copy-start.4
  13.8 0.7 shard_map.112
  14.5 0.0 copy-start
  14.5 6.6 %all-to-all-start.2 = ((bf16[8,32,384]{2,1,0:T(8,128)(2,1)}), bf16[8,32,384]{2,1,0:T(8,128)(2,1)S(1)}, u32[]{:S(2)}, u32[]{:S(2)}) async-start(bf16[8,32,384]{2,1,0:T(8,128)(2,1)} %shard_map.112), calls=%async_computation.2 | async-start | bytes 393216 | tf_op jit(solution)/shard_map/all_to_all | solution.py:383
  21.1 0.0 copy-start.1
  21.1 0.0 copy-done.2
  21.1 0.0 copy-done.3
  21.1 0.0 copy-done.4
  21.1 1.4 %shard_map.110 = (bf16[3,128,128]{2,1,0:T(8,128)(2,1)S(1)}, bf16[3,128,128]{2,1,0:T(8,128)(2,1)S(1)}, bf16[3,128,128]{2,1,0:T(8,128)(2,1)S(1)}, bf16[96,256]{1,0...) custom-call(s32[3]{0:T(128)S(1)} %copy-done.4, bf16[3,64,128]{2,1,0:T(8,128)(2,1)S(1)} %bitcast.6, ...), custom_call_target="tpu_custom_call" | custom-call | tf_op jit(solution)/shard_map/pallas_call | solution.py:309
  22.5 3.1 %all-to-all-done.2.far_in = bf16[8,32,384]{2,1,0:T(8,128)(2,1)S(1)} async-done(((bf16[8,32,384]{2,1,0:T(8,128)(2,1)}), bf16[8,32,384]{2,1,0:T(8,128)(2,1)S(1)}, u32[]{:S(2)}, u32[]{:S(2)}) %all-to-all-start.2) | async-done | bytes 196640 | tf_op jit(solution)/shard_map/all_to_all | solution.py:383
  25.6 11.2 %all-to-all-start = ((bf16[4,64,384]{2,1,0:T(8,128)(2,1)}), bf16[4,64,384]{2,1,0:T(8,128)(2,1)S(1)}, u32[]{:S(2)}, u32[]{:S(2)}) async-start(bf16[4,64,384]{2,1,0:T(8,128)(2,1)} %get-tuple-element.33), calls=%async_computation | async-start | bytes 393216 | tf_op jit(solution)/shard_map/all_to_all | solution.py:415
  36.8 6.3 %collective-permute-start = (bf16[8,32,384]{2,1,0:T(8,128)(2,1)S(1)}, bf16[8,32,384]{2,1,0:T(8,128)(2,1)S(1)}, u32[]{:S(2)}, u32[]{:S(2)}) collective-permute-start(bf16[8,32,384]{2,1,0:T(8,128)(2,1)S(1)} %all_to_all.30.line_in), channel_id=1, source_target_pairs={{0,4},{4,0},{8,12},{12,8},{16,20},{20,16},{24,28},{28,24},{32,36},... | collective-permute-start | bytes 589832 | tf_op jit(solution)/shard_map/ppermute | solution.py:387
  43.1 1.9 %collective-permute-start.1 = (bf16[8,32,384]{2,1,0:T(8,128)(2,1)S(1)}, bf16[8,32,384]{2,1,0:T(8,128)(2,1)S(1)}, u32[]{:S(2)}, u32[]{:S(2)}) collective-permute-start(bf16[8,32,384]{2,1,0:T(8,128)(2,1)S(1)} %all-to-all-done.2.far_in), channel_id=1, source_target_pairs={{0,4},{4,0},{8,12},{12,8},{16,20},{20,16},{24,28},{28,24},{32,36},... | collective-permute-start | bytes 589832 | tf_op jit(solution)/shard_map/ppermute | solution.py:387
  45.0 0.0 all-to-all-done.grads
  45.0 0.0 collective-permute-done.other_in
  45.0 1.4 %collective-permute-done.1.other_far_in = bf16[8,32,384]{2,1,0:T(8,128)(2,1)S(1)} collective-permute-done((bf16[8,32,384]{2,1,0:T(8,128)(2,1)S(1)}, bf16[8,32,384]{2,1,0:T(8,128)(2,1)S(1)}, u32[]{:S(2)}, u32[]{:S(2)}) %collective-permute-start.1) | collective-permute-done | bytes 196640 | tf_op jit(solution)/shard_map/ppermute | solution.py:387
  46.4 0.0 copy-done
  46.4 0.0 copy-done.1
  46.4 3.0 %shard_map.113 = (f32[2,64,384]{2,1,0:T(8,128)S(1)}, bf16[2,64,384]{2,1,0:T(8,128)(2,1)S(1)}, bf16[3,64,128]{2,1,0:T(8,128)(2,1)}, bf16[576,384]{1,0:T(8,128)(2,...) custom-call(bf16[3,128,128]{2,1,0:T(8,128)(2,1)S(1)} %get-tuple-elem, ...), custom_call_target="tpu_custom_call" | custom-call | tf_op jit(solution)/shard_map/pallas_call | solution.py:309
  49.4 2.0 %collective-permute-start.2 = (bf16[576,384]{1,0:T(8,128)(2,1)S(1)}, bf16[576,384]{1,0:T(8,128)(2,1)S(1)}, u32[]{:S(2)}, u32[]{:S(2)}) collective-permute-start(bf16[576,384]{1,0:T(8,128)(2,1)S(1)} %get-tuple-element.36), channel_id=1, source_target_pairs={{0,4},{4,0},{8,12},{12,8},{16,20},{20,16},{24,28},{28,24},{32,36},... | collective-permute-start | bytes 1327112 | tf_op jit(solution)/shard_map/ppermute | solution.py:387
  51.4 1.6 %collective-permute-done.2.received = bf16[576,384]{1,0:T(8,128)(2,1)S(1)} collective-permute-done((bf16[576,384]{1,0:T(8,128)(2,1)S(1)}, bf16[576,384]{1,0:T(8,128)(2,1)S(1)}, u32[]{:S(2)}, u32[]{:S(2)}) %collective-permute-start.2) | collective-permute-done | bytes 442400 | tf_op jit(solution)/shard_map/ppermute | solution.py:387
  53.1 0.2 shard_map.114
  53.3 11.3 %all_to_all.31.far_in = bf16[8,56,384]{2,1,0:T(8,128)(2,1)S(1)} all-to-all(bf16[8,56,384]{2,1,0:T(8,128)(2,1)S(1)} %shard_map.114), channel_id=1, replica_groups={{192,128,64,0,448,384,320,256},{196,132,68,4,452,388,324,260},{200,136,..., dimensions={0} | all-to-all | bytes 688128 | tf_op jit(solution)/shard_map/all_to_all | solution.py:383
  64.7 0.8 shard_map.115
  65.5 5.9 %all-to-all-start.4 = ((bf16[8,56,384]{2,1,0:T(8,128)(2,1)}), bf16[8,56,384]{2,1,0:T(8,128)(2,1)S(1)}, u32[]{:S(2)}, u32[]{:S(2)}) async-start(bf16[8,56,384]{2,1,0:T(8,128)(2,1)} %shard_map.115), calls=%async_computation.4 | async-start | bytes 688128 | tf_op jit(solution)/shard_map/all_to_all | solution.py:383
  71.4 3.9 %collective-permute-start.3 = (bf16[2,64,384]{2,1,0:T(8,128)(2,1)S(1)}, bf16[2,64,384]{2,1,0:T(8,128)(2,1)S(1)}, u32[]{:S(2)}, u32[]{:S(2)}) collective-permute-start(bf16[2,64,384]{2,1,0:T(8,128)(2,1)S(1)} %get-tuple-element.42), channel_id=1, source_target_pairs={{0,1},{1,0},{2,3},{3,2},{4,5},{5,4},{6,7},{7,6},{8,9},{9,8},{10,11... | collective-permute-start | bytes 294920 | tf_op jit(solution)/shard_map/ppermute | solution.py:391
  75.3 3.6 %collective-permute-done.3.first = bf16[2,64,384]{2,1,0:T(8,128)(2,1)S(1)} collective-permute-done((bf16[2,64,384]{2,1,0:T(8,128)(2,1)S(1)}, bf16[2,64,384]{2,1,0:T(8,128)(2,1)S(1)}, u32[]{:S(2)}, u32[]{:S(2)}) %collective-permute-start.3) | collective-permute-done | bytes 98336 | tf_op jit(solution)/shard_map/ppermute | solution.py:391
  78.8 0.0 all-to-all-done.4.line_in
  78.8 0.8 shard_map.116
  79.6 6.0 %all-to-all-start.5 = ((bf16[16,24,384]{2,1,0:T(8,128)(2,1)}), bf16[16,24,384]{2,1,0:T(8,128)(2,1)S(1)}, u32[]{:S(2)}, u32[]{:S(2)}) async-start(bf16[16,24,384]{2,1,0:T(8,128)(2,1)} %get-tuple-element.43), calls=%async_computation.5 | async-start | bytes 589824 | tf_op jit(solution)/shard_map/all_to_all | solution.py:383
  85.6 4.8 %collective-permute-start.4 = (bf16[64,384]{1,0:T(8,128)(2,1)S(1)}, bf16[64,384]{1,0:T(8,128)(2,1)S(1)}, u32[]{:S(2)}, u32[]{:S(2)}) collective-permute-start(bf16[64,384]{1,0:T(8,128)(2,1)S(1)} %get-tuple-element.45), channel_id=1, source_target_pairs={{0,3},{1,2},{2,1},{3,0},{4,7},{5,6},{6,5},{7,4},{8,11},{9,10},{10,... | collective-permute-start | bytes 147464 | tf_op jit(solution)/shard_map/ppermute | solution.py:391
  90.4 0.9 shard_map.118
  91.3 2.0 %collective-permute-done.4.second = bf16[64,384]{1,0:T(8,128)(2,1)S(1)} collective-permute-done((bf16[64,384]{1,0:T(8,128)(2,1)S(1)}, bf16[64,384]{1,0:T(8,128)(2,1)S(1)}, u32[]{:S(2)}, u32[]{:S(2)}) %collective-permute-start.4) | collective-permute-done | bytes 49184 | tf_op jit(solution)/shard_map/ppermute | solution.py:391
  93.3 0.0 all-to-all-done.5.spread_in
  93.3 0.9 shard_map.117
Async XLA Ops:
  13.8 7.3 %copy-start.2 = (bf16[64,3,128]{2,0,1:T(8,128)(2,1)S(1)}, bf16[64,3,128]{2,0,1:T(8,128)(2,1)}, u32[]{:S(2)}) copy-start(bf16[64,3,128]{2,0,1:T(8,128)(2,1)} %param.7) | copy-start | bytes 147460
  13.8 7.3 %copy-start.3 = (bf16[64,384]{1,0:T(8,128)(2,1)S(1)}, bf16[64,384]{1,0:T(8,128)(2,1)}, u32[]{:S(2)}) copy-start(bf16[64,384]{1,0:T(8,128)(2,1)} %grad.1) | copy-start | bytes 147460
  13.8 7.3 %copy-start.4 = (s32[3]{0:T(128)S(1)}, s32[3]{0:T(128)}, u32[]{:S(2)}) copy-start(s32[3]{0:T(128)} %offsets_far.1) | copy-start | bytes 40
  14.5 32.0 %copy-start = (f32[832,128]{1,0:T(8,128)S(1)}, f32[832,128]{1,0:T(8,128)}, u32[]{:S(2)}) copy-start(f32[832,128]{1,0:T(8,128)} %constant.2.clone.bias) | copy-start | bytes 1277956
  14.5 11.2 %all-to-all-start.2 = ((bf16[8,32,384]{2,1,0:T(8,128)(2,1)}), bf16[8,32,384]{2,1,0:T(8,128)(2,1)S(1)}, u32[]{:S(2)}, u32[]{:S(2)}) async-start(bf16[8,32,384]{2,1,0:T(8,128)(2,1)} %shard_map.112), calls=%async_computation.2 | async-start | bytes 393216 | tf_op jit(solution)/shard_map/all_to_all | solution.py:383
  21.1 25.4 %copy-start.1 = (bf16[192,768]{1,0:T(8,128)(2,1)S(1)}, bf16[192,768]{1,0:T(8,128)(2,1)}, u32[]{:S(2)}) copy-start(bf16[192,768]{1,0:T(8,128)(2,1)} %weight.1) | copy-start | bytes 884740
  25.6 19.4 %all-to-all-start = ((bf16[4,64,384]{2,1,0:T(8,128)(2,1)}), bf16[4,64,384]{2,1,0:T(8,128)(2,1)S(1)}, u32[]{:S(2)}, u32[]{:S(2)}) async-start(bf16[4,64,384]{2,1,0:T(8,128)(2,1)} %get-tuple-element.33), calls=%async_computation | async-start | bytes 393216 | tf_op jit(solution)/shard_map/all_to_all | solution.py:415
  36.8 8.2 %collective-permute-start = (bf16[8,32,384]{2,1,0:T(8,128)(2,1)S(1)}, bf16[8,32,384]{2,1,0:T(8,128)(2,1)S(1)}, u32[]{:S(2)}, u32[]{:S(2)}) collective-permute-start(bf16[8,32,384]{2,1,0:T(8,128)(2,1)S(1)} %all_to_all.30.line_in), channel_id=1, source_target_pairs={{0,4},{4,0},{8,12},{12,8},{16,20},{20,16},{24,28},{28,24},{32,36},... | collective-permute-start | bytes 589832 | tf_op jit(solution)/shard_map/ppermute | solution.py:387
  43.1 3.3 %collective-permute-start.1 = (bf16[8,32,384]{2,1,0:T(8,128)(2,1)S(1)}, bf16[8,32,384]{2,1,0:T(8,128)(2,1)S(1)}, u32[]{:S(2)}, u32[]{:S(2)}) collective-permute-start(bf16[8,32,384]{2,1,0:T(8,128)(2,1)S(1)} %all-to-all-done.2.far_in), channel_id=1, source_target_pairs={{0,4},{4,0},{8,12},{12,8},{16,20},{20,16},{24,28},{28,24},{32,36},... | collective-permute-start | bytes 589832 | tf_op jit(solution)/shard_map/ppermute | solution.py:387
  49.4 3.7 %collective-permute-start.2 = (bf16[576,384]{1,0:T(8,128)(2,1)S(1)}, bf16[576,384]{1,0:T(8,128)(2,1)S(1)}, u32[]{:S(2)}, u32[]{:S(2)}) collective-permute-start(bf16[576,384]{1,0:T(8,128)(2,1)S(1)} %get-tuple-element.36), channel_id=1, source_target_pairs={{0,4},{4,0},{8,12},{12,8},{16,20},{20,16},{24,28},{28,24},{32,36},... | collective-permute-start | bytes 1327112 | tf_op jit(solution)/shard_map/ppermute | solution.py:387
  65.5 13.3 %all-to-all-start.4 = ((bf16[8,56,384]{2,1,0:T(8,128)(2,1)}), bf16[8,56,384]{2,1,0:T(8,128)(2,1)S(1)}, u32[]{:S(2)}, u32[]{:S(2)}) async-start(bf16[8,56,384]{2,1,0:T(8,128)(2,1)} %shard_map.115), calls=%async_computation.4 | async-start | bytes 688128 | tf_op jit(solution)/shard_map/all_to_all | solution.py:383
  71.4 7.4 %collective-permute-start.3 = (bf16[2,64,384]{2,1,0:T(8,128)(2,1)S(1)}, bf16[2,64,384]{2,1,0:T(8,128)(2,1)S(1)}, u32[]{:S(2)}, u32[]{:S(2)}) collective-permute-start(bf16[2,64,384]{2,1,0:T(8,128)(2,1)S(1)} %get-tuple-element.42), channel_id=1, source_target_pairs={{0,1},{1,0},{2,3},{3,2},{4,5},{5,4},{6,7},{7,6},{8,9},{9,8},{10,11... | collective-permute-start | bytes 294920 | tf_op jit(solution)/shard_map/ppermute | solution.py:391
  79.6 13.8 %all-to-all-start.5 = ((bf16[16,24,384]{2,1,0:T(8,128)(2,1)}), bf16[16,24,384]{2,1,0:T(8,128)(2,1)S(1)}, u32[]{:S(2)}, u32[]{:S(2)}) async-start(bf16[16,24,384]{2,1,0:T(8,128)(2,1)} %get-tuple-element.43), calls=%async_computation.5 | async-start | bytes 589824 | tf_op jit(solution)/shard_map/all_to_all | solution.py:383
  85.6 7.8 %collective-permute-start.4 = (bf16[64,384]{1,0:T(8,128)(2,1)S(1)}, bf16[64,384]{1,0:T(8,128)(2,1)S(1)}, u32[]{:S(2)}, u32[]{:S(2)}) collective-permute-start(bf16[64,384]{1,0:T(8,128)(2,1)S(1)} %get-tuple-element.45), channel_id=1, source_target_pairs={{0,3},{1,2},{2,1},{3,0},{4,7},{5,6},{6,5},{7,4},{8,11},{9,10},{10,... | collective-permute-start | bytes 147464 | tf_op jit(solution)/shard_map/ppermute | solution.py:391

commit v10 on v9

--- a/solution.py
+++ b/solution.py
@@ -10,7 +10,7 @@
 
 FAR, LINE, CORE = 8, 8, 2
 FAR_FIRST, LINE_FIRST, HEAD_FIRST = 3, 6, 3
-FAR_BACK, LINE_BACK, SPREAD_FIRST, SPREAD_CORE = 3, 7, 2, 1
+FAR_BACK, LINE_BACK, SPREAD_FIRST, SPREAD_CORE = 3, 5, 1, 1
 ROWS = 128
 LOCAL = 3
 SIZE = 64

time: 95.6 us -> 95.1 us (level)
  waiting for transfers between devices: 11.7 us -> 14.1 us
  starting transfers between devices: 48.6 us -> 46.4 us
    ppermute x2, waiting for transfers between devices: 5.58 us -> 7.99 us  [swap_heads(): return lax.ppermute(block, 'head', [(i, i ^ way) for i in range(4)])]
    all_to_all x3, starting transfers between devices: 18.5 us -> 16.8 us  [trade(): lax.all_to_all(pieces, 'seq', 0, 0, axis_index_groups=groups, tiled=True)]
where the time goes in v10:
time: 95.1 us; the launch traced here: 94.4 us
  starting transfers between devices  46.4 us (49%)
  blocking collectives  23.4 us (25%)
  waiting for transfers between devices  14.1 us (15%)
  Pallas kernels  9.73 us (10%)
    all_to_all x2, blocking collectives, trade(): lax.all_to_all(pieces, 'seq', 0, 0, axis_index_groups=groups, tiled=True)  23.4 us
    all_to_all x3, starting transfers between devices, trade(): lax.all_to_all(pieces, 'seq', 0, 0, axis_index_groups=groups, tiled=True)  16.8 us
    all_to_all x1, starting transfers between devices, shards(): lax.all_to_all(grads_out, 'head', 0, 0, axis_index_groups=[head_group], t...  11.2 us
    ppermute x3, starting transfers between devices, swap_cores(): lax.ppermute(block, 'seq', [(i, i ^ 1) for i in range(FAR * LINE * CORE)])  10.2 us
    pallas_call x9, Pallas kernels, call(): pl.pallas_call(kernel, out_shape=[jax.ShapeDtypeStruct(shape, dtype) for...  9.73 us
    ppermute x2, starting transfers between devices, swap_heads(): return lax.ppermute(block, 'head', [(i, i ^ way) for i in range(4)])  8.21 us
    ppermute x2, waiting for transfers between devices, swap_heads(): return lax.ppermute(block, 'head', [(i, i ^ way) for i in range(4)])  7.99 us
    all_to_all x3, waiting for transfers between devices, trade(): lax.all_to_all(pieces, 'seq', 0, 0, axis_index_groups=groups, tiled=True)  3.11 us
  transfers between devices with their start and end apart: 9, of which 5 were waited for; matrix products, arithmetic and copies ran while one was open for 0% of the time, Pallas kernels for 2%

profile of v10, /device:TPU:1, one launch (start us, length us, event | category | flops | bytes accessed | tf_op | source)
XLA Modules:
  0.0 94.4 jit_solution(7346129306689530720)
XLA Ops:
  0.6 1.1 %shard_map.111 = (bf16[128,384]{1,0:T(8,128)(2,1)S(1)}, bf16[8,32,384]{2,1,0:T(8,128)(2,1)S(1)}) custom-call(s32[3]{0:T(128)} %offsets_far.1, bf16[3,64,128]{2,1,0:T(8,128)(2,1)} %bitcast.7, bf16[3,64,128]{2,1,0:T(8,128)(2,1)} %bitcast.8), custom_call_target="tpu_custom_call" | custom-call | tf_op jit(solution)/shard_map/pallas_call | solution.py:309
  1.7 12.0 %all_to_all.30.line_in = bf16[8,32,384]{2,1,0:T(8,128)(2,1)S(1)} all-to-all(bf16[8,32,384]{2,1,0:T(8,128)(2,1)S(1)} %get-tuple-element.35), channel_id=1, replica_groups={{48,56,32,40,16,24,0,8},{52,60,36,44,20,28,4,12},{112,120,96,104,80,88,..., dimensions={0} | all-to-all | bytes 393216 | tf_op jit(solution)/shard_map/all_to_all | solution.py:383
  13.8 0.0 copy-start.2
  13.8 0.0 copy-start.3
  13.8 0.0 copy-start.4
  13.8 0.7 shard_map.112
  14.5 0.0 copy-start
  14.5 6.6 %all-to-all-start.2 = ((bf16[8,32,384]{2,1,0:T(8,128)(2,1)}), bf16[8,32,384]{2,1,0:T(8,128)(2,1)S(1)}, u32[]{:S(2)}, u32[]{:S(2)}) async-start(bf16[8,32,384]{2,1,0:T(8,128)(2,1)} %shard_map.112), calls=%async_computation.2 | async-start | bytes 393216 | tf_op jit(solution)/shard_map/all_to_all | solution.py:383
  21.1 0.0 copy-start.1
  21.1 0.0 copy-done.2
  21.1 0.0 copy-done.3
  21.1 0.0 copy-done.4
  21.1 1.4 %shard_map.110 = (bf16[3,128,128]{2,1,0:T(8,128)(2,1)S(1)}, bf16[3,128,128]{2,1,0:T(8,128)(2,1)S(1)}, bf16[3,128,128]{2,1,0:T(8,128)(2,1)S(1)}, bf16[96,256]{1,0...) custom-call(s32[3]{0:T(128)S(1)} %copy-done.4, bf16[3,64,128]{2,1,0:T(8,128)(2,1)S(1)} %bitcast.6, ...), custom_call_target="tpu_custom_call" | custom-call | tf_op jit(solution)/shard_map/pallas_call | solution.py:309
  22.5 3.1 %all-to-all-done.2.far_in = bf16[8,32,384]{2,1,0:T(8,128)(2,1)S(1)} async-done(((bf16[8,32,384]{2,1,0:T(8,128)(2,1)}), bf16[8,32,384]{2,1,0:T(8,128)(2,1)S(1)}, u32[]{:S(2)}, u32[]{:S(2)}) %all-to-all-start.2) | async-done | bytes 196640 | tf_op jit(solution)/shard_map/all_to_all | solution.py:383
  25.6 11.2 %all-to-all-start = ((bf16[4,64,384]{2,1,0:T(8,128)(2,1)}), bf16[4,64,384]{2,1,0:T(8,128)(2,1)S(1)}, u32[]{:S(2)}, u32[]{:S(2)}) async-start(bf16[4,64,384]{2,1,0:T(8,128)(2,1)} %get-tuple-element.33), calls=%async_computation | async-start | bytes 393216 | tf_op jit(solution)/shard_map/all_to_all | solution.py:415
  36.8 6.3 %collective-permute-start = (bf16[8,32,384]{2,1,0:T(8,128)(2,1)S(1)}, bf16[8,32,384]{2,1,0:T(8,128)(2,1)S(1)}, u32[]{:S(2)}, u32[]{:S(2)}) collective-permute-start(bf16[8,32,384]{2,1,0:T(8,128)(2,1)S(1)} %all_to_all.30.line_in), channel_id=1, source_target_pairs={{0,4},{4,0},{8,12},{12,8},{16,20},{20,16},{24,28},{28,24},{32,36},... | collective-permute-start | bytes 589832 | tf_op jit(solution)/shard_map/ppermute | solution.py:387
  43.1 1.9 %collective-permute-start.1 = (bf16[8,32,384]{2,1,0:T(8,128)(2,1)S(1)}, bf16[8,32,384]{2,1,0:T(8,128)(2,1)S(1)}, u32[]{:S(2)}, u32[]{:S(2)}) collective-permute-start(bf16[8,32,384]{2,1,0:T(8,128)(2,1)S(1)} %all-to-all-done.2.far_in), channel_id=1, source_target_pairs={{0,4},{4,0},{8,12},{12,8},{16,20},{20,16},{24,28},{28,24},{32,36},... | collective-permute-start | bytes 589832 | tf_op jit(solution)/shard_map/ppermute | solution.py:387
  45.0 0.0 all-to-all-done.grads
  45.0 0.0 collective-permute-done.other_in
  45.0 1.4 %collective-permute-done.1.other_far_in = bf16[8,32,384]{2,1,0:T(8,128)(2,1)S(1)} collective-permute-done((bf16[8,32,384]{2,1,0:T(8,128)(2,1)S(1)}, bf16[8,32,384]{2,1,0:T(8,128)(2,1)S(1)}, u32[]{:S(2)}, u32[]{:S(2)}) %collective-permute-start.1) | collective-permute-done | bytes 196640 | tf_op jit(solution)/shard_map/ppermute | solution.py:387
  46.4 0.0 copy-done
  46.4 0.0 copy-done.1
  46.4 3.0 %shard_map.113 = (f32[2,64,384]{2,1,0:T(8,128)S(1)}, bf16[2,64,384]{2,1,0:T(8,128)(2,1)S(1)}, bf16[3,64,128]{2,1,0:T(8,128)(2,1)}, bf16[576,384]{1,0:T(8,128)(2,...) custom-call(bf16[3,128,128]{2,1,0:T(8,128)(2,1)S(1)} %get-tuple-elem, ...), custom_call_target="tpu_custom_call" | custom-call | tf_op jit(solution)/shard_map/pallas_call | solution.py:309
  49.4 2.0 %collective-permute-start.2 = (bf16[576,384]{1,0:T(8,128)(2,1)S(1)}, bf16[576,384]{1,0:T(8,128)(2,1)S(1)}, u32[]{:S(2)}, u32[]{:S(2)}) collective-permute-start(bf16[576,384]{1,0:T(8,128)(2,1)S(1)} %get-tuple-element.36), channel_id=1, source_target_pairs={{0,4},{4,0},{8,12},{12,8},{16,20},{20,16},{24,28},{28,24},{32,36},... | collective-permute-start | bytes 1327112 | tf_op jit(solution)/shard_map/ppermute | solution.py:387
  51.4 1.6 %collective-permute-done.2.received = bf16[576,384]{1,0:T(8,128)(2,1)S(1)} collective-permute-done((bf16[576,384]{1,0:T(8,128)(2,1)S(1)}, bf16[576,384]{1,0:T(8,128)(2,1)S(1)}, u32[]{:S(2)}, u32[]{:S(2)}) %collective-permute-start.2) | collective-permute-done | bytes 442400 | tf_op jit(solution)/shard_map/ppermute | solution.py:387
  53.1 0.2 shard_map.114
  53.3 11.3 %all_to_all.31.far_in = bf16[8,56,384]{2,1,0:T(8,128)(2,1)S(1)} all-to-all(bf16[8,56,384]{2,1,0:T(8,128)(2,1)S(1)} %shard_map.114), channel_id=1, replica_groups={{192,128,64,0,448,384,320,256},{196,132,68,4,452,388,324,260},{200,136,..., dimensions={0} | all-to-all | bytes 688128 | tf_op jit(solution)/shard_map/all_to_all | solution.py:383
  64.7 0.8 shard_map.115
  65.5 6.8 %all-to-all-start.4 = ((bf16[8,56,384]{2,1,0:T(8,128)(2,1)}), bf16[8,56,384]{2,1,0:T(8,128)(2,1)S(1)}, u32[]{:S(2)}, u32[]{:S(2)}) async-start(bf16[8,56,384]{2,1,0:T(8,128)(2,1)} %shard_map.115), calls=%async_computation.4 | async-start | bytes 688128 | tf_op jit(solution)/shard_map/all_to_all | solution.py:383
  72.2 3.5 %collective-permute-start.3 = (bf16[2,64,384]{2,1,0:T(8,128)(2,1)S(1)}, bf16[2,64,384]{2,1,0:T(8,128)(2,1)S(1)}, u32[]{:S(2)}, u32[]{:S(2)}) collective-permute-start(bf16[2,64,384]{2,1,0:T(8,128)(2,1)S(1)} %get-tuple-element.42), channel_id=1, source_target_pairs={{0,1},{1,0},{2,3},{3,2},{4,5},{5,4},{6,7},{7,6},{8,9},{9,8},{10,11... | collective-permute-start | bytes 294920 | tf_op jit(solution)/shard_map/ppermute | solution.py:391
  75.7 6.0 %collective-permute-done.3.first = bf16[2,64,384]{2,1,0:T(8,128)(2,1)S(1)} collective-permute-done((bf16[2,64,384]{2,1,0:T(8,128)(2,1)S(1)}, bf16[2,64,384]{2,1,0:T(8,128)(2,1)S(1)}, u32[]{:S(2)}, u32[]{:S(2)}) %collective-permute-start.3) | collective-permute-done | bytes 98336 | tf_op jit(solution)/shard_map/ppermute | solution.py:391
  81.7 0.0 all-to-all-done.4.line_in
  81.7 0.8 shard_map.116
  82.4 3.4 %all-to-all-start.5 = ((bf16[16,24,384]{2,1,0:T(8,128)(2,1)}), bf16[16,24,384]{2,1,0:T(8,128)(2,1)S(1)}, u32[]{:S(2)}, u32[]{:S(2)}) async-start(bf16[16,24,384]{2,1,0:T(8,128)(2,1)} %get-tuple-element.43), calls=%async_computation.5 | async-start | bytes 589824 | tf_op jit(solution)/shard_map/all_to_all | solution.py:383
  85.9 4.7 %collective-permute-start.4 = (bf16[64,384]{1,0:T(8,128)(2,1)S(1)}, bf16[64,384]{1,0:T(8,128)(2,1)S(1)}, u32[]{:S(2)}, u32[]{:S(2)}) collective-permute-start(bf16[64,384]{1,0:T(8,128)(2,1)S(1)} %get-tuple-element.45), channel_id=1, source_target_pairs={{0,3},{1,2},{2,1},{3,0},{4,7},{5,6},{6,5},{7,4},{8,11},{9,10},{10,... | collective-permute-start | bytes 147464 | tf_op jit(solution)/shard_map/ppermute | solution.py:391
  90.6 0.9 shard_map.118
  91.5 2.0 %collective-permute-done.4.second = bf16[64,384]{1,0:T(8,128)(2,1)S(1)} collective-permute-done((bf16[64,384]{1,0:T(8,128)(2,1)S(1)}, bf16[64,384]{1,0:T(8,128)(2,1)S(1)}, u32[]{:S(2)}, u32[]{:S(2)}) %collective-permute-start.4) | collective-permute-done | bytes 49184 | tf_op jit(solution)/shard_map/ppermute | solution.py:391
  93.5 0.0 all-to-all-done.5.spread_in
  93.5 0.9 shard_map.117
Async XLA Ops:
  13.8 7.3 %copy-start.2 = (bf16[64,3,128]{2,0,1:T(8,128)(2,1)S(1)}, bf16[64,3,128]{2,0,1:T(8,128)(2,1)}, u32[]{:S(2)}) copy-start(bf16[64,3,128]{2,0,1:T(8,128)(2,1)} %param.7) | copy-start | bytes 147460
  13.8 7.3 %copy-start.3 = (bf16[64,384]{1,0:T(8,128)(2,1)S(1)}, bf16[64,384]{1,0:T(8,128)(2,1)}, u32[]{:S(2)}) copy-start(bf16[64,384]{1,0:T(8,128)(2,1)} %grad.1) | copy-start | bytes 147460
  13.8 7.3 %copy-start.4 = (s32[3]{0:T(128)S(1)}, s32[3]{0:T(128)}, u32[]{:S(2)}) copy-start(s32[3]{0:T(128)} %offsets_far.1) | copy-start | bytes 40
  14.5 32.0 %copy-start = (f32[832,128]{1,0:T(8,128)S(1)}, f32[832,128]{1,0:T(8,128)}, u32[]{:S(2)}) copy-start(f32[832,128]{1,0:T(8,128)} %constant.2.clone.bias) | copy-start | bytes 1277956
  14.5 11.2 %all-to-all-start.2 = ((bf16[8,32,384]{2,1,0:T(8,128)(2,1)}), bf16[8,32,384]{2,1,0:T(8,128)(2,1)S(1)}, u32[]{:S(2)}, u32[]{:S(2)}) async-start(bf16[8,32,384]{2,1,0:T(8,128)(2,1)} %shard_map.112), calls=%async_computation.2 | async-start | bytes 393216 | tf_op jit(solution)/shard_map/all_to_all | solution.py:383
  21.1 25.4 %copy-start.1 = (bf16[192,768]{1,0:T(8,128)(2,1)S(1)}, bf16[192,768]{1,0:T(8,128)(2,1)}, u32[]{:S(2)}) copy-start(bf16[192,768]{1,0:T(8,128)(2,1)} %weight.1) | copy-start | bytes 884740
  25.6 19.4 %all-to-all-start = ((bf16[4,64,384]{2,1,0:T(8,128)(2,1)}), bf16[4,64,384]{2,1,0:T(8,128)(2,1)S(1)}, u32[]{:S(2)}, u32[]{:S(2)}) async-start(bf16[4,64,384]{2,1,0:T(8,128)(2,1)} %get-tuple-element.33), calls=%async_computation | async-start | bytes 393216 | tf_op jit(solution)/shard_map/all_to_all | solution.py:415
  36.8 8.2 %collective-permute-start = (bf16[8,32,384]{2,1,0:T(8,128)(2,1)S(1)}, bf16[8,32,384]{2,1,0:T(8,128)(2,1)S(1)}, u32[]{:S(2)}, u32[]{:S(2)}) collective-permute-start(bf16[8,32,384]{2,1,0:T(8,128)(2,1)S(1)} %all_to_all.30.line_in), channel_id=1, source_target_pairs={{0,4},{4,0},{8,12},{12,8},{16,20},{20,16},{24,28},{28,24},{32,36},... | collective-permute-start | bytes 589832 | tf_op jit(solution)/shard_map/ppermute | solution.py:387
  43.1 3.3 %collective-permute-start.1 = (bf16[8,32,384]{2,1,0:T(8,128)(2,1)S(1)}, bf16[8,32,384]{2,1,0:T(8,128)(2,1)S(1)}, u32[]{:S(2)}, u32[]{:S(2)}) collective-permute-start(bf16[8,32,384]{2,1,0:T(8,128)(2,1)S(1)} %all-to-all-done.2.far_in), channel_id=1, source_target_pairs={{0,4},{4,0},{8,12},{12,8},{16,20},{20,16},{24,28},{28,24},{32,36},... | collective-permute-start | bytes 589832 | tf_op jit(solution)/shard_map/ppermute | solution.py:387
  49.4 3.7 %collective-permute-start.2 = (bf16[576,384]{1,0:T(8,128)(2,1)S(1)}, bf16[576,384]{1,0:T(8,128)(2,1)S(1)}, u32[]{:S(2)}, u32[]{:S(2)}) collective-permute-start(bf16[576,384]{1,0:T(8,128)(2,1)S(1)} %get-tuple-element.36), channel_id=1, source_target_pairs={{0,4},{4,0},{8,12},{12,8},{16,20},{20,16},{24,28},{28,24},{32,36},... | collective-permute-start | bytes 1327112 | tf_op jit(solution)/shard_map/ppermute | solution.py:387
  65.5 16.2 %all-to-all-start.4 = ((bf16[8,56,384]{2,1,0:T(8,128)(2,1)}), bf16[8,56,384]{2,1,0:T(8,128)(2,1)S(1)}, u32[]{:S(2)}, u32[]{:S(2)}) async-start(bf16[8,56,384]{2,1,0:T(8,128)(2,1)} %shard_map.115), calls=%async_computation.4 | async-start | bytes 688128 | tf_op jit(solution)/shard_map/all_to_all | solution.py:383
  72.2 9.4 %collective-permute-start.3 = (bf16[2,64,384]{2,1,0:T(8,128)(2,1)S(1)}, bf16[2,64,384]{2,1,0:T(8,128)(2,1)S(1)}, u32[]{:S(2)}, u32[]{:S(2)}) collective-permute-start(bf16[2,64,384]{2,1,0:T(8,128)(2,1)S(1)} %get-tuple-element.42), channel_id=1, source_target_pairs={{0,1},{1,0},{2,3},{3,2},{4,5},{5,4},{6,7},{7,6},{8,9},{9,8},{10,11... | collective-permute-start | bytes 294920 | tf_op jit(solution)/shard_map/ppermute | solution.py:391
  82.4 11.1 %all-to-all-start.5 = ((bf16[16,24,384]{2,1,0:T(8,128)(2,1)}), bf16[16,24,384]{2,1,0:T(8,128)(2,1)S(1)}, u32[]{:S(2)}, u32[]{:S(2)}) async-start(bf16[16,24,384]{2,1,0:T(8,128)(2,1)} %get-tuple-element.43), calls=%async_computation.5 | async-start | bytes 589824 | tf_op jit(solution)/shard_map/all_to_all | solution.py:383
  85.9 7.7 %collective-permute-start.4 = (bf16[64,384]{1,0:T(8,128)(2,1)S(1)}, bf16[64,384]{1,0:T(8,128)(2,1)S(1)}, u32[]{:S(2)}, u32[]{:S(2)}) collective-permute-start(bf16[64,384]{1,0:T(8,128)(2,1)S(1)} %get-tuple-element.45), channel_id=1, source_target_pairs={{0,3},{1,2},{2,1},{3,0},{4,7},{5,6},{6,5},{7,4},{8,11},{9,10},{10,... | collective-permute-start | bytes 147464 | tf_op jit(solution)/shard_map/ppermute | solution.py:391
